TPU v7x, 128 devices: a whole 4x4x4 slice. The times are simulated.
128 devices in a mesh: enc: 4 (over x), dp: 32 (over z, y, core).
Axes of the slice: x: 4, y: 4, z: 4, core: 2. Of those that a mesh axis runs over, the one named last changes fastest.
Arguments:
- queries: bfloat16 [512, 64, 2048], P('dp', None, 'enc'), may hold values from -6 to 6
- encodings: bfloat16 [2048, 128, 512], P(('enc', 'dp')), may hold values from -6 to 6
- w_key: bfloat16 [512, 2048], P(None, 'enc'), may hold values from -0.25 to 0.25
- w_value: bfloat16 [512, 2048], P(None, 'enc'), may hold values from -0.25 to 0.25
- neighbours: int32 [512, 2], P('dp'), may hold values from 0 to 2047, as said below
- d_out: bfloat16 [512, 64, 2048], P('dp', None, 'enc'), may hold values from -48 to 48
Outputs:
- attended: bfloat16 [512, 64, 2048], P('dp', None, 'enc')
- d_queries: bfloat16 [512, 64, 2048], P('dp', None, 'enc')
- d_encodings: bfloat16 [2048, 128, 512], P(('enc', 'dp'))
- d_w_key: float32 [512, 2048], P('dp', 'enc')
- d_w_value: float32 [512, 2048], P('dp', 'enc')
Inputs may be any that keep to these rules, and one draw needn't show every extreme that they name: Neighbour n is held by the device at flat index n // 16 of enc+dp. No neighbour is named twice among the stretches of one dp index. The stretches of one dp index name at most 2 neighbours held by one device, and some device is named exactly 2 times by the stretches of every dp index. Of the 32 pairs of one dp index at most 12 name neighbours of one encoder group, and exactly that many do in some group.
All inputs are finite; a program needn't handle non-finite values.
Results may differ from a plain program's by a relative error of at most 0.025.
Values may be sent and summed in bfloat16 or wider, within the bound.
No kernel may reach another device: no remote copies, remote signals or barrier semaphores. Data moves between devices by JAX's collectives and lax.ppermute only.
A program may use at most 256 MiB of HBM per device.

v0:
```python
import math

import jax
import jax.numpy as jnp
from jax import lax
from jax.sharding import PartitionSpec as P

D_HEAD = 128
PAIR_G = 12


EPSILON = 1e-06


def unit_rows(values):
    factor = lax.rsqrt(jnp.mean(values * values, axis=-1, keepdims=True) + EPSILON)
    return (values * factor, factor)


def unit_grad(gradient, unit_vals, factor):
    return factor * (gradient - unit_vals * jnp.mean(gradient * unit_vals, axis=-1, keepdims=True))


def placed(target, payload, extent):
    matches = target[:, None] == jnp.arange(extent, dtype=jnp.int32)[None, :]
    return jnp.sum(jnp.where(matches, payload[:, None], 0), axis=0)


def picked(source, position):
    fetched = jnp.take(source, jnp.maximum(position - 1, 0), axis=0)
    present = (position > 0).reshape((-1,) + (1,) * (source.ndim - 1))
    return jnp.where(present, fetched, jnp.zeros_like(fetched))


def body(queries, encodings, w_key, w_value, neighbours, d_out):
    enc_count = lax.axis_size("enc")
    shard_count = lax.axis_size("dp")
    my_group = lax.axis_index("enc")
    held_rows, neigh_len, enc_width = encodings.shape
    stretch_count, stretch_span, head_cols = queries.shape
    head_count = head_cols // D_HEAD
    pair_count = neighbours.shape[0] * neighbours.shape[1]
    owners = enc_count * shard_count
    capacity = 2 * ((3 * stretch_count // 4 + 2 * shard_count - 1) // (2 * shard_count))
    inverse = 1.0 / math.sqrt(D_HEAD)
    contract = (((0,), (0,)), ((), ()))
    pair_ids = neighbours.reshape(-1)
    owner_flat = pair_ids // held_rows
    group_of = owner_flat // shard_count
    home_shard = owner_flat % shard_count
    local_row = pair_ids % held_rows
    numbered = jnp.arange(pair_count, dtype=jnp.int32)
    owner_hits = (owner_flat[:, None] == jnp.arange(owners, dtype=jnp.int32)[None, :]).astype(
        jnp.int32
    )
    slot_index = jnp.sum((jnp.cumsum(owner_hits, axis=0) - owner_hits) * owner_hits, axis=1)
    group_hits = (group_of[:, None] == jnp.arange(enc_count, dtype=jnp.int32)[None, :]).astype(
        jnp.int32
    )
    group_rank = jnp.sum((jnp.cumsum(group_hits, axis=0) - group_hits) * group_hits, axis=1)
    in_group = group_of == my_group
    wanted = placed(
        jnp.where(in_group, home_shard * capacity + slot_index, -1),
        local_row + 1,
        shard_count * capacity,
    ).reshape(shard_count, capacity)
    served = lax.all_to_all(wanted, "dp", split_axis=0, concat_axis=0, tiled=True)
    outgoing_rows = picked(encodings, served.reshape(-1)).reshape(
        shard_count, capacity, neigh_len, enc_width
    )
    arrived = lax.all_to_all(outgoing_rows, "dp", split_axis=0, concat_axis=0, tiled=True).reshape(
        shard_count * capacity, neigh_len, enc_width
    )
    source = placed(
        jnp.where(in_group, group_rank, -1), home_shard * capacity + slot_index + 1, PAIR_G
    )
    compact = picked(arrived, source)
    every_group = lax.all_gather(compact, "enc", axis=0, tiled=True)
    pair_rows = jnp.take(every_group, group_of * PAIR_G + group_rank, axis=0)
    flat_rows = pair_rows.reshape(pair_count * neigh_len, enc_width)
    key_rows = jnp.dot(flat_rows, w_key, preferred_element_type=jnp.float32).astype(jnp.bfloat16)
    value_rows = jnp.dot(flat_rows, w_value, preferred_element_type=jnp.float32).astype(
        jnp.bfloat16
    )
    key_heads = key_rows.reshape(
        stretch_count, pair_count // stretch_count * neigh_len, head_count, D_HEAD
    )
    value_heads = value_rows.reshape(
        stretch_count, pair_count // stretch_count * neigh_len, head_count, D_HEAD
    )
    query_unit, query_scale = unit_rows(
        queries.reshape(stretch_count, stretch_span, head_count, D_HEAD).astype(jnp.float32)
    )
    key_unit, key_scale = unit_rows(key_heads.astype(jnp.float32))
    query_bf = query_unit.astype(jnp.bfloat16)
    key_bf = key_unit.astype(jnp.bfloat16)
    scores = (
        jnp.einsum("cqhd,ckhd->chqk", query_bf, key_bf, preferred_element_type=jnp.float32)
        * inverse
    )
    raised = jnp.exp(scores)
    weights = raised / jnp.sum(raised, axis=-1, keepdims=True)
    probabilities = weights.astype(jnp.bfloat16)
    attended = jnp.einsum(
        "chqk,ckhd->cqhd", probabilities, value_heads, preferred_element_type=jnp.float32
    )
    attended = attended.astype(jnp.bfloat16).reshape(stretch_count, stretch_span, head_cols)
    grad_heads = d_out.reshape(stretch_count, stretch_span, head_count, D_HEAD)
    d_probs = jnp.einsum(
        "cqhd,ckhd->chqk", grad_heads, value_heads, preferred_element_type=jnp.float32
    )
    d_scores = (
        weights * (d_probs - jnp.sum(d_probs * weights, axis=-1, keepdims=True)) * inverse
    ).astype(jnp.bfloat16)
    d_query_unit = jnp.einsum(
        "chqk,ckhd->cqhd", d_scores, key_bf, preferred_element_type=jnp.float32
    )
    d_queries = (
        unit_grad(d_query_unit, query_unit, query_scale)
        .astype(jnp.bfloat16)
        .reshape(stretch_count, stretch_span, head_cols)
    )
    d_key_unit = jnp.einsum(
        "chqk,cqhd->ckhd", d_scores, query_bf, preferred_element_type=jnp.float32
    )
    d_keys = (
        unit_grad(d_key_unit, key_unit, key_scale)
        .astype(jnp.bfloat16)
        .reshape(pair_count * neigh_len, head_cols)
    )
    d_values = jnp.einsum(
        "chqk,cqhd->ckhd", probabilities, grad_heads, preferred_element_type=jnp.float32
    )
    d_values = d_values.astype(jnp.bfloat16).reshape(pair_count * neigh_len, head_cols)
    partial_value = jnp.dot(d_keys, w_key.T, preferred_element_type=jnp.float32) + jnp.dot(
        d_values, w_value.T, preferred_element_type=jnp.float32
    )
    partial_value = partial_value.astype(jnp.bfloat16).reshape(pair_count, neigh_len, enc_width)
    key_part = lax.dot_general(flat_rows, d_keys, contract, preferred_element_type=jnp.float32)
    value_part = lax.dot_general(flat_rows, d_values, contract, preferred_element_type=jnp.float32)
    weight_sums = lax.psum_scatter(
        jnp.concatenate([key_part, value_part], axis=1).astype(jnp.bfloat16),
        "dp",
        scatter_dimension=0,
        tiled=True,
    ).astype(jnp.float32)
    spread = placed(group_of * PAIR_G + group_rank, numbered + 1, enc_count * PAIR_G)
    arranged = picked(partial_value, spread).astype(jnp.float32)
    head_sum = lax.psum_scatter(
        arranged.astype(jnp.bfloat16), "enc", scatter_dimension=0, tiled=True
    )
    back_index = placed(
        jnp.where(in_group, home_shard * capacity + slot_index, -1),
        group_rank + 1,
        shard_count * capacity,
    )
    outgoing = picked(head_sum, back_index).reshape(shard_count, capacity, neigh_len, enc_width)
    returned = lax.all_to_all(outgoing, "dp", split_axis=0, concat_axis=0, tiled=True)
    row_match = (
        served.reshape(-1)[:, None] - 1 == jnp.arange(held_rows, dtype=jnp.int32)[None, :]
    ).astype(jnp.bfloat16)
    d_encodings = lax.dot_general(
        row_match,
        returned.reshape(shard_count * capacity, neigh_len * enc_width),
        contract,
        preferred_element_type=jnp.float32,
    )
    d_encodings = d_encodings.astype(jnp.bfloat16).reshape(held_rows, neigh_len, enc_width)
    return (
        attended,
        d_queries,
        d_encodings,
        weight_sums[:, :head_cols],
        weight_sums[:, head_cols:],
    )


def solution(mesh):
    in_specs = (
        P("dp", None, "enc"),
        P(("enc", "dp"), None, None),
        P(None, "enc"),
        P(None, "enc"),
        P("dp", None),
        P("dp", None, "enc"),
    )
    out_specs = (
        P("dp", None, "enc"),
        P("dp", None, "enc"),
        P(("enc", "dp"), None, None),
        P("dp", "enc"),
        P("dp", "enc"),
    )
    return jax.shard_map(body, mesh=mesh, in_specs=in_specs, out_specs=out_specs, check_vma=False)
```

profile of v0, /device:TPU:1, one launch (start us, length us, event | category | flops | bytes accessed | tf_op | source)
XLA Modules:
  0.0 618.3 jit_solution(4523997614172628935)
XLA Ops:
  9.1 16.3 %all_to_all.19 = s32[32,1,2]{2,1,0:T(1,128)S(1)} all-to-all(s32[32,1,2]{2,1,0:T(1,128)S(1)} %bitcast.166), channel_id=1, replica_groups=mesh['enc'=4,'dp'=32] {'dp'}, dimensions={0} | all-to-all | bytes 512 | tf_op jit(solution)/shard_map/all_to_all | solution.py:67
  31.2 7.6 %select_select_fusion.1 = bf16[32,2,128,512]{3,2,1,0:T(8,128)(2,1)} fusion(bf16[32,2,128,512]{3,2,1,0:T(8,128)(2,1)} %bitcast.154, pred[32,2]{1,0:T(8,128)(4,1)S(1)} %copy.126, pred[32,2]{1,0:T(8,128)(4,1)S(1)} %copy.124), kind=kLoop, calls=%fused_computation.15 | loop fusion | flops 8388608 | bytes 16777344 | tf_op jit(solution)/shard_map/jit(_where)/select_n | solution.py:32
  44.3 99.6 %all-to-all-done.1 = bf16[32,2,128,512]{3,2,1,0:T(8,128)(2,1)} async-done(((bf16[32,2,128,512]{3,2,1,0:T(8,128)(2,1)}), bf16[32,2,128,512]{3,2,1,0:T(8,128)(2,1)}, u32[]{:S(2)}, u32[]{:S(2)}) %all-to-all-start.1) | async-done | bytes 8388640 | tf_op jit(solution)/shard_map/all_to_all | solution.py:71
  157.2 62.9 %all-gather.2.cloned.1.call-done = bf16[48,128,512]{2,1,0:T(8,128)(2,1)} async-done(((bf16[12,128,512]{2,1,0:T(8,128)(2,1)}), bf16[48,128,512]{2,1,0:T(8,128)(2,1)}) %all-gather.2.cloned.1.call-update) | async-done | bytes 6291472 | tf_op jit(solution)/shard_map/all_gather | solution.py:78
  230.3 5.6 fusion.4
  235.9 9.9 %reshape.539 = f32[16,256,4,128]{3,2,1,0:T(4,128)} reshape(f32[4096,512]{1,0:T(8,128)} %fusion.4) | data formatting | bytes 16777216 | tf_op jit(solution)/shard_map/convert_element_type | solution.py:94
  245.8 9.9 %copy.134 = f32[16,256,4,128]{1,3,2,0:T(8,128)} copy(f32[16,256,4,128]{3,2,1,0:T(4,128)} %reshape.539) | data formatting | bytes 16777216 | tf_op jit(solution)/shard_map/convert_element_type | solution.py:94
  255.7 9.3 %multiply_reduce_fusion = f32[16,256,4]{2,1,0:T(8,128)} fusion(f32[16,256,4,128]{3,2,1,0:T(4,128)} %reshape.539), kind=kLoop, calls=%fused_computation.14 | loop fusion | flops 4177920 | bytes 8454144 | tf_op jit(solution)/shard_map/reduce_sum | solution.py:16
  265.0 6.5 %convolution_convert_fusion.2 = bf16[4096,512]{1,0:T(8,128)(2,1)} fusion(bf16[4096,512]{1,0:T(8,128)(2,1)} %copy-done.5, bf16[512,512]{1,0:T(8,128)(2,1)S(1)} %copy-done.13), kind=kOutput, calls=%fused_computation.20 | convolution fusion | flops 2149580800 | bytes 8912896 | tf_op jit(solution)/shard_map/dot_general | solution.py:82
  271.5 7.0 %reshape.529 = bf16[16,256,4,128]{3,2,1,0:T(4,128)(2,1)} reshape(bf16[4096,512]{1,0:T(8,128)(2,1)} %convolution_convert_fusion.2) | data formatting | bytes 8388608 | tf_op jit(solution)/shard_map/reshape | solution.py:88
  280.8 5.7 fusion.10
  297.1 33.0 %fusion.1 = (f32[16,256,4]{1,2,0:T(4,128)S(1)}, f32[16,4,128,256]{3,2,1,0:T(8,128)}) fusion(f32[16,256,4,128]{1,3,2,0:T(8,128)} %copy.134, f32[16,256,4]{1,2,0:T(4,128)S(1)} %copy.133, f32[16,4,256,64]{2,3,1,0:T(8,128)} %fusion.10, f32[16,4,64]{2,1,0:T(4,128)S(1)} %get-tuple-element.59, f32[16,4,64,256]{3,2,1,0:T(8,128)} %copy-done.9, ...), kind=kOutput, calls=%fused_computation.9 | convolution fusion | flops 285724928 | bytes 26378240 | tf_op jit(solution)/shard_map/chqk,cqhd->ckhd/dot_general | solution.py:123
  330.1 10.6 %fusion.3 = bf16[16,256,4,128]{1,3,2,0:T(8,128)(2,1)} fusion(f32[16,4,128,256]{3,2,1,0:T(8,128)} %get-tuple-element.64, f32[16,256,4,128]{1,3,2,0:T(8,128)} %copy.134, f32[16,256,4]{1,2,0:T(4,128)S(1)} %copy.146, f32[16,256,4]{1,2,0:T(4,128)S(1)} %copy.133), kind=kLoop, calls=%fused_computation.11 | loop fusion | flops 10485760 | bytes 21102592 | tf_op jit(solution)/shard_map/convert_element_type | solution.py:128
  349.4 5.7 fusion.56
  355.1 8.1 %copy.149 = bf16[16,256,4,128]{1,0,3,2:T(8,128)(2,1)} copy(bf16[16,256,4,128]{3,1,2,0:T(8,128)(2,1)} %convert_bitcast_fusion) | data formatting | bytes 8388608 | tf_op jit(solution)/shard_map/convert_element_type | solution.py:134
  372.5 7.2 %gather_fusion.3 = bf16[48,128,512]{2,1,0:T(8,128)(2,1)} fusion(bf16[32,128,512]{2,1,0:T(8,128)(2,1)} %bitcast.152, s32[1024]{0:T(1024)S(1)} %pad_clamp_fusion.1), kind=kCustom, calls=%fused_computation.3 | custom fusion | bytes 12583104 | tf_op jit(solution)/shard_map/jit(_take)/gather | solution.py:30
  379.7 6.3 %select_select_fusion.2 = bf16[48,128,512]{2,1,0:T(8,128)(2,1)} fusion(bf16[48,128,512]{2,1,0:T(8,128)(2,1)} %gather_fusion.3, pred[48]{0:T(512)(128)(4,1)S(1)} %get-tuple-element.52, pred[48]{0:T(512)(128)(4,1)S(1)} %get-tuple-element.51), kind=kLoop, calls=%fused_computation.17 | loop fusion | flops 6291456 | bytes 12583008 | tf_op jit(solution)/shard_map/jit(_where)/select_n | solution.py:32
  386.3 64.5 %reduce-scatter.5.cloned.1.call-done = bf16[12,128,512]{2,1,0:T(8,128)(2,1)} async-done(((bf16[48,128,512]{2,1,0:T(8,128)(2,1)}), bf16[12,128,512]{2,1,0:T(8,128)(2,1)}) %reduce-scatter.5.cloned.1.call-update) | async-done | bytes 1572880 | tf_op jit(solution)/shard_map/reduce_scatter | solution.py:149
  450.8 6.7 %gather_fusion.4 = bf16[64,128,512]{2,1,0:T(8,128)(2,1)} fusion(bf16[12,128,512]{2,1,0:T(8,128)(2,1)} %reduce-scatter.5.cloned.1.call-done, s32[1024]{0:T(1024)S(1)} %pad_clamp_fusion), kind=kCustom, calls=%fused_computation.4 | custom fusion | bytes 16777472 | tf_op jit(solution)/shard_map/jit(_take)/gather | solution.py:30
  457.5 7.6 %select_select_fusion = bf16[32,2,128,512]{3,2,1,0:T(8,128)(2,1)} fusion(bf16[32,2,128,512]{3,2,1,0:T(8,128)(2,1)} %bitcast.153, pred[32,2]{1,0:T(8,128)(4,1)S(1)} %le.67, pred[32,2]{1,0:T(8,128)(4,1)S(1)} %gt.38), kind=kLoop, calls=%fused_computation.12 | loop fusion | flops 8388608 | bytes 16777344 | tf_op jit(solution)/shard_map/jit(_where)/select_n | solution.py:32
  465.1 7.7 %all-to-all-start.2 = ((bf16[32,2,128,512]{3,2,1,0:T(8,128)(2,1)}), bf16[32,2,128,512]{3,2,1,0:T(8,128)(2,1)}, u32[]{:S(2)}, u32[]{:S(2)}) async-start(bf16[32,2,128,512]{3,2,1,0:T(8,128)(2,1)} %select_select_fusion), calls=%async_computation.3 | async-start | bytes 16777216 | tf_op jit(solution)/shard_map/all_to_all | solution.py:158
  482.9 32.9 %fusion.14 = (f32[16,64,4]{1,2,0:T(4,128)S(1)}, f32[16,4,128,64]{2,3,1,0:T(8,128)}) fusion(f32[16,64,4]{1,2,0:T(4,128)S(1)} %copy.130, f32[16,4,256,64]{2,3,1,0:T(8,128)} %fusion.10, f32[16,4,64]{2,1,0:T(4,128)S(1)} %get-tuple-element.59, f32[16,4,64,256]{3,2,1,0:T(8,128)} %copy-done.9, f32[16,256,4,128]{1,3,2,0:T(8,128)} %copy.134, ...), kind=kOutput, calls=%fused_computation.39 | convolution fusion | flops 284164352 | bytes 20037632 | tf_op jit(solution)/shard_map/chqk,ckhd->cqhd/dot_general | solution.py:115
  523.3 67.1 %reduce-scatter.7.cloned.1.call-done = bf16[16,1024]{1,0:T(8,128)(2,1)} async-done(((bf16[512,1024]{1,0:T(8,128)(2,1)}), bf16[16,1024]{1,0:T(8,128)(2,1)}) %reduce-scatter.7.cloned.1.call-update) | async-done | bytes 32784
  592.9 11.8 %copy.162 = bf16[8,8,128,512]{3,1,2,0:T(8,128)(2,1)} copy(bf16[8,8,128,512]{3,2,1,0:T(8,128)(2,1)} %bitcast.39) | data formatting | bytes 16777216
  (115 shorter events, 94.3 us)
Async XLA Ops:
  7.2 18.8 %copy-start = (bf16[16,128,512]{2,1,0:T(8,128)(2,1)S(1)}, bf16[16,128,512]{2,1,0:T(8,128)(2,1)}, u32[]{:S(2)}) copy-start(bf16[16,128,512]{2,1,0:T(8,128)(2,1)} %param.7) | copy-start | bytes 6291460
  38.8 105.0 %all-to-all-start.1 = ((bf16[32,2,128,512]{3,2,1,0:T(8,128)(2,1)}), bf16[32,2,128,512]{3,2,1,0:T(8,128)(2,1)}, u32[]{:S(2)}, u32[]{:S(2)}) async-start(bf16[32,2,128,512]{3,2,1,0:T(8,128)(2,1)} %select_select_fusion.1), calls=%async_computation.1 | async-start | bytes 16777216 | tf_op jit(solution)/shard_map/all_to_all | solution.py:71
  44.0 108.1 %copy-start.8 = (bf16[16,64,512]{2,1,0:T(8,128)(2,1)S(1)}, bf16[16,64,512]{2,1,0:T(8,128)(2,1)}, u32[]{:S(2)}) copy-start(bf16[16,64,512]{2,1,0:T(8,128)(2,1)} %param.6) | copy-start | bytes 3145732
  44.1 176.1 %all-gather.2.cloned.1.call-start = ((), (), s32[]{:S(2)}) async-start(), calls=%async_computation.5 | async-start | bytes 7864320 | tf_op jit(solution)/shard_map/all_gather | solution.py:78
  151.9 299.0 %reduce-scatter.5.cloned.1.call-start = ((), (), s32[]{:S(2)}) async-start(), calls=%async_computation.6 | async-start | bytes 7864320 | tf_op jit(solution)/shard_map/reduce_scatter | solution.py:149
  225.7 4.6 copy-start.11
  228.3 1.9 copy-start.5
  255.7 9.3 %copy-start.13 = (bf16[512,512]{1,0:T(8,128)(2,1)S(1)}, bf16[512,512]{1,0:T(8,128)(2,1)}, u32[]{:S(2)}) copy-start(bf16[512,512]{1,0:T(8,128)(2,1)} %param.9) | copy-start | bytes 1572868
  271.5 9.3 %copy-start.12 = (bf16[16,64,512]{2,1,0:T(8,128)(2,1)S(1)}, bf16[16,64,512]{2,1,0:T(8,128)(2,1)}, u32[]{:S(2)}) copy-start(bf16[16,64,512]{2,1,0:T(8,128)(2,1)} %param.11) | copy-start | bytes 3145732
  291.3 2.0 copy-start.9
  347.5 1.9 copy-start.6
  363.2 4.7 copy-start.2
  367.9 4.7 copy-start.3
  465.1 127.7 %all-to-all-start.2 = ((bf16[32,2,128,512]{3,2,1,0:T(8,128)(2,1)}), bf16[32,2,128,512]{3,2,1,0:T(8,128)(2,1)}, u32[]{:S(2)}, u32[]{:S(2)}) async-start(bf16[32,2,128,512]{3,2,1,0:T(8,128)(2,1)} %select_select_fusion), calls=%async_computation.3 | async-start | bytes 16777216 | tf_op jit(solution)/shard_map/all_to_all | solution.py:158
  472.8 117.6 %reduce-scatter.7.cloned.1.call-start = ((), (), s32[]{:S(2)}) async-start(), calls=%async_computation.7 | async-start | bytes 1081344
  473.3 3.5 copy-start.4
  476.7 2.3 copy-start.7
  515.9 5.0 copy-start.10
  604.6 6.9 %copy-start.1 = (bf16[16,128,512]{2,1,0:T(8,128)(2,1)S(1)}, bf16[16,128,512]{2,1,0:T(8,128)(2,1)}, u32[]{:S(2)}) copy-start(bf16[16,128,512]{2,1,0:T(8,128)(2,1)} %param.7) | copy-start | bytes 6291460
Sparse Core Ops, SparseCore 0:
  152.0 68.0 all-gather.1
  386.1 64.6 reduce-scatter.4
  483.0 107.3 reduce-scatter.6
where the time goes:
time: 624 us; the launch traced here: 618 us
  waiting for transfers between devices  294 us (47%)
  matrix products  117 us (19%)
  local copies, waits for them, and re-layouts  107 us (17%)
  other arithmetic  56.1 us (9%)
  blocking collectives  16.3 us (3%)
  between operations  14.5 us (2%)
  starting transfers between devices  13.4 us (2%)
    all_to_all x1, waiting for transfers between devices, body(): lax.all_to_all(outgoing_rows, 'dp', split_axis=0, concat_axis=0, tiled=True)  99.6 us
    unnamed x4, waiting for transfers between devices  67.1 us
    reduce_scatter x1, waiting for transfers between devices, body(): lax.psum_scatter(arranged.astype(jnp.bfloat16), 'enc', scatter_dimension=...  64.5 us
    all_gather x1, waiting for transfers between devices, body(): every_group = lax.all_gather(compact, 'enc', axis=0, tiled=True)  62.9 us
    dot_general x1, matrix products, body(): jnp.einsum('chqk,cqhd->ckhd', d_scores, query_bf, preferred_element_type=...  33 us
    dot_general x1, matrix products, body(): jnp.einsum('chqk,ckhd->cqhd', d_scores, key_bf, preferred_element_type=jn...  32.9 us
    unnamed x37, local copies, waits for them, and re-layouts  31.8 us
    gather x4, local copies, waits for them, and re-layouts, picked(): fetched = jnp.take(source, jnp.maximum(position - 1, 0), axis=0)  24.4 us
  transfers between devices with their start and end apart: 5, of which 4 were waited for; matrix products, arithmetic and copies ran while one was open for 9% of the time, Pallas kernels for 0%

commit v1 on v0

v1 whole, which is shorter than its diff:
```python
import functools
import math

import jax
import jax.numpy as jnp
from jax import lax
from jax.experimental import pallas as pl
from jax.experimental.pallas import tpu as pltpu
from jax.sharding import PartitionSpec as P

D_HEAD = 128
EPSILON = 1e-06
BOTH = ("enc", "dp")
CHUNKS = 1
PER_STEP = 1
F32 = jnp.float32
BF16 = jnp.bfloat16
ROWS = (((0,), (0,)), ((), ()))
COLS = (((1,), (1,)), ((), ()))


def mm(a, b, dims=(((1,), (0,)), ((), ()))):
    return lax.dot_general(a, b, dims, preferred_element_type=F32)


def attention_kernel(first, x_ref, q_ref, do_ref, w_ref, wt_ref, *refs):
    if first:
        att_ref, dq_ref, part_ref, dw_ref, acc = refs
    else:
        acc_in, _, _, att_ref, dq_ref, part_ref, dw_ref, acc = refs
    step = pl.program_id(0)
    inverse = 1.0 / math.sqrt(D_HEAD)
    per_step, span, cols = q_ref.shape
    sources, pairs, rows, width = x_ref.shape
    knb = pairs // per_step
    keys_n = sources * knb * rows
    heads = cols // D_HEAD

    @pl.when(step == 0)
    def _():
        acc[...] = jnp.zeros_like(acc) if first else acc_in[...]

    for s in range(per_step):
        x = x_ref[:, s * knb : (s + 1) * knb].reshape(keys_n, width)
        kv = mm(x, w_ref[...]).astype(BF16)
        d_key_parts, d_value_parts = [], []
        for h in range(heads):
            at = slice(h * D_HEAD, (h + 1) * D_HEAD)
            query = q_ref[s, :, at].astype(F32)
            grad = do_ref[s, :, at]
            key = kv[:, at].astype(F32)
            value = kv[:, cols + h * D_HEAD : cols + (h + 1) * D_HEAD]
            query_scale = lax.rsqrt(jnp.mean(query * query, axis=-1, keepdims=True) + EPSILON)
            query_unit = query * query_scale
            query_bf = query_unit.astype(BF16)
            key_scale = lax.rsqrt(jnp.mean(key * key, axis=-1, keepdims=True) + EPSILON)
            key_unit = key * key_scale
            key_bf = key_unit.astype(BF16)
            raised = jnp.exp(mm(query_bf, key_bf, COLS) * inverse)
            weights = raised * (1.0 / jnp.sum(raised, axis=-1, keepdims=True))
            probs = weights.astype(BF16)
            att_ref[s, :, at] = mm(probs, value).astype(BF16)
            d_probs = mm(grad, value, COLS)
            inner = jnp.sum(d_probs * weights, axis=-1, keepdims=True)
            d_scores = (weights * (d_probs - inner) * inverse).astype(BF16)
            d_query_unit = mm(d_scores, key_bf)
            mean_q = jnp.mean(d_query_unit * query_unit, axis=-1, keepdims=True)
            dq_ref[s, :, at] = (query_scale * (d_query_unit - query_unit * mean_q)).astype(BF16)
            d_key_unit = mm(d_scores, query_bf, ROWS)
            mean_k = jnp.mean(d_key_unit * key_unit, axis=-1, keepdims=True)
            d_key_parts.append((key_scale * (d_key_unit - key_unit * mean_k)).astype(BF16))
            d_value_parts.append(mm(probs, grad, ROWS).astype(BF16))
        d_kv = jnp.concatenate(d_key_parts + d_value_parts, axis=1)
        part = mm(d_kv, wt_ref[...]).astype(BF16)
        part_ref[:, s * knb : (s + 1) * knb] = part.reshape(sources, knb, rows, width)
        acc[...] += mm(x, d_kv, ROWS)

    @pl.when(step == pl.num_programs(0) - 1)
    def _():
        dw_ref[...] = acc[...].astype(dw_ref.dtype)


def attention(chunk, chunks, x, queries, d_out, w, wt, carried):
    stretches, span, cols = queries.shape
    sources, pairs, rows, width = x.shape
    mine = stretches // chunks
    knb = pairs // mine
    steps = mine // PER_STEP
    first, last = chunk == 0, chunk == chunks - 1
    offset = chunk * steps
    by_stretch = pl.BlockSpec((PER_STEP, span, cols), lambda i: (offset + i, 0, 0))
    by_pair = pl.BlockSpec((sources, PER_STEP * knb, rows, width), lambda i: (0, i, 0, 0))
    whole = lambda shape: pl.BlockSpec(shape, lambda i: (0,) * len(shape))
    in_specs = [by_pair, by_stretch, by_stretch, whole(w.shape), whole(wt.shape)]
    args = [x, queries, d_out, w, wt]
    aliases = {}
    if not first:
        att, dq, acc = carried
        in_specs += [whole(acc.shape), pl.BlockSpec(memory_space=pl.ANY), pl.BlockSpec(memory_space=pl.ANY)]
        args += [acc, att, dq]
        aliases = {6: 0, 7: 1}
    return pl.pallas_call(
        functools.partial(attention_kernel, first),
        grid=(steps,),
        in_specs=in_specs,
        out_specs=[by_stretch, by_stretch, by_pair, whole(w.shape)],
        out_shape=[
            jax.ShapeDtypeStruct(queries.shape, BF16),
            jax.ShapeDtypeStruct(queries.shape, BF16),
            jax.ShapeDtypeStruct(x.shape, BF16),
            jax.ShapeDtypeStruct(w.shape, BF16 if last else F32),
        ],
        scratch_shapes=[pltpu.VMEM(w.shape, F32)],
        input_output_aliases=aliases,
        compiler_params=pltpu.CompilerParams(vmem_limit_bytes=48 * 1024 * 1024),
        cost_estimate=pl.CostEstimate(
            flops=mine * 900_000_000, bytes_accessed=mine * 800_000, transcendentals=mine * 66_000
        ),
        name="attention",
    )(*args)


def pick_kernel(ids_ref, table_ref, out_ref):
    ids = ids_ref[...]
    count = table_ref.shape[0]
    hit = ids == lax.broadcasted_iota(jnp.int32, (ids.shape[0], count), 1)
    out_ref[...] = mm(hit.astype(BF16), table_ref[...]).astype(BF16)


def pick_rows(ids, table, tile=256):
    count, width = table.shape
    wanted = ids.shape[0]
    return pl.pallas_call(
        pick_kernel,
        grid=(wanted // tile,),
        in_specs=[
            pl.BlockSpec((tile, 1), lambda i: (i, 0)),
            pl.BlockSpec((count, width), lambda i: (0, 0)),
        ],
        out_specs=pl.BlockSpec((tile, width), lambda i: (i, 0)),
        out_shape=jax.ShapeDtypeStruct((wanted, width), BF16),
        compiler_params=pltpu.CompilerParams(vmem_limit_bytes=48 * 1024 * 1024),
        name="pick_rows",
    )(ids.reshape(wanted, 1), table)


def place_kernel(ids_ref, rows_ref, out_ref):
    ids = ids_ref[...]
    tile = out_ref.shape[0]
    row = lax.broadcasted_iota(jnp.int32, (tile, ids.shape[1]), 0) + pl.program_id(0) * tile
    out_ref[...] = mm((ids == row).astype(BF16), rows_ref[...]).astype(BF16)


def place_rows(ids, rows, count, tile=256):
    given, width = rows.shape
    return pl.pallas_call(
        place_kernel,
        grid=(count // tile,),
        in_specs=[
            pl.BlockSpec((1, given), lambda i: (0, 0)),
            pl.BlockSpec((given, width), lambda i: (0, 0)),
        ],
        out_specs=pl.BlockSpec((tile, width), lambda i: (i, 0)),
        out_shape=jax.ShapeDtypeStruct((count, width), BF16),
        compiler_params=pltpu.CompilerParams(vmem_limit_bytes=48 * 1024 * 1024),
        name="place_rows",
    )(ids.reshape(1, given), rows)


def body(queries, encodings, w_key, w_value, neighbours, d_out):
    enc_count = lax.axis_size("enc")
    shards = lax.axis_size("dp")
    devices = enc_count * shards
    held, neigh_len, width = encodings.shape
    stretches, _, cols = queries.shape
    pair_count = neighbours.size
    per_chunk = pair_count // CHUNKS
    w = jnp.concatenate([w_key, w_value], axis=1)
    wt = w.T
    ids = lax.all_gather(neighbours.reshape(-1), "dp", axis=0, tiled=True)
    ids = ids.reshape(shards, CHUNKS, per_chunk)
    by_row = jnp.swapaxes(encodings, 0, 1)
    table = lax.all_to_all(by_row, BOTH, 0, 0, tiled=True).reshape(devices * held, width)
    inputs = []
    for c in range(CHUNKS):
        sent = pick_rows(ids[:, c].reshape(-1), table).reshape(shards, per_chunk, width)
        got = lax.all_to_all(sent, "dp", 0, 0, tiled=True)
        inputs.append(lax.all_gather(jnp.swapaxes(got, 0, 1), "enc", axis=0, tiled=False))
    carried = None
    returned = []
    for c in range(CHUNKS):
        att, dq, part, acc = attention(c, CHUNKS, inputs[c], queries, d_out, w, wt, carried)
        carried = (att, dq, acc)
        summed = lax.psum_scatter(part, "enc", scatter_dimension=0, tiled=False)
        back = lax.all_to_all(jnp.swapaxes(summed, 0, 1), "dp", 0, 0, tiled=True)
        returned.append(back.reshape(shards * per_chunk, width))
    order = jnp.swapaxes(ids, 0, 1).reshape(-1)
    rows = jnp.concatenate(returned, axis=0) if CHUNKS > 1 else returned[0]
    placed = place_rows(order, rows, devices * held).reshape(devices, held, width)
    d_encodings = jnp.swapaxes(lax.all_to_all(placed, BOTH, 0, 0, tiled=True), 0, 1)
    d_w = lax.all_to_all(acc.reshape(shards, -1, 2 * cols), "dp", 0, 0, tiled=True)
    d_w = jnp.sum(d_w.astype(F32), axis=0)
    return att, dq, d_encodings, d_w[:, :cols], d_w[:, cols:]


def solution(mesh):
    in_specs = (
        P("dp", None, "enc"),
        P(("enc", "dp"), None, None),
        P(None, "enc"),
        P(None, "enc"),
        P("dp", None),
        P("dp", None, "enc"),
    )
    out_specs = (
        P("dp", None, "enc"),
        P("dp", None, "enc"),
        P(("enc", "dp"), None, None),
        P("dp", "enc"),
        P("dp", "enc"),
    )
    return jax.shard_map(body, mesh=mesh, in_specs=in_specs, out_specs=out_specs, check_vma=False)
```

time: 624 us -> 321 us (0.51)
  waiting for transfers between devices: 294 us -> 138 us
  matrix products: 117 us -> 0 us
  local copies, waits for them, and re-layouts: 107 us -> 15.2 us
  blocking collectives: 16.3 us -> 75.5 us
  Pallas kernels: 0 us -> 56.2 us
  other arithmetic: 56.1 us -> 0.3 us
    dot_general x13 -> x0, matrix products: 117 us -> none  [the longest x1 33 us: body(): jnp.einsum('chqk,cqhd->ckhd', d_scores, query_bf, preferred_element_type=...]
    unnamed x4 -> x2, waiting for transfers between devices: 67.1 us -> 0.03 us
    all_to_all x2 -> x3, waiting for transfers between devices: 99.6 us -> 42.7 us  [the longest x1 29.6 us: body(): lax.all_to_all(placed, BOTH, 0, 0, tiled=True)]
    pallas_call x0 -> x3, Pallas kernels: none -> 56.2 us  [the longest x1 48.1 us: attention(): pl.pallas_call(functools.partial(attention_kernel, first), grid=(steps,),...]
    convert_element_type x5 -> x0, local copies, waits for them, and re-layouts: 34.1 us -> none  [the longest x2 19.8 us: body(): key_unit, key_scale = unit_rows(key_heads.astype(jnp.float32))]
    all_to_all x1 -> x2, blocking collectives: 16.3 us -> 48 us  [the longest x1 24.6 us: body(): back = lax.all_to_all(jnp.swapaxes(summed, 0, 1), 'dp', 0, 0, tiled=True)]
    gather x5 -> x0, local copies, waits for them, and re-layouts: 29.9 us -> none  [the longest x4 24.4 us: picked(): fetched = jnp.take(source, jnp.maximum(position - 1, 0), axis=0)]
    select_n x9 -> x0, other arithmetic: 29.8 us -> none  [the longest x4 24.3 us: picked(): return jnp.where(present, fetched, jnp.zeros_like(fetched))]
  transfers between devices with their start and end apart: 5 -> 5, of which waited for: 4 -> 5; matrix products, arithmetic and copies ran while one was open for 9% -> 1% of each run, Pallas kernels for 0% -> 2%
where the time goes in v1:
time: 321 us; the launch traced here: 320 us
  waiting for transfers between devices  138 us (43%)
  blocking collectives  75.5 us (24%)
  Pallas kernels  56.2 us (18%)
  starting transfers between devices  19.5 us (6%)
  local copies, waits for them, and re-layouts  15.2 us (5%)
  between operations  14.8 us (5%)
    all_gather x1, waiting for transfers between devices, body(): lax.all_gather(jnp.swapaxes(got, 0, 1), 'enc', axis=0, tiled=False)  48.4 us
    pallas_call x1, Pallas kernels, attention(): pl.pallas_call(functools.partial(attention_kernel, first), grid=(steps,),...  48.1 us
    reduce_scatter x1, waiting for transfers between devices, body(): summed = lax.psum_scatter(part, 'enc', scatter_dimension=0, tiled=False)  47.3 us
    all_to_all x1, waiting for transfers between devices, body(): lax.all_to_all(placed, BOTH, 0, 0, tiled=True)  29.6 us
    unnamed x1, blocking collectives  27.6 us
    all_to_all x1, blocking collectives, body(): back = lax.all_to_all(jnp.swapaxes(summed, 0, 1), 'dp', 0, 0, tiled=True)  24.6 us
    all_to_all x1, blocking collectives, body(): got = lax.all_to_all(sent, 'dp', 0, 0, tiled=True)  23.3 us
    all_to_all x1, waiting for transfers between devices, body(): lax.all_to_all(acc.reshape(shards, -1, 2 * cols), 'dp', 0, 0, tiled=True)  12.3 us
  transfers between devices with their start and end apart: 5, of which 5 were waited for; matrix products, arithmetic and copies ran while one was open for 1% of the time, Pallas kernels for 2%

profile of v1, /device:TPU:1, one launch (start us, length us, event | category | flops | bytes accessed | tf_op | source)
XLA Modules:
  0.0 320.0 jit_solution(2906228015069770204)
XLA Ops:
  7.2 4.1 %copy.38 = bf16[16,128,512]{2,0,1:T(8,128)(2,1)} copy(bf16[16,128,512]{2,1,0:T(8,128)(2,1)} %param.7) | data formatting | bytes 4194304 | tf_op args[1]
  11.2 11.5 %all-to-all-start = ((bf16[128,16,512]{2,1,0:T(8,128)(2,1)}), bf16[128,16,512]{2,1,0:T(8,128)(2,1)S(1)}, u32[]{:S(2)}, u32[]{:S(2)}) async-start(bf16[128,16,512]{2,1,0:T(8,128)(2,1)} %bitcast.24), calls=%async_computation | async-start | bytes 4194304 | tf_op jit(solution)/shard_map/all_to_all | solution.py:183
  23.0 0.6 dynamic-slice
  24.3 0.2 dynamic-update-slice
  24.5 27.6 %all-reduce = s32[1024]{0:T(1024)S(1)} all-reduce(s32[1024]{0:T(1024)S(1)} %dynamic-update-slice), channel_id=1, replica_groups=mesh['enc'=4,'dp'=32] {'dp'}, use_global_device_ids=true, to_apply=%add | all-reduce | flops 1024 | bytes 8192
  52.3 0.8 all-to-all-done
  53.1 3.0 pick_rows.1
  56.2 23.3 %all_to_all.25 = bf16[32,32,512]{2,1,0:T(8,128)(2,1)S(1)} all-to-all(bf16[32,32,512]{2,1,0:T(8,128)(2,1)S(1)} %bitcast.20), channel_id=1, replica_groups=mesh['enc'=4,'dp'=32] {'dp'}, dimensions={0} | all-to-all | bytes 2097152 | tf_op jit(solution)/shard_map/all_to_all | solution.py:187
  79.5 1.5 copy.31
  81.7 0.5 copy.34.w_ref
  82.3 48.4 %all-gather.3.cloned.1.call-done = bf16[128,32,512]{2,1,0:T(8,128)(2,1)} async-done(((bf16[32,32,512]{2,1,0:T(8,128)(2,1)}), bf16[128,32,512]{2,1,0:T(8,128)(2,1)}) %all-gather.3.cloned.1.call-update) | async-done | bytes 4194320 | tf_op jit(solution)/shard_map/all_gather | solution.py:188
  130.6 1.2 copy-done
  131.9 1.2 copy-done.1
  133.1 48.1 %attention.1 = (bf16[16,64,512]{2,1,0:T(8,128)(2,1)}, bf16[16,64,512]{2,1,0:T(8,128)(2,1)}, bf16[4,32,32,512]{3,2,1,0:T(8,128)(2,1)}, bf16[512,1024]{1,0:T(8,128)(2,1)}) custom-call(bf16[4,32,32,512]{3,2,1,0:T(8,128)(2,1)} %bitcast.28, bf16[16,64,512]{2,1,0:T(8,128)(2,1)S(1)} %copy-done, bf16[16,64,512]{2,1,0:T(8,128)(2,1)S(1)} %copy-done.1, ...), custom_call_target="tpu_custom_call" | custom-call | flops 14400000000 | bytes 12800000 | tf_op jit(solution)/shard_map/attention/pallas_call | solution.py:102
  181.2 47.3 %reduce-scatter.2.cloned.1.call-done = bf16[1,32,32,512]{3,2,1,0:T(8,128)(2,1)} async-done(((bf16[4,32,32,512]{3,2,1,0:T(8,128)(2,1)}), bf16[1,32,32,512]{3,2,1,0:T(8,128)(2,1)}) %reduce-scatter.2.cloned.1.call-update) | async-done | bytes 1048592 | tf_op jit(solution)/shard_map/reduce_scatter | solution.py:194
  228.6 1.8 copy.35
  230.4 24.6 %all_to_all.26 = bf16[32,32,512]{2,1,0:T(8,128)(2,1)S(1)} all-to-all(bf16[32,32,512]{2,1,0:T(8,128)(2,1)S(1)} %copy.35), channel_id=1, replica_groups=mesh['enc'=4,'dp'=32] {'dp'}, dimensions={0} | all-to-all | bytes 2097152 | tf_op jit(solution)/shard_map/all_to_all | solution.py:195
  255.0 4.0 %all-to-all-start.4 = ((bf16[32,16,1024]{2,1,0:T(8,128)(2,1)}), bf16[32,16,1024]{2,1,0:T(8,128)(2,1)S(1)}, u32[]{:S(2)}, u32[]{:S(2)}) async-start(bf16[32,16,1024]{2,1,0:T(8,128)(2,1)} %bitcast.14), calls=%async_computation.5 | async-start | bytes 2097152 | tf_op jit(solution)/shard_map/all_to_all | solution.py:201
  259.0 5.0 %place_rows.1 = bf16[2048,512]{1,0:T(8,128)(2,1)} custom-call(s32[1,1024]{1,0:T(1,128)S(1)} %bitcast.23, bf16[1024,512]{1,0:T(8,128)(2,1)S(1)} %bitcast.21), custom_call_target="tpu_custom_call" | custom-call | tf_op jit(solution)/shard_map/place_rows/pallas_call | solution.py:156
  264.0 12.3 %all-to-all-done.4 = bf16[32,16,1024]{2,1,0:T(8,128)(2,1)S(1)} async-done(((bf16[32,16,1024]{2,1,0:T(8,128)(2,1)}), bf16[32,16,1024]{2,1,0:T(8,128)(2,1)S(1)}, u32[]{:S(2)}, u32[]{:S(2)}) %all-to-all-start.4) | async-done | bytes 1048608 | tf_op jit(solution)/shard_map/all_to_all | solution.py:201
  276.3 4.0 %all-to-all-start.3 = ((bf16[128,16,512]{2,1,0:T(8,128)(2,1)}), bf16[128,16,512]{2,1,0:T(8,128)(2,1)S(1)}, u32[]{:S(2)}, u32[]{:S(2)}) async-start(bf16[128,16,512]{2,1,0:T(8,128)(2,1)} %bitcast.12), calls=%async_computation.4 | async-start | bytes 4194304 | tf_op jit(solution)/shard_map/all_to_all | solution.py:200
  280.4 0.6 fusion.1
  281.1 29.6 %all-to-all-done.3 = bf16[128,16,512]{2,1,0:T(8,128)(2,1)S(1)} async-done(((bf16[128,16,512]{2,1,0:T(8,128)(2,1)}), bf16[128,16,512]{2,1,0:T(8,128)(2,1)S(1)}, u32[]{:S(2)}, u32[]{:S(2)}) %all-to-all-start.3) | async-done | bytes 2097184 | tf_op jit(solution)/shard_map/all_to_all | solution.py:200
  310.7 2.5 copy.36
  (22 shorter events, 1.3 us)
Async XLA Ops:
  11.2 11.6 %copy-start.4 = (s32[16,2]{0,1:T(2,128)S(1)}, s32[16,2]{0,1:T(2,128)}, u32[]{:S(2)}) copy-start(s32[16,2]{0,1:T(2,128)} %param.10) | copy-start | bytes 388
  11.2 11.8 %copy-start.5 = (u32[128]{0:T(128)S(1)}, u32[128]{0:T(128)}, u32[]{:S(2)}) copy-start(u32[128]{0:T(128)} %constant.8) | copy-start | bytes 1540
  11.2 41.9 %all-to-all-start = ((bf16[128,16,512]{2,1,0:T(8,128)(2,1)}), bf16[128,16,512]{2,1,0:T(8,128)(2,1)S(1)}, u32[]{:S(2)}, u32[]{:S(2)}) async-start(bf16[128,16,512]{2,1,0:T(8,128)(2,1)} %bitcast.24), calls=%async_computation | async-start | bytes 4194304 | tf_op jit(solution)/shard_map/all_to_all | solution.py:183
  22.7 107.9 %all-gather.3.cloned.1.call-start = ((), (), s32[]{:S(2)}) async-start(), calls=%async_computation.7 | async-start | bytes 5242880 | tf_op jit(solution)/shard_map/all_gather | solution.py:188
  79.5 1.6 copy-start.2
  79.5 1.9 copy-start.3
  81.1 147.5 %reduce-scatter.2.cloned.1.call-start = ((), (), s32[]{:S(2)}) async-start(), calls=%async_computation.6 | async-start | bytes 5242880 | tf_op jit(solution)/shard_map/reduce_scatter | solution.py:194
  130.6 1.2 copy-start
  131.9 1.2 copy-start.1
  255.0 21.3 %all-to-all-start.4 = ((bf16[32,16,1024]{2,1,0:T(8,128)(2,1)}), bf16[32,16,1024]{2,1,0:T(8,128)(2,1)S(1)}, u32[]{:S(2)}, u32[]{:S(2)}) async-start(bf16[32,16,1024]{2,1,0:T(8,128)(2,1)} %bitcast.14), calls=%async_computation.5 | async-start | bytes 2097152 | tf_op jit(solution)/shard_map/all_to_all | solution.py:201
  276.3 34.4 %all-to-all-start.3 = ((bf16[128,16,512]{2,1,0:T(8,128)(2,1)}), bf16[128,16,512]{2,1,0:T(8,128)(2,1)S(1)}, u32[]{:S(2)}, u32[]{:S(2)}) async-start(bf16[128,16,512]{2,1,0:T(8,128)(2,1)} %bitcast.12), calls=%async_computation.4 | async-start | bytes 4194304 | tf_op jit(solution)/shard_map/all_to_all | solution.py:200
Sparse Core Ops, SparseCore 0:
  81.2 49.3 all-gather.2
  181.4 47.1 reduce-scatter.1

commit v2 on v1

v2 whole, which is shorter than its diff:
```python
import functools
import math

import jax
import jax.numpy as jnp
from jax import lax
from jax.experimental import pallas as pl
from jax.experimental.pallas import tpu as pltpu
from jax.sharding import PartitionSpec as P

D_HEAD = 128
EPSILON = 1e-06
BOTH = ("enc", "dp")
CHUNKS = (8, 8)
PER_STEP = 2
PIECES = 4
FAR_FIRST = (2, 1, -1)
F32 = jnp.float32
BF16 = jnp.bfloat16
ROWS = (((0,), (0,)), ((), ()))
COLS = (((1,), (1,)), ((), ()))


def mm(a, b, dims=(((1,), (0,)), ((), ()))):
    return lax.dot_general(a, b, dims, preferred_element_type=F32)


def mean(value):
    return jnp.mean(value, axis=-1, keepdims=True)


def attention_kernel(first, *refs):
    x_refs, (q_ref, do_ref, w_ref) = refs[:PIECES], refs[PIECES : PIECES + 3]
    acc_in = None if first else refs[PIECES + 3]
    att_ref, dq_ref, *part_refs, dw_ref, acc = refs[PIECES + (3 if first else 6) :]
    step = pl.program_id(0)
    inverse = 1.0 / math.sqrt(D_HEAD)
    per_step, span, cols = q_ref.shape
    pairs, rows, width = x_refs[0].shape
    knb = pairs // per_step
    heads = cols // D_HEAD

    @pl.when(step == 0)
    def _():
        acc[...] = jnp.zeros_like(acc) if first else acc_in[...]

    heads_at = [slice(h * D_HEAD, (h + 1) * D_HEAD) for h in range(heads)]
    each = lambda f, *lists: [f(*parts) for parts in zip(*lists)]
    x = jnp.concatenate(
        [ref[s * knb : (s + 1) * knb].reshape(knb * rows, width) for s in range(per_step) for ref in x_refs], axis=0
    )
    count = knb * rows * len(x_refs)
    spans = [slice(s * count, (s + 1) * count) for s in range(per_step)]
    both = [(s, at) for s in range(per_step) for at in heads_at]
    queries = [q_ref[s, :, at].astype(F32) for s, at in both]
    grads = [do_ref[s, :, at] for s, at in both]
    query_scales = each(lambda q: lax.rsqrt(mean(q * q) + EPSILON), queries)
    query_units = each(lambda q, c: q * c, queries, query_scales)
    query_bfs = each(lambda u: u.astype(BF16), query_units)
    keys_all = mm(x, w_ref[:, :cols]).astype(BF16).astype(F32)
    keys = [keys_all[spans[s], at] for s, at in both]
    key_scales = each(lambda k: lax.rsqrt(mean(k * k) + EPSILON), keys)
    key_units = each(lambda k, c: k * c, keys, key_scales)
    key_bfs = each(lambda u: u.astype(BF16), key_units)
    values_all = mm(x, w_ref[:, cols:]).astype(BF16)
    values = [values_all[spans[s], at] for s, at in both]
    raised = each(lambda q, k: jnp.exp(mm(q, k, COLS) * inverse), query_bfs, key_bfs)
    d_probs = each(lambda g, v: mm(g, v, COLS), grads, values)
    weights = each(lambda e: e * (1.0 / jnp.sum(e, axis=-1, keepdims=True)), raised)
    probs = each(lambda p: p.astype(BF16), weights)
    attended = each(lambda p, v: mm(p, v).astype(BF16), probs, values)
    d_values = each(lambda p, g: mm(p, g, ROWS).astype(BF16), probs, grads)
    d_scores = each(
        lambda p, d: (p * (d - jnp.sum(d * p, axis=-1, keepdims=True)) * inverse).astype(BF16), weights, d_probs
    )
    d_query_units = each(lambda d, k: mm(d, k), d_scores, key_bfs)
    d_key_units = each(lambda d, q: mm(d, q, ROWS), d_scores, query_bfs)
    d_queries = each(
        lambda c, d, u: (c * (d - u * mean(d * u))).astype(BF16), query_scales, d_query_units, query_units
    )
    d_keys = each(lambda c, d, u: (c * (d - u * mean(d * u))).astype(BF16), key_scales, d_key_units, key_units)
    d_kv = []
    for s in range(per_step):
        mine = slice(s * heads, (s + 1) * heads)
        att_ref[s] = jnp.concatenate(attended[mine], axis=1)
        dq_ref[s] = jnp.concatenate(d_queries[mine], axis=1)
        d_kv.append(jnp.concatenate(d_keys[mine] + d_values[mine], axis=1))
    d_kv = jnp.concatenate(d_kv, axis=0)
    part = mm(d_kv, w_ref[...], COLS).astype(BF16)
    for s in range(per_step):
        for i, ref in enumerate(part_refs):
            at = s * count + i * knb * rows
            ref[s * knb : (s + 1) * knb] = part[at : at + knb * rows].reshape(knb, rows, width)
    acc[...] += mm(x, d_kv, ROWS)

    @pl.when(step == pl.num_programs(0) - 1)
    def _():
        dw_ref[...] = acc[...].astype(dw_ref.dtype)


def attention(chunk, pieces, queries, d_out, w, carried):
    _, span, cols = queries.shape
    pairs, rows, width = pieces[0].shape
    mine = CHUNKS[chunk]
    knb = pairs // mine
    steps = mine // PER_STEP
    first, last = chunk == 0, chunk == len(CHUNKS) - 1
    offset = sum(CHUNKS[:chunk]) // PER_STEP
    by_stretch = pl.BlockSpec((PER_STEP, span, cols), lambda i: (offset + i, 0, 0))
    by_pair = pl.BlockSpec((PER_STEP * knb, rows, width), lambda i: (i, 0, 0))
    whole = pl.BlockSpec(w.shape, lambda i: (0, 0))
    in_specs = [by_pair] * PIECES + [by_stretch] * 2 + [whole]
    args = [*pieces, queries, d_out, w]
    aliases = {}
    if not first:
        att, dq, acc = carried
        in_specs += [whole, pl.BlockSpec(memory_space=pl.ANY), pl.BlockSpec(memory_space=pl.ANY)]
        args += [acc, att, dq]
        aliases = {PIECES + 4: 0, PIECES + 5: 1}
    out = pl.pallas_call(
        functools.partial(attention_kernel, first),
        grid=(steps,),
        in_specs=in_specs,
        out_specs=[by_stretch, by_stretch] + [by_pair] * PIECES + [whole],
        out_shape=[jax.ShapeDtypeStruct(queries.shape, BF16)] * 2
        + [jax.ShapeDtypeStruct((pairs, rows, width), BF16)] * PIECES
        + [jax.ShapeDtypeStruct(w.shape, BF16 if last else F32)],
        scratch_shapes=[pltpu.VMEM(w.shape, F32)],
        input_output_aliases=aliases,
        compiler_params=pltpu.CompilerParams(vmem_limit_bytes=40 * 1024 * 1024),
        cost_estimate=pl.CostEstimate(
            flops=mine * 900_000_000, bytes_accessed=mine * 800_000, transcendentals=mine * 66_000
        ),
        name="attention",
    )(*args)
    return out[2:-1], (out[0], out[1], out[-1])


def pick_kernel(ids_ref, table_ref, out_ref):
    ids = ids_ref[...]
    count = table_ref.shape[0]
    hit = ids == lax.broadcasted_iota(jnp.int32, (ids.shape[0], count), 1)
    out_ref[...] = mm(hit.astype(BF16), table_ref[...]).astype(BF16)


def pick_rows(ids, table, tile=256):
    count, width = table.shape
    wanted = ids.shape[0]
    return pl.pallas_call(
        pick_kernel,
        grid=(wanted // tile,),
        in_specs=[
            pl.BlockSpec((tile, 1), lambda i: (i, 0)),
            pl.BlockSpec((count, width), lambda i: (0, 0)),
        ],
        out_specs=pl.BlockSpec((tile, width), lambda i: (i, 0)),
        out_shape=jax.ShapeDtypeStruct((wanted, width), BF16),
        compiler_params=pltpu.CompilerParams(vmem_limit_bytes=48 * 1024 * 1024),
        name="pick_rows",
    )(ids.reshape(wanted, 1), table)


def place_kernel(ids_ref, rows_ref, out_ref):
    ids = ids_ref[...]
    tile = out_ref.shape[0]
    row = lax.broadcasted_iota(jnp.int32, (tile, ids.shape[1]), 0) + pl.program_id(0) * tile
    out_ref[...] = mm((ids == row).astype(BF16), rows_ref[...]).astype(BF16)


def place_rows(ids, rows, count, tile=256):
    given, width = rows.shape
    return pl.pallas_call(
        place_kernel,
        grid=(count // tile,),
        in_specs=[
            pl.BlockSpec((1, given), lambda i: (0, 0)),
            pl.BlockSpec((given, width), lambda i: (0, 0)),
        ],
        out_specs=pl.BlockSpec((tile, width), lambda i: (i, 0)),
        out_shape=jax.ShapeDtypeStruct((count, width), BF16),
        compiler_params=pltpu.CompilerParams(vmem_limit_bytes=48 * 1024 * 1024),
        name="place_rows",
    )(ids.reshape(1, given), rows)


def shift(value, by):
    count = lax.axis_size("enc")
    return lax.ppermute(value, "enc", [(i, (i + by) % count) for i in range(count)])


def gather_pieces(own):
    return [own] + [shift(own, by) for by in FAR_FIRST]


def sum_pieces(parts):
    back = [shift(part, -by) for by, part in zip(FAR_FIRST, parts[1:])]
    return sum(part.astype(F32) for part in [parts[0], *back]).astype(BF16)


def body(queries, encodings, w_key, w_value, neighbours, d_out):
    enc_count = lax.axis_size("enc")
    shards = lax.axis_size("dp")
    devices = enc_count * shards
    held, neigh_len, width = encodings.shape
    stretches, _, cols = queries.shape
    pair_count = neighbours.size
    w = jnp.concatenate([w_key, w_value], axis=1)
    own_ids = jnp.broadcast_to(neighbours.reshape(1, -1), (shards, pair_count))
    ids = lax.all_to_all(own_ids, "dp", 0, 0, tiled=True).reshape(-1)
    by_row = jnp.swapaxes(encodings, 0, 1)
    table = lax.all_to_all(by_row, BOTH, 0, 0, tiled=True).reshape(devices * held, width)
    knb = pair_count // stretches
    sent, start = [], 0
    for size in CHUNKS:
        wanted = ids.reshape(shards, pair_count)[:, start * knb : (start + size) * knb]
        sent.append(pick_rows(wanted.reshape(-1), table).reshape(shards, size * knb, width))
        start += size
    pieces = []
    for c in range(len(CHUNKS)):
        if c > 0:
            sent[c], own = lax.optimization_barrier((sent[c], own))
            pieces.append(gather_pieces(own))
        own = jnp.swapaxes(lax.all_to_all(sent[c], "dp", 0, 0, tiled=True), 0, 1)
    pieces.append(gather_pieces(own))
    carried = None
    returned = []
    for c in range(len(CHUNKS)):
        parts, carried = attention(c, pieces[c], queries, d_out, w, carried)
        returned.append(sum_pieces(parts))
    att, dq, acc = carried
    d_w = lax.all_to_all(acc.reshape(shards, -1, 2 * cols), "dp", 0, 0, tiled=True)
    summed = jnp.swapaxes(jnp.concatenate(returned, axis=0), 0, 1)
    summed, d_w = lax.optimization_barrier((summed, d_w))
    rows = lax.all_to_all(summed, "dp", 0, 0, tiled=True).reshape(shards * pair_count, width)
    placed = place_rows(ids, rows, devices * held).reshape(devices, held, width)
    d_encodings = jnp.swapaxes(lax.all_to_all(placed, BOTH, 0, 0, tiled=True), 0, 1)
    d_w = jnp.sum(d_w.astype(F32), axis=0)
    return att, dq, d_encodings, d_w[:, :cols], d_w[:, cols:]


def solution(mesh):
    in_specs = (
        P("dp", None, "enc"),
        P(("enc", "dp"), None, None),
        P(None, "enc"),
        P(None, "enc"),
        P("dp", None),
        P("dp", None, "enc"),
    )
    out_specs = (
        P("dp", None, "enc"),
        P("dp", None, "enc"),
        P(("enc", "dp"), None, None),
        P("dp", "enc"),
        P("dp", "enc"),
    )
    return jax.shard_map(body, mesh=mesh, in_specs=in_specs, out_specs=out_specs, check_vma=False)
```

time: 321 us -> 243 us (0.76)
  blocking collectives: 75.5 us -> 0 us
  starting transfers between devices: 19.5 us -> 58.6 us
  Pallas kernels: 56.2 us -> 36.4 us
  waiting for transfers between devices: 138 us -> 120 us
  between operations: 14.8 us -> 0.81 us
  local copies, waits for them, and re-layouts: 15.2 us -> 21.6 us
  other arithmetic: 0.3 us -> 4.21 us
    all_gather x1 -> x0, waiting for transfers between devices: 48.4 us -> none  [body(): lax.all_gather(jnp.swapaxes(got, 0, 1), 'enc', axis=0, tiled=False)]
    all_to_all x2 -> x0, blocking collectives: 48 us -> none  [the longest x1 24.6 us: body(): back = lax.all_to_all(jnp.swapaxes(summed, 0, 1), 'dp', 0, 0, tiled=True)]
    reduce_scatter x1 -> x0, waiting for transfers between devices: 47.3 us -> none  [body(): summed = lax.psum_scatter(part, 'enc', scatter_dimension=0, tiled=False)]
    all_to_all x0 -> x4, waiting for transfers between devices: none -> 37.5 us  [the longest x2 18.8 us: body(): own = jnp.swapaxes(lax.all_to_all(sent[c], 'dp', 0, 0, tiled=True), 0, 1)]
    all_to_all x0 -> x4, starting transfers between devices: none -> 29.7 us  [the longest x2 10.8 us: body(): own = jnp.swapaxes(lax.all_to_all(sent[c], 'dp', 0, 0, tiled=True), 0, 1)]
    all_to_all x1, waiting for transfers between devices: 0.83 us -> 30.2 us  [body(): lax.all_to_all(by_row, BOTH, 0, 0, tiled=True)]
    unnamed x1 -> x0, blocking collectives: 27.6 us -> none
    ppermute x0 -> x12, waiting for transfers between devices: none -> 24.5 us  [shift(): lax.ppermute(value, 'enc', [(i, (i + by) % count) for i in range(count)])]
  transfers between devices with their start and end apart: 5 -> 19, of which waited for: 5 -> 11; matrix products, arithmetic and copies ran while one was open for 1% -> 6% of each run, Pallas kernels for 2% -> 12%
where the time goes in v2:
time: 243 us; the launch traced here: 242 us
  waiting for transfers between devices  120 us (49%)
  starting transfers between devices  58.6 us (24%)
  Pallas kernels  36.4 us (15%)
  local copies, waits for them, and re-layouts  21.6 us (9%)
  other arithmetic  4.21 us (2%)
    all_to_all x1, waiting for transfers between devices, body(): lax.all_to_all(by_row, BOTH, 0, 0, tiled=True)  30.2 us
    all_to_all x1, waiting for transfers between devices, body(): lax.all_to_all(placed, BOTH, 0, 0, tiled=True)  28.4 us
    pallas_call x2, Pallas kernels, attention(): pl.pallas_call(functools.partial(attention_kernel, first), grid=(steps,),...  26.9 us
    ppermute x12, waiting for transfers between devices, shift(): lax.ppermute(value, 'enc', [(i, (i + by) % count) for i in range(count)])  24.5 us
    all_to_all x2, waiting for transfers between devices, body(): own = jnp.swapaxes(lax.all_to_all(sent[c], 'dp', 0, 0, tiled=True), 0, 1)  18.8 us
    all_to_all x1, waiting for transfers between devices, body(): lax.all_to_all(summed, 'dp', 0, 0, tiled=True)  15.9 us
    unnamed x26, local copies, waits for them, and re-layouts  13.9 us
    ppermute x12, starting transfers between devices, shift(): lax.ppermute(value, 'enc', [(i, (i + by) % count) for i in range(count)])  13.3 us
  transfers between devices with their start and end apart: 19, of which 11 were waited for; matrix products, arithmetic and copies ran while one was open for 6% of the time, Pallas kernels for 12%

profile of v2, /device:TPU:1, one launch (start us, length us, event | category | flops | bytes accessed | tf_op | source)
XLA Modules:
  0.0 242.1 jit_solution(13196929365685776320)
XLA Ops:
  2.1 9.6 %all-to-all-start = ((s32[32,1,32]{2,1,0:T(1,128)}), s32[32,1,32]{2,1,0:T(1,128)S(1)}, u32[]{:S(2)}, u32[]{:S(2)}) async-start(s32[32,1,32]{2,1,0:T(1,128)} %broadcast_in_dim.8), calls=%async_computation | async-start | bytes 32768 | tf_op jit(solution)/shard_map/all_to_all | solution.py:209
  11.7 4.1 %copy.36 = bf16[16,128,512]{2,0,1:T(8,128)(2,1)} copy(bf16[16,128,512]{2,1,0:T(8,128)(2,1)} %param.7) | data formatting | bytes 4194304 | tf_op args[1]
  15.8 2.8 %all-to-all-done = s32[32,1,32]{2,1,0:T(1,128)S(1)} async-done(((s32[32,1,32]{2,1,0:T(1,128)}), s32[32,1,32]{2,1,0:T(1,128)S(1)}, u32[]{:S(2)}, u32[]{:S(2)}) %all-to-all-start) | async-done | bytes 4128 | tf_op jit(solution)/shard_map/all_to_all | solution.py:209
  18.6 6.5 %all-to-all-start.1 = ((bf16[128,16,512]{2,1,0:T(8,128)(2,1)}), bf16[128,16,512]{2,1,0:T(8,128)(2,1)S(1)}, u32[]{:S(2)}, u32[]{:S(2)}) async-start(bf16[128,16,512]{2,1,0:T(8,128)(2,1)} %bitcast.31), calls=%async_computation.1 | async-start | bytes 4194304 | tf_op jit(solution)/shard_map/all_to_all | solution.py:211
  25.3 30.2 %all-to-all-done.1 = bf16[128,16,512]{2,1,0:T(8,128)(2,1)S(1)} async-done(((bf16[128,16,512]{2,1,0:T(8,128)(2,1)}), bf16[128,16,512]{2,1,0:T(8,128)(2,1)S(1)}, u32[]{:S(2)}, u32[]{:S(2)}) %all-to-all-start.1) | async-done | bytes 2097184 | tf_op jit(solution)/shard_map/all_to_all | solution.py:211
  57.7 5.3 %all-to-all-start.2 = ((bf16[32,16,512]{2,1,0:T(8,128)(2,1)}), bf16[32,16,512]{2,1,0:T(8,128)(2,1)}, u32[]{:S(2)}, u32[]{:S(2)}) async-start(bf16[32,16,512]{2,1,0:T(8,128)(2,1)} %bitcast.4), calls=%async_computation.2 | async-start | bytes 1048576 | tf_op jit(solution)/shard_map/all_to_all | solution.py:223
  63.1 2.2 pick_rows.2
  65.4 9.3 %all-to-all-done.2 = bf16[32,16,512]{2,1,0:T(8,128)(2,1)} async-done(((bf16[32,16,512]{2,1,0:T(8,128)(2,1)}), bf16[32,16,512]{2,1,0:T(8,128)(2,1)}, u32[]{:S(2)}, u32[]{:S(2)}) %all-to-all-start.2) | async-done | bytes 524320 | tf_op jit(solution)/shard_map/all_to_all | solution.py:223
  77.5 2.3 collective-permute-start.5
  79.8 5.5 %all-to-all-start.3 = ((bf16[32,16,512]{2,1,0:T(8,128)(2,1)}), bf16[32,16,512]{2,1,0:T(8,128)(2,1)}, u32[]{:S(2)}, u32[]{:S(2)}) async-start(bf16[32,16,512]{2,1,0:T(8,128)(2,1)} %bitcast.3), calls=%async_computation.3 | async-start | bytes 1048576 | tf_op jit(solution)/shard_map/all_to_all | solution.py:223
  87.6 9.5 %all-to-all-done.3 = bf16[32,16,512]{2,1,0:T(8,128)(2,1)} async-done(((bf16[32,16,512]{2,1,0:T(8,128)(2,1)}), bf16[32,16,512]{2,1,0:T(8,128)(2,1)}, u32[]{:S(2)}, u32[]{:S(2)}) %all-to-all-start.3) | async-done | bytes 524320 | tf_op jit(solution)/shard_map/all_to_all | solution.py:223
  100.3 2.4 collective-permute-start.2
  105.1 13.8 %attention.2 = (bf16[16,64,512]{2,1,0:T(8,128)(2,1)}, bf16[16,64,512]{2,1,0:T(8,128)(2,1)}, bf16[16,32,512]{2,1,0:T(8,128)(2,1)S(1)}, bf16[16,32,512]{2,1,0:T(8,...) custom-call(bf16[16,32,512]{2,1,0:T(8,128)(2,1)S(1)} %bitcast.29, ...), custom_call_target="tpu_custom_call" | custom-call | flops 7200000000 | bytes 6400000 | tf_op jit(solution)/shard_map/attention/pallas_call | solution.py:120
  122.4 3.5 %collective-permute-done.1.refs_2_ = bf16[16,32,512]{2,1,0:T(8,128)(2,1)S(1)} collective-permute-done((bf16[16,32,512]{2,1,0:T(8,128)(2,1)S(1)}, bf16[16,32,512]{2,1,0:T(8,128)(2,1)S(1)}, u32[]{:S(2)}, u32[]{:S(2)}) %collective-permute-start.1) | collective-permute-done | bytes 524320 | tf_op jit(solution)/shard_map/ppermute | solution.py:188
  125.9 13.1 %attention.3 = (bf16[16,64,512]{2,1,0:T(8,128)(2,1)}, bf16[16,64,512]{2,1,0:T(8,128)(2,1)}, bf16[16,32,512]{2,1,0:T(8,128)(2,1)S(1)}, bf16[16,32,512]{2,1,0:T(8,...) custom-call(bf16[16,32,512]{2,1,0:T(8,128)(2,1)S(1)} %bitcast.25, ...), custom_call_target="tpu_custom_call", output_to_operand_aliasing={{0}: (8, {}), {1}: (9, {})} | custom-call | flops 7200000000 | bytes 6400000 | tf_op jit(solution)/shard_map/attention/pallas_call | solution.py:120
  141.4 5.0 %all-to-all-start.4 = ((bf16[32,16,1024]{2,1,0:T(8,128)(2,1)}), bf16[32,16,1024]{2,1,0:T(8,128)(2,1)}, u32[]{:S(2)}, u32[]{:S(2)}) async-start(bf16[32,16,1024]{2,1,0:T(8,128)(2,1)} %bitcast.8), calls=%async_computation.4 | async-start | bytes 2097152 | tf_op jit(solution)/shard_map/all_to_all | solution.py:231
  150.6 9.0 %collective-permute-done.10 = bf16[16,32,512]{2,1,0:T(8,128)(2,1)S(1)} collective-permute-done((bf16[16,32,512]{2,1,0:T(8,128)(2,1)S(1)}, bf16[16,32,512]{2,1,0:T(8,128)(2,1)S(1)}, u32[]{:S(2)}, u32[]{:S(2)}) %collective-permute-start.10) | collective-permute-done | bytes 524320 | tf_op jit(solution)/shard_map/ppermute | solution.py:188
  161.5 10.0 %collective-permute-done.9 = bf16[16,32,512]{2,1,0:T(8,128)(2,1)S(1)} collective-permute-done((bf16[16,32,512]{2,1,0:T(8,128)(2,1)S(1)}, bf16[16,32,512]{2,1,0:T(8,128)(2,1)S(1)}, u32[]{:S(2)}, u32[]{:S(2)}) %collective-permute-start.9) | collective-permute-done | bytes 524320 | tf_op jit(solution)/shard_map/ppermute | solution.py:188
  173.5 9.3 %all-to-all-start.5 = ((bf16[32,32,512]{2,1,0:T(8,128)(2,1)}), bf16[32,32,512]{2,1,0:T(8,128)(2,1)S(1)}, u32[]{:S(2)}, u32[]{:S(2)}) async-start(bf16[32,32,512]{2,1,0:T(8,128)(2,1)} %copy.31), calls=%async_computation.5 | async-start | bytes 2097152 | tf_op jit(solution)/shard_map/all_to_all | solution.py:234
  184.1 15.9 %all-to-all-done.5 = bf16[32,32,512]{2,1,0:T(8,128)(2,1)S(1)} async-done(((bf16[32,32,512]{2,1,0:T(8,128)(2,1)}), bf16[32,32,512]{2,1,0:T(8,128)(2,1)S(1)}, u32[]{:S(2)}, u32[]{:S(2)}) %all-to-all-start.5) | async-done | bytes 1048608 | tf_op jit(solution)/shard_map/all_to_all | solution.py:234
  200.0 5.0 %place_rows.1 = bf16[2048,512]{1,0:T(8,128)(2,1)} custom-call(s32[1,1024]{1,0:T(1,128)S(1)} %reshape_reshape.11.ids_ref, bf16[1024,512]{1,0:T(8,128)(2,1)S(1)} %bitcast.21), custom_call_target="tpu_custom_call" | custom-call | tf_op jit(solution)/shard_map/place_rows/pallas_call | solution.py:172
  205.0 4.2 %all-to-all-start.6 = ((bf16[128,16,512]{2,1,0:T(8,128)(2,1)}), bf16[128,16,512]{2,1,0:T(8,128)(2,1)S(1)}, u32[]{:S(2)}, u32[]{:S(2)}) async-start(bf16[128,16,512]{2,1,0:T(8,128)(2,1)} %bitcast.10), calls=%async_computation.6 | async-start | bytes 4194304 | tf_op jit(solution)/shard_map/all_to_all | solution.py:236
  211.2 28.4 %all-to-all-done.6 = bf16[128,16,512]{2,1,0:T(8,128)(2,1)S(1)} async-done(((bf16[128,16,512]{2,1,0:T(8,128)(2,1)}), bf16[128,16,512]{2,1,0:T(8,128)(2,1)S(1)}, u32[]{:S(2)}, u32[]{:S(2)}) %all-to-all-start.6) | async-done | bytes 2097184 | tf_op jit(solution)/shard_map/all_to_all | solution.py:236
  239.6 2.5 %copy.32 = bf16[16,128,512]{2,1,0:T(8,128)(2,1)} copy(bf16[16,128,512]{2,0,1:T(8,128)(2,1)S(1)} %bitcast.30) | data formatting | bytes 4194304
  (62 shorter events, 32.1 us)
Async XLA Ops:
  2.1 16.5 %all-to-all-start = ((s32[32,1,32]{2,1,0:T(1,128)}), s32[32,1,32]{2,1,0:T(1,128)S(1)}, u32[]{:S(2)}, u32[]{:S(2)}) async-start(s32[32,1,32]{2,1,0:T(1,128)} %broadcast_in_dim.8), calls=%async_computation | async-start | bytes 32768 | tf_op jit(solution)/shard_map/all_to_all | solution.py:209
  18.6 36.9 %all-to-all-start.1 = ((bf16[128,16,512]{2,1,0:T(8,128)(2,1)}), bf16[128,16,512]{2,1,0:T(8,128)(2,1)S(1)}, u32[]{:S(2)}, u32[]{:S(2)}) async-start(bf16[128,16,512]{2,1,0:T(8,128)(2,1)} %bitcast.31), calls=%async_computation.1 | async-start | bytes 4194304 | tf_op jit(solution)/shard_map/all_to_all | solution.py:211
  57.7 17.0 %all-to-all-start.2 = ((bf16[32,16,512]{2,1,0:T(8,128)(2,1)}), bf16[32,16,512]{2,1,0:T(8,128)(2,1)}, u32[]{:S(2)}, u32[]{:S(2)}) async-start(bf16[32,16,512]{2,1,0:T(8,128)(2,1)} %bitcast.4), calls=%async_computation.2 | async-start | bytes 1048576 | tf_op jit(solution)/shard_map/all_to_all | solution.py:223
  76.0 26.8 %copy-start = (bf16[16,64,512]{2,1,0:T(8,128)(2,1)S(1)}, bf16[16,64,512]{2,1,0:T(8,128)(2,1)}, u32[]{:S(2)}) copy-start(bf16[16,64,512]{2,1,0:T(8,128)(2,1)} %refs_4_.3) | copy-start | bytes 3145732
  76.0 23.5 %collective-permute-start.3 = (bf16[16,32,512]{2,1,0:T(8,128)(2,1)S(1)}, bf16[16,32,512]{2,1,0:T(8,128)(2,1)S(1)}, u32[]{:S(2)}, u32[]{:S(2)}) collective-permute-start(bf16[16,32,512]{2,1,0:T(8,128)(2,1)S(1)} %bitcast.26), channel_id=1, source_target_pairs={{0,64},{32,96},{64,0},{96,32},{1,65},{33,97},{65,1},{97,33},{2,66}... | collective-permute-start | bytes 1572872 | tf_op jit(solution)/shard_map/ppermute | solution.py:188
  77.2 25.7 %collective-permute-start.4 = (bf16[16,32,512]{2,1,0:T(8,128)(2,1)S(1)}, bf16[16,32,512]{2,1,0:T(8,128)(2,1)}, u32[]{:S(2)}, u32[]{:S(2)}) collective-permute-start(bf16[16,32,512]{2,1,0:T(8,128)(2,1)S(1)} %bitcast.27), channel_id=1, source_target_pairs={{0,32},{32,64},{64,96},{96,0},{1,33},{33,65},{65,97},{97,1},{2,34}... | collective-permute-start | bytes 1572872 | tf_op jit(solution)/shard_map/ppermute | solution.py:188
  77.5 25.3 %collective-permute-start.5 = (bf16[16,32,512]{2,1,0:T(8,128)(2,1)S(1)}, bf16[16,32,512]{2,1,0:T(8,128)(2,1)}, u32[]{:S(2)}, u32[]{:S(2)}) collective-permute-start(bf16[16,32,512]{2,1,0:T(8,128)(2,1)S(1)} %bitcast.28), channel_id=1, source_target_pairs={{0,96},{32,0},{64,32},{96,64},{1,97},{33,1},{65,33},{97,65},{2,98}... | collective-permute-start | bytes 1572872 | tf_op jit(solution)/shard_map/ppermute | solution.py:188
  79.8 17.2 %all-to-all-start.3 = ((bf16[32,16,512]{2,1,0:T(8,128)(2,1)}), bf16[32,16,512]{2,1,0:T(8,128)(2,1)}, u32[]{:S(2)}, u32[]{:S(2)}) async-start(bf16[32,16,512]{2,1,0:T(8,128)(2,1)} %bitcast.3), calls=%async_computation.3 | async-start | bytes 1048576 | tf_op jit(solution)/shard_map/all_to_all | solution.py:223
  97.0 28.8 %copy-start.2 = (bf16[16,64,512]{2,1,0:T(8,128)(2,1)S(1)}, bf16[16,64,512]{2,1,0:T(8,128)(2,1)}, u32[]{:S(2)}) copy-start(bf16[16,64,512]{2,1,0:T(8,128)(2,1)} %refs_5_.3) | copy-start | bytes 3145732
  98.5 23.9 %collective-permute-start = (bf16[16,32,512]{2,1,0:T(8,128)(2,1)S(1)}, bf16[16,32,512]{2,1,0:T(8,128)(2,1)S(1)}, u32[]{:S(2)}, u32[]{:S(2)}) collective-permute-start(bf16[16,32,512]{2,1,0:T(8,128)(2,1)S(1)} %bitcast.22), channel_id=1, source_target_pairs={{0,64},{32,96},{64,0},{96,32},{1,65},{33,97},{65,1},{97,33},{2,66}... | collective-permute-start | bytes 1572872 | tf_op jit(solution)/shard_map/ppermute | solution.py:188
  99.3 26.6 %collective-permute-start.1 = (bf16[16,32,512]{2,1,0:T(8,128)(2,1)S(1)}, bf16[16,32,512]{2,1,0:T(8,128)(2,1)S(1)}, u32[]{:S(2)}, u32[]{:S(2)}) collective-permute-start(bf16[16,32,512]{2,1,0:T(8,128)(2,1)S(1)} %bitcast.23), channel_id=1, source_target_pairs={{0,32},{32,64},{64,96},{96,0},{1,33},{33,65},{65,97},{97,1},{2,34}... | collective-permute-start | bytes 1572872 | tf_op jit(solution)/shard_map/ppermute | solution.py:188
  100.3 25.5 %collective-permute-start.2 = (bf16[16,32,512]{2,1,0:T(8,128)(2,1)S(1)}, bf16[16,32,512]{2,1,0:T(8,128)(2,1)S(1)}, u32[]{:S(2)}, u32[]{:S(2)}) collective-permute-start(bf16[16,32,512]{2,1,0:T(8,128)(2,1)S(1)} %bitcast.24), channel_id=1, source_target_pairs={{0,96},{32,0},{64,32},{96,64},{1,97},{33,1},{65,33},{97,65},{2,98}... | collective-permute-start | bytes 1572872 | tf_op jit(solution)/shard_map/ppermute | solution.py:188
  118.9 29.0 %collective-permute-start.6 = (bf16[16,32,512]{2,1,0:T(8,128)(2,1)}, bf16[16,32,512]{2,1,0:T(8,128)(2,1)}, u32[]{:S(2)}, u32[]{:S(2)}) collective-permute-start(bf16[16,32,512]{2,1,0:T(8,128)(2,1)} %get-tuple-element.31), channel_id=1, source_target_pairs={{0,64},{32,96},{64,0},{96,32},{1,65},{33,97},{65,1},{97,33},{2,66}... | collective-permute-start | bytes 1572872 | tf_op jit(solution)/shard_map/ppermute | solution.py:188
  120.2 28.8 %collective-permute-start.7 = (bf16[16,32,512]{2,1,0:T(8,128)(2,1)}, bf16[16,32,512]{2,1,0:T(8,128)(2,1)}, u32[]{:S(2)}, u32[]{:S(2)}) collective-permute-start(bf16[16,32,512]{2,1,0:T(8,128)(2,1)} %get-tuple-element.32), channel_id=1, source_target_pairs={{0,96},{32,0},{64,32},{96,64},{1,97},{33,1},{65,33},{97,65},{2,98}... | collective-permute-start | bytes 1572872 | tf_op jit(solution)/shard_map/ppermute | solution.py:188
  122.4 26.6 %collective-permute-start.8 = (bf16[16,32,512]{2,1,0:T(8,128)(2,1)}, bf16[16,32,512]{2,1,0:T(8,128)(2,1)}, u32[]{:S(2)}, u32[]{:S(2)}) collective-permute-start(bf16[16,32,512]{2,1,0:T(8,128)(2,1)} %get-tuple-element.33), channel_id=1, source_target_pairs={{0,32},{32,64},{64,96},{96,0},{1,33},{33,65},{65,97},{97,1},{2,34}... | collective-permute-start | bytes 1572872 | tf_op jit(solution)/shard_map/ppermute | solution.py:188
  141.4 5.0 %copy-start.10 = (bf16[16,32,512]{2,1,0:T(8,128)(2,1)S(1)}, bf16[16,32,512]{2,1,0:T(8,128)(2,1)}, u32[]{:S(2)}) copy-start(bf16[16,32,512]{2,1,0:T(8,128)(2,1)} %copy-done.9) | copy-start | bytes 1572868
  141.4 5.5 %copy-start.8 = (bf16[16,32,512]{2,1,0:T(8,128)(2,1)S(1)}, bf16[16,32,512]{2,1,0:T(8,128)(2,1)}, u32[]{:S(2)}) copy-start(bf16[16,32,512]{2,1,0:T(8,128)(2,1)} %copy-done.7) | copy-start | bytes 1572868
  141.4 6.5 %copy-start.4 = (bf16[16,32,512]{2,1,0:T(8,128)(2,1)S(1)}, bf16[16,32,512]{2,1,0:T(8,128)(2,1)}, u32[]{:S(2)}) copy-start(bf16[16,32,512]{2,1,0:T(8,128)(2,1)} %copy-done.3) | copy-start | bytes 1572868
  141.4 30.6 %all-to-all-start.4 = ((bf16[32,16,1024]{2,1,0:T(8,128)(2,1)}), bf16[32,16,1024]{2,1,0:T(8,128)(2,1)}, u32[]{:S(2)}, u32[]{:S(2)}) async-start(bf16[32,16,1024]{2,1,0:T(8,128)(2,1)} %bitcast.8), calls=%async_computation.4 | async-start | bytes 2097152 | tf_op jit(solution)/shard_map/all_to_all | solution.py:231
  146.4 13.3 %collective-permute-start.10 = (bf16[16,32,512]{2,1,0:T(8,128)(2,1)S(1)}, bf16[16,32,512]{2,1,0:T(8,128)(2,1)S(1)}, u32[]{:S(2)}, u32[]{:S(2)}) collective-permute-start(bf16[16,32,512]{2,1,0:T(8,128)(2,1)S(1)} %copy-done.10), channel_id=1, source_target_pairs={{0,96},{32,0},{64,32},{96,64},{1,97},{33,1},{65,33},{97,65},{2,98}... | collective-permute-start | bytes 1572872 | tf_op jit(solution)/shard_map/ppermute | solution.py:188
  146.9 14.6 %collective-permute-start.11 = (bf16[16,32,512]{2,1,0:T(8,128)(2,1)S(1)}, bf16[16,32,512]{2,1,0:T(8,128)(2,1)S(1)}, u32[]{:S(2)}, u32[]{:S(2)}) collective-permute-start(bf16[16,32,512]{2,1,0:T(8,128)(2,1)S(1)} %copy-done.8), channel_id=1, source_target_pairs={{0,32},{32,64},{64,96},{96,0},{1,33},{33,65},{65,97},{97,1},{2,34}... | collective-permute-start | bytes 1572872 | tf_op jit(solution)/shard_map/ppermute | solution.py:188
  147.9 23.6 %collective-permute-start.9 = (bf16[16,32,512]{2,1,0:T(8,128)(2,1)S(1)}, bf16[16,32,512]{2,1,0:T(8,128)(2,1)S(1)}, u32[]{:S(2)}, u32[]{:S(2)}) collective-permute-start(bf16[16,32,512]{2,1,0:T(8,128)(2,1)S(1)} %copy-done.4), channel_id=1, source_target_pairs={{0,64},{32,96},{64,0},{96,32},{1,65},{33,97},{65,1},{97,33},{2,66}... | collective-permute-start | bytes 1572872 | tf_op jit(solution)/shard_map/ppermute | solution.py:188
  173.5 26.5 %all-to-all-start.5 = ((bf16[32,32,512]{2,1,0:T(8,128)(2,1)}), bf16[32,32,512]{2,1,0:T(8,128)(2,1)S(1)}, u32[]{:S(2)}, u32[]{:S(2)}) async-start(bf16[32,32,512]{2,1,0:T(8,128)(2,1)} %copy.31), calls=%async_computation.5 | async-start | bytes 2097152 | tf_op jit(solution)/shard_map/all_to_all | solution.py:234
  205.0 34.6 %all-to-all-start.6 = ((bf16[128,16,512]{2,1,0:T(8,128)(2,1)}), bf16[128,16,512]{2,1,0:T(8,128)(2,1)S(1)}, u32[]{:S(2)}, u32[]{:S(2)}) async-start(bf16[128,16,512]{2,1,0:T(8,128)(2,1)} %bitcast.10), calls=%async_computation.6 | async-start | bytes 4194304 | tf_op jit(solution)/shard_map/all_to_all | solution.py:236
  (6 other events, 5.5 us)

commit v3 on v2

--- a/solution.py
+++ b/solution.py
@@ -14,6 +14,8 @@
 CHUNKS = (8, 8)
 PER_STEP = 2
 PIECES = 4
+LANES = 128
+EXTRA = 8
 FAR_FIRST = (2, 1, -1)
 F32 = jnp.float32
 BF16 = jnp.bfloat16
@@ -136,22 +138,54 @@
     return out[2:-1], (out[0], out[1], out[-1])
 
 
-def pick_kernel(ids_ref, table_ref, out_ref):
+def spread_kernel(x_ref, ids_ref, out_ref):
+    held, rows, width = x_ref.shape
+    count = held * rows
+    at = lax.broadcasted_iota(jnp.int32, (count, count), 0)
+    source = lax.rem(at, held) * rows + at // held
+    turn = (source == lax.broadcasted_iota(jnp.int32, (count, count), 1)).astype(BF16)
+    turned = mm(turn, x_ref[...].reshape(count, width)).astype(BF16).reshape(rows, held, width)
+    blocks = width // LANES
+    for i in range(blocks):
+        out_ref[:, i * held : (i + 1) * held] = turned[:, :, i * LANES : (i + 1) * LANES]
+    out_ref[:, blocks * held :] = jnp.broadcast_to(ids_ref[...], (rows, EXTRA, LANES))
+
+
+def spread_rows(x, ids, tile=16):
+    held, rows, width = x.shape
+    lines = width // LANES * held + EXTRA
+    return pl.pallas_call(
+        spread_kernel,
+        grid=(rows // tile,),
+        in_specs=[pl.BlockSpec((held, tile, width), lambda i: (0, i, 0)), pl.BlockSpec(ids.shape, lambda i: (0, 0))],
+        out_specs=pl.BlockSpec((tile, lines, LANES), lambda i: (i, 0, 0)),
+        out_shape=jax.ShapeDtypeStruct((rows, lines, LANES), BF16),
+        compiler_params=pltpu.CompilerParams(vmem_limit_bytes=32 * 1024 * 1024),
+        name="spread_rows",
+    )(x, ids)
+
+
+def pick_kernel(held, ids_ref, table_ref, out_ref):
     ids = ids_ref[...]
-    count = table_ref.shape[0]
-    hit = ids == lax.broadcasted_iota(jnp.int32, (ids.shape[0], count), 1)
-    out_ref[...] = mm(hit.astype(BF16), table_ref[...]).astype(BF16)
-
-
-def pick_rows(ids, table, tile=256):
-    count, width = table.shape
+    senders, lines, lanes = table_ref.shape
+    count = senders * held
+    hit = (ids == lax.broadcasted_iota(jnp.int32, (ids.shape[0], count), 1)).astype(BF16)
+    blocks = [table_ref[:, at : at + held].reshape(count, lanes) for at in range(0, lines - EXTRA, held)]
+    for i in range(0, len(blocks), 2):
+        picked = mm(hit, jnp.concatenate(blocks[i : i + 2], axis=1))
+        out_ref[:, i * lanes : (i + 2) * lanes] = picked.astype(BF16)
+
+
+def pick_rows(ids, table, held, tile=256):
+    senders, lines, lanes = table.shape
+    width = (lines - EXTRA) // held * lanes
     wanted = ids.shape[0]
     return pl.pallas_call(
-        pick_kernel,
+        functools.partial(pick_kernel, held),
         grid=(wanted // tile,),
         in_specs=[
             pl.BlockSpec((tile, 1), lambda i: (i, 0)),
-            pl.BlockSpec((count, width), lambda i: (0, 0)),
+            pl.BlockSpec(table.shape, lambda i: (0, 0, 0)),
         ],
         out_specs=pl.BlockSpec((tile, width), lambda i: (i, 0)),
         out_shape=jax.ShapeDtypeStruct((wanted, width), BF16),
@@ -167,7 +201,7 @@
     out_ref[...] = mm((ids == row).astype(BF16), rows_ref[...]).astype(BF16)
 
 
-def place_rows(ids, rows, count, tile=256):
+def place_rows(ids, rows, count, tile=512):
     given, width = rows.shape
     return pl.pallas_call(
         place_kernel,
@@ -205,15 +239,18 @@
     stretches, _, cols = queries.shape
     pair_count = neighbours.size
     w = jnp.concatenate([w_key, w_value], axis=1)
-    own_ids = jnp.broadcast_to(neighbours.reshape(1, -1), (shards, pair_count))
-    ids = lax.all_to_all(own_ids, "dp", 0, 0, tiled=True).reshape(-1)
-    by_row = jnp.swapaxes(encodings, 0, 1)
-    table = lax.all_to_all(by_row, BOTH, 0, 0, tiled=True).reshape(devices * held, width)
+    blocks = width // LANES
+    own_ids = neighbours.reshape(-1)
+    own_ids = jnp.stack([own_ids // held, own_ids % held]).astype(BF16)
+    by_row = spread_rows(encodings, jnp.pad(own_ids, ((0, EXTRA - 2), (0, LANES - pair_count))))
+    table = lax.all_to_all(by_row, BOTH, 0, 0, tiled=True)
+    ids = table[:shards, blocks * held : blocks * held + 2, :pair_count].astype(jnp.int32)
+    ids = ids[:, 0] * held + ids[:, 1]
     knb = pair_count // stretches
     sent, start = [], 0
     for size in CHUNKS:
-        wanted = ids.reshape(shards, pair_count)[:, start * knb : (start + size) * knb]
-        sent.append(pick_rows(wanted.reshape(-1), table).reshape(shards, size * knb, width))
+        wanted = ids[:, start * knb : (start + size) * knb]
+        sent.append(pick_rows(wanted.reshape(-1), table, held).reshape(shards, size * knb, width))
         start += size
     pieces = []
     for c in range(len(CHUNKS)):
@@ -232,7 +269,7 @@
     summed = jnp.swapaxes(jnp.concatenate(returned, axis=0), 0, 1)
     summed, d_w = lax.optimization_barrier((summed, d_w))
     rows = lax.all_to_all(summed, "dp", 0, 0, tiled=True).reshape(shards * pair_count, width)
-    placed = place_rows(ids, rows, devices * held).reshape(devices, held, width)
+    placed = place_rows(ids.reshape(-1), rows, devices * held).reshape(devices, held, width)
     d_encodings = jnp.swapaxes(lax.all_to_all(placed, BOTH, 0, 0, tiled=True), 0, 1)
     d_w = jnp.sum(d_w.astype(F32), axis=0)
     return att, dq, d_encodings, d_w[:, :cols], d_w[:, cols:]

time: 243 us -> 236 us (0.971)
  blocking collectives: 0 us -> 44.6 us
  waiting for transfers between devices: 120 us -> 88.8 us
  starting transfers between devices: 58.6 us -> 41.8 us
  local copies, waits for them, and re-layouts: 21.6 us -> 17.5 us
    all_to_all x0 -> x1, blocking collectives: none -> 44.6 us  [body(): table = lax.all_to_all(by_row, BOTH, 0, 0, tiled=True)]
    all_to_all x2 -> x0, waiting for transfers between devices: 32.9 us -> none  [the longest x1 30.2 us: body(): lax.all_to_all(by_row, BOTH, 0, 0, tiled=True)]
    all_to_all x2 -> x0, starting transfers between devices: 16.1 us -> none  [the longest x1 9.6 us: body(): ids = lax.all_to_all(own_ids, 'dp', 0, 0, tiled=True).reshape(-1)]
    unnamed x26 -> x27, local copies, waits for them, and re-layouts: 13.9 us -> 11.4 us
    pallas_call x2 -> x3, Pallas kernels: 4.45 us -> 6.56 us  [the longest x2 4.47 us: pick_rows(): pl.pallas_call(functools.partial(pick_kernel, held), grid=(wanted // tile...]
  transfers between devices with their start and end apart: 19 -> 17, of which waited for: 11 -> 9; matrix products, arithmetic and copies ran while one was open for 6% -> 3% of each run, Pallas kernels for 12% -> 12%
where the time goes in v3:
time: 236 us; the launch traced here: 235 us
  waiting for transfers between devices  88.8 us (38%)
  blocking collectives  44.6 us (19%)
  starting transfers between devices  41.8 us (18%)
  Pallas kernels  37.2 us (16%)
  local copies, waits for them, and re-layouts  17.5 us (7%)
  other arithmetic  4.27 us (2%)
    all_to_all x1, blocking collectives, body(): table = lax.all_to_all(by_row, BOTH, 0, 0, tiled=True)  44.6 us
    all_to_all x1, waiting for transfers between devices, body(): lax.all_to_all(placed, BOTH, 0, 0, tiled=True)  28.4 us
    pallas_call x2, Pallas kernels, attention(): pl.pallas_call(functools.partial(attention_kernel, first), grid=(steps,),...  26.9 us
    ppermute x12, waiting for transfers between devices, shift(): lax.ppermute(value, 'enc', [(i, (i + by) % count) for i in range(count)])  24.6 us
    all_to_all x2, waiting for transfers between devices, body(): own = jnp.swapaxes(lax.all_to_all(sent[c], 'dp', 0, 0, tiled=True), 0, 1)  18.7 us
    all_to_all x1, waiting for transfers between devices, body(): lax.all_to_all(summed, 'dp', 0, 0, tiled=True)  17.1 us
    ppermute x12, starting transfers between devices, shift(): lax.ppermute(value, 'enc', [(i, (i + by) % count) for i in range(count)])  13.2 us
    unnamed x27, local copies, waits for them, and re-layouts  11.4 us
  transfers between devices with their start and end apart: 17, of which 9 were waited for; matrix products, arithmetic and copies ran while one was open for 3% of the time, Pallas kernels for 12%

profile of v3, /device:TPU:1, one launch (start us, length us, event | category | flops | bytes accessed | tf_op | source)
XLA Modules:
  0.0 235.0 jit_solution(9716963838375596336)
XLA Ops:
  3.1 2.1 spread_rows.1
  5.2 44.6 %all_to_all.30.table_ref = bf16[128,72,128]{2,1,0:T(8,128)(2,1)S(1)} all-to-all(bf16[128,72,128]{2,1,0:T(8,128)(2,1)S(1)} %spread_rows.1), channel_id=1, replica_groups=mesh['enc'=4,'dp'=32] {'enc','dp'}, dimensions={0} | all-to-all | bytes 4718592 | tf_op jit(solution)/shard_map/all_to_all | solution.py:246
  51.3 2.2 pick_rows.3
  53.5 4.6 %all-to-all-start.1 = ((bf16[32,16,512]{2,1,0:T(8,128)(2,1)}), bf16[32,16,512]{2,1,0:T(8,128)(2,1)S(1)}, u32[]{:S(2)}, u32[]{:S(2)}) async-start(bf16[32,16,512]{2,1,0:T(8,128)(2,1)} %bitcast.2), calls=%async_computation.1 | async-start | bytes 1048576 | tf_op jit(solution)/shard_map/all_to_all | solution.py:260
  58.3 2.2 pick_rows.2
  60.5 9.3 %all-to-all-done.1 = bf16[32,16,512]{2,1,0:T(8,128)(2,1)S(1)} async-done(((bf16[32,16,512]{2,1,0:T(8,128)(2,1)}), bf16[32,16,512]{2,1,0:T(8,128)(2,1)S(1)}, u32[]{:S(2)}, u32[]{:S(2)}) %all-to-all-start.1) | async-done | bytes 524320 | tf_op jit(solution)/shard_map/all_to_all | solution.py:260
  71.6 2.4 %collective-permute-start.5 = (bf16[16,32,512]{2,1,0:T(8,128)(2,1)S(1)}, bf16[16,32,512]{2,1,0:T(8,128)(2,1)}, u32[]{:S(2)}, u32[]{:S(2)}) collective-permute-start(bf16[16,32,512]{2,1,0:T(8,128)(2,1)S(1)} %bitcast.22), channel_id=1, source_target_pairs={{0,96},{32,0},{64,32},{96,64},{1,97},{33,1},{65,33},{97,65},{2,98}... | collective-permute-start | bytes 1572872 | tf_op jit(solution)/shard_map/ppermute | solution.py:222
  74.0 5.5 %all-to-all-start.2 = ((bf16[32,16,512]{2,1,0:T(8,128)(2,1)}), bf16[32,16,512]{2,1,0:T(8,128)(2,1)}, u32[]{:S(2)}, u32[]{:S(2)}) async-start(bf16[32,16,512]{2,1,0:T(8,128)(2,1)} %bitcast.1), calls=%async_computation.2 | async-start | bytes 1048576 | tf_op jit(solution)/shard_map/all_to_all | solution.py:260
  81.7 9.5 %all-to-all-done.2 = bf16[32,16,512]{2,1,0:T(8,128)(2,1)} async-done(((bf16[32,16,512]{2,1,0:T(8,128)(2,1)}), bf16[32,16,512]{2,1,0:T(8,128)(2,1)}, u32[]{:S(2)}, u32[]{:S(2)}) %all-to-all-start.2) | async-done | bytes 524320 | tf_op jit(solution)/shard_map/all_to_all | solution.py:260
  94.4 2.4 %collective-permute-start.2 = (bf16[16,32,512]{2,1,0:T(8,128)(2,1)S(1)}, bf16[16,32,512]{2,1,0:T(8,128)(2,1)S(1)}, u32[]{:S(2)}, u32[]{:S(2)}) collective-permute-start(bf16[16,32,512]{2,1,0:T(8,128)(2,1)S(1)} %bitcast.18), channel_id=1, source_target_pairs={{0,96},{32,0},{64,32},{96,64},{1,97},{33,1},{65,33},{97,65},{2,98}... | collective-permute-start | bytes 1572872 | tf_op jit(solution)/shard_map/ppermute | solution.py:222
  99.1 13.8 %attention.2 = (bf16[16,64,512]{2,1,0:T(8,128)(2,1)}, bf16[16,64,512]{2,1,0:T(8,128)(2,1)}, bf16[16,32,512]{2,1,0:T(8,128)(2,1)S(1)}, bf16[16,32,512]{2,1,0:T(8,...) custom-call(bf16[16,32,512]{2,1,0:T(8,128)(2,1)S(1)} %bitcast.23, ...), custom_call_target="tpu_custom_call" | custom-call | flops 7200000000 | bytes 6400000 | tf_op jit(solution)/shard_map/attention/pallas_call | solution.py:122
  114.4 2.0 collective-permute-start.7
  116.4 3.6 %collective-permute-done.1.refs_2_ = bf16[16,32,512]{2,1,0:T(8,128)(2,1)S(1)} collective-permute-done((bf16[16,32,512]{2,1,0:T(8,128)(2,1)S(1)}, bf16[16,32,512]{2,1,0:T(8,128)(2,1)S(1)}, u32[]{:S(2)}, u32[]{:S(2)}) %collective-permute-start.1) | collective-permute-done | bytes 524320 | tf_op jit(solution)/shard_map/ppermute | solution.py:222
  120.0 13.1 %attention.3 = (bf16[16,64,512]{2,1,0:T(8,128)(2,1)}, bf16[16,64,512]{2,1,0:T(8,128)(2,1)}, bf16[16,32,512]{2,1,0:T(8,128)(2,1)S(1)}, bf16[16,32,512]{2,1,0:T(8,...) custom-call(bf16[16,32,512]{2,1,0:T(8,128)(2,1)S(1)} %bitcast.19, ...), custom_call_target="tpu_custom_call", output_to_operand_aliasing={{0}: (8, {}), {1}: (9, {})} | custom-call | flops 7200000000 | bytes 6400000 | tf_op jit(solution)/shard_map/attention/pallas_call | solution.py:122
  135.5 5.0 %all-to-all-start.3 = ((bf16[32,16,1024]{2,1,0:T(8,128)(2,1)}), bf16[32,16,1024]{2,1,0:T(8,128)(2,1)}, u32[]{:S(2)}, u32[]{:S(2)}) async-start(bf16[32,16,1024]{2,1,0:T(8,128)(2,1)} %bitcast.6), calls=%async_computation.3 | async-start | bytes 2097152 | tf_op jit(solution)/shard_map/all_to_all | solution.py:268
  144.7 9.1 %collective-permute-done.10 = bf16[16,32,512]{2,1,0:T(8,128)(2,1)S(1)} collective-permute-done((bf16[16,32,512]{2,1,0:T(8,128)(2,1)S(1)}, bf16[16,32,512]{2,1,0:T(8,128)(2,1)S(1)}, u32[]{:S(2)}, u32[]{:S(2)}) %collective-permute-start.10) | collective-permute-done | bytes 524320 | tf_op jit(solution)/shard_map/ppermute | solution.py:222
  153.8 2.0 collective-permute-done.11
  155.8 9.8 %collective-permute-done.9 = bf16[16,32,512]{2,1,0:T(8,128)(2,1)S(1)} collective-permute-done((bf16[16,32,512]{2,1,0:T(8,128)(2,1)S(1)}, bf16[16,32,512]{2,1,0:T(8,128)(2,1)S(1)}, u32[]{:S(2)}, u32[]{:S(2)}) %collective-permute-start.9) | collective-permute-done | bytes 524320 | tf_op jit(solution)/shard_map/ppermute | solution.py:222
  167.6 9.4 %all-to-all-start.4 = ((bf16[32,32,512]{2,1,0:T(8,128)(2,1)}), bf16[32,32,512]{2,1,0:T(8,128)(2,1)S(1)}, u32[]{:S(2)}, u32[]{:S(2)}) async-start(bf16[32,32,512]{2,1,0:T(8,128)(2,1)} %copy.30), calls=%async_computation.4 | async-start | bytes 2097152 | tf_op jit(solution)/shard_map/all_to_all | solution.py:271
  177.1 17.1 %all-to-all-done.4 = bf16[32,32,512]{2,1,0:T(8,128)(2,1)S(1)} async-done(((bf16[32,32,512]{2,1,0:T(8,128)(2,1)}), bf16[32,32,512]{2,1,0:T(8,128)(2,1)S(1)}, u32[]{:S(2)}, u32[]{:S(2)}) %all-to-all-start.4) | async-done | bytes 1048608 | tf_op jit(solution)/shard_map/all_to_all | solution.py:271
  194.2 3.7 %place_rows.1 = bf16[2048,512]{1,0:T(8,128)(2,1)} custom-call(s32[1,1024]{1,0:T(1,128)S(1)} %add.60.ids_ref, bf16[1024,512]{1,0:T(8,128)(2,1)S(1)} %bitcast.15), custom_call_target="tpu_custom_call" | custom-call | tf_op jit(solution)/shard_map/place_rows/pallas_call | solution.py:206
  197.9 4.2 %all-to-all-start.5 = ((bf16[128,16,512]{2,1,0:T(8,128)(2,1)}), bf16[128,16,512]{2,1,0:T(8,128)(2,1)S(1)}, u32[]{:S(2)}, u32[]{:S(2)}) async-start(bf16[128,16,512]{2,1,0:T(8,128)(2,1)} %bitcast.8), calls=%async_computation.5 | async-start | bytes 4194304 | tf_op jit(solution)/shard_map/all_to_all | solution.py:273
  204.1 28.4 %all-to-all-done.5 = bf16[128,16,512]{2,1,0:T(8,128)(2,1)S(1)} async-done(((bf16[128,16,512]{2,1,0:T(8,128)(2,1)}), bf16[128,16,512]{2,1,0:T(8,128)(2,1)S(1)}, u32[]{:S(2)}, u32[]{:S(2)}) %all-to-all-start.5) | async-done | bytes 2097184 | tf_op jit(solution)/shard_map/all_to_all | solution.py:273
  232.5 2.5 %copy.31 = bf16[16,128,512]{2,1,0:T(8,128)(2,1)} copy(bf16[16,128,512]{2,0,1:T(8,128)(2,1)S(1)} %bitcast.24) | data formatting | bytes 4194304
  (63 shorter events, 25.8 us)
Async XLA Ops:
  1.5 1.6 copy-start
  53.5 16.3 %all-to-all-start.1 = ((bf16[32,16,512]{2,1,0:T(8,128)(2,1)}), bf16[32,16,512]{2,1,0:T(8,128)(2,1)S(1)}, u32[]{:S(2)}, u32[]{:S(2)}) async-start(bf16[32,16,512]{2,1,0:T(8,128)(2,1)} %bitcast.2), calls=%async_computation.1 | async-start | bytes 1048576 | tf_op jit(solution)/shard_map/all_to_all | solution.py:260
  70.1 26.8 %copy-start.1 = (bf16[16,64,512]{2,1,0:T(8,128)(2,1)S(1)}, bf16[16,64,512]{2,1,0:T(8,128)(2,1)}, u32[]{:S(2)}) copy-start(bf16[16,64,512]{2,1,0:T(8,128)(2,1)} %refs_4_.3) | copy-start | bytes 3145732
  70.1 23.5 %collective-permute-start.3 = (bf16[16,32,512]{2,1,0:T(8,128)(2,1)S(1)}, bf16[16,32,512]{2,1,0:T(8,128)(2,1)S(1)}, u32[]{:S(2)}, u32[]{:S(2)}) collective-permute-start(bf16[16,32,512]{2,1,0:T(8,128)(2,1)S(1)} %bitcast.20), channel_id=1, source_target_pairs={{0,64},{32,96},{64,0},{96,32},{1,65},{33,97},{65,1},{97,33},{2,66}... | collective-permute-start | bytes 1572872 | tf_op jit(solution)/shard_map/ppermute | solution.py:222
  71.3 25.6 %collective-permute-start.4 = (bf16[16,32,512]{2,1,0:T(8,128)(2,1)S(1)}, bf16[16,32,512]{2,1,0:T(8,128)(2,1)}, u32[]{:S(2)}, u32[]{:S(2)}) collective-permute-start(bf16[16,32,512]{2,1,0:T(8,128)(2,1)S(1)} %bitcast.21), channel_id=1, source_target_pairs={{0,32},{32,64},{64,96},{96,0},{1,33},{33,65},{65,97},{97,1},{2,34}... | collective-permute-start | bytes 1572872 | tf_op jit(solution)/shard_map/ppermute | solution.py:222
  71.6 25.2 %collective-permute-start.5 = (bf16[16,32,512]{2,1,0:T(8,128)(2,1)S(1)}, bf16[16,32,512]{2,1,0:T(8,128)(2,1)}, u32[]{:S(2)}, u32[]{:S(2)}) collective-permute-start(bf16[16,32,512]{2,1,0:T(8,128)(2,1)S(1)} %bitcast.22), channel_id=1, source_target_pairs={{0,96},{32,0},{64,32},{96,64},{1,97},{33,1},{65,33},{97,65},{2,98}... | collective-permute-start | bytes 1572872 | tf_op jit(solution)/shard_map/ppermute | solution.py:222
  74.0 17.2 %all-to-all-start.2 = ((bf16[32,16,512]{2,1,0:T(8,128)(2,1)}), bf16[32,16,512]{2,1,0:T(8,128)(2,1)}, u32[]{:S(2)}, u32[]{:S(2)}) async-start(bf16[32,16,512]{2,1,0:T(8,128)(2,1)} %bitcast.1), calls=%async_computation.2 | async-start | bytes 1048576 | tf_op jit(solution)/shard_map/all_to_all | solution.py:260
  91.2 28.8 %copy-start.3 = (bf16[16,64,512]{2,1,0:T(8,128)(2,1)S(1)}, bf16[16,64,512]{2,1,0:T(8,128)(2,1)}, u32[]{:S(2)}) copy-start(bf16[16,64,512]{2,1,0:T(8,128)(2,1)} %refs_5_.3) | copy-start | bytes 3145732
  92.6 23.8 %collective-permute-start = (bf16[16,32,512]{2,1,0:T(8,128)(2,1)S(1)}, bf16[16,32,512]{2,1,0:T(8,128)(2,1)S(1)}, u32[]{:S(2)}, u32[]{:S(2)}) collective-permute-start(bf16[16,32,512]{2,1,0:T(8,128)(2,1)S(1)} %bitcast.16), channel_id=1, source_target_pairs={{0,64},{32,96},{64,0},{96,32},{1,65},{33,97},{65,1},{97,33},{2,66}... | collective-permute-start | bytes 1572872 | tf_op jit(solution)/shard_map/ppermute | solution.py:222
  93.3 26.7 %collective-permute-start.1 = (bf16[16,32,512]{2,1,0:T(8,128)(2,1)S(1)}, bf16[16,32,512]{2,1,0:T(8,128)(2,1)S(1)}, u32[]{:S(2)}, u32[]{:S(2)}) collective-permute-start(bf16[16,32,512]{2,1,0:T(8,128)(2,1)S(1)} %bitcast.17), channel_id=1, source_target_pairs={{0,32},{32,64},{64,96},{96,0},{1,33},{33,65},{65,97},{97,1},{2,34}... | collective-permute-start | bytes 1572872 | tf_op jit(solution)/shard_map/ppermute | solution.py:222
  94.4 25.6 %collective-permute-start.2 = (bf16[16,32,512]{2,1,0:T(8,128)(2,1)S(1)}, bf16[16,32,512]{2,1,0:T(8,128)(2,1)S(1)}, u32[]{:S(2)}, u32[]{:S(2)}) collective-permute-start(bf16[16,32,512]{2,1,0:T(8,128)(2,1)S(1)} %bitcast.18), channel_id=1, source_target_pairs={{0,96},{32,0},{64,32},{96,64},{1,97},{33,1},{65,33},{97,65},{2,98}... | collective-permute-start | bytes 1572872 | tf_op jit(solution)/shard_map/ppermute | solution.py:222
  96.8 1.2 copy-start.2
  112.9 29.1 %collective-permute-start.6 = (bf16[16,32,512]{2,1,0:T(8,128)(2,1)}, bf16[16,32,512]{2,1,0:T(8,128)(2,1)}, u32[]{:S(2)}, u32[]{:S(2)}) collective-permute-start(bf16[16,32,512]{2,1,0:T(8,128)(2,1)} %get-tuple-element.31), channel_id=1, source_target_pairs={{0,64},{32,96},{64,0},{96,32},{1,65},{33,97},{65,1},{97,33},{2,66}... | collective-permute-start | bytes 1572872 | tf_op jit(solution)/shard_map/ppermute | solution.py:222
  114.4 28.6 %collective-permute-start.7 = (bf16[16,32,512]{2,1,0:T(8,128)(2,1)}, bf16[16,32,512]{2,1,0:T(8,128)(2,1)}, u32[]{:S(2)}, u32[]{:S(2)}) collective-permute-start(bf16[16,32,512]{2,1,0:T(8,128)(2,1)} %get-tuple-element.32), channel_id=1, source_target_pairs={{0,96},{32,0},{64,32},{96,64},{1,97},{33,1},{65,33},{97,65},{2,98}... | collective-permute-start | bytes 1572872 | tf_op jit(solution)/shard_map/ppermute | solution.py:222
  116.4 26.6 %collective-permute-start.8 = (bf16[16,32,512]{2,1,0:T(8,128)(2,1)}, bf16[16,32,512]{2,1,0:T(8,128)(2,1)}, u32[]{:S(2)}, u32[]{:S(2)}) collective-permute-start(bf16[16,32,512]{2,1,0:T(8,128)(2,1)} %get-tuple-element.33), channel_id=1, source_target_pairs={{0,32},{32,64},{64,96},{96,0},{1,33},{33,65},{65,97},{97,1},{2,34}... | collective-permute-start | bytes 1572872 | tf_op jit(solution)/shard_map/ppermute | solution.py:222
  135.5 5.0 %copy-start.11 = (bf16[16,32,512]{2,1,0:T(8,128)(2,1)S(1)}, bf16[16,32,512]{2,1,0:T(8,128)(2,1)}, u32[]{:S(2)}) copy-start(bf16[16,32,512]{2,1,0:T(8,128)(2,1)} %copy-done.10) | copy-start | bytes 1572868
  135.5 5.5 %copy-start.9 = (bf16[16,32,512]{2,1,0:T(8,128)(2,1)S(1)}, bf16[16,32,512]{2,1,0:T(8,128)(2,1)}, u32[]{:S(2)}) copy-start(bf16[16,32,512]{2,1,0:T(8,128)(2,1)} %copy-done.8) | copy-start | bytes 1572868
  135.5 6.5 %copy-start.5 = (bf16[16,32,512]{2,1,0:T(8,128)(2,1)S(1)}, bf16[16,32,512]{2,1,0:T(8,128)(2,1)}, u32[]{:S(2)}) copy-start(bf16[16,32,512]{2,1,0:T(8,128)(2,1)} %copy-done.4) | copy-start | bytes 1572868
  135.5 30.5 %all-to-all-start.3 = ((bf16[32,16,1024]{2,1,0:T(8,128)(2,1)}), bf16[32,16,1024]{2,1,0:T(8,128)(2,1)}, u32[]{:S(2)}, u32[]{:S(2)}) async-start(bf16[32,16,1024]{2,1,0:T(8,128)(2,1)} %bitcast.6), calls=%async_computation.3 | async-start | bytes 2097152 | tf_op jit(solution)/shard_map/all_to_all | solution.py:268
  140.5 13.3 %collective-permute-start.10 = (bf16[16,32,512]{2,1,0:T(8,128)(2,1)S(1)}, bf16[16,32,512]{2,1,0:T(8,128)(2,1)S(1)}, u32[]{:S(2)}, u32[]{:S(2)}) collective-permute-start(bf16[16,32,512]{2,1,0:T(8,128)(2,1)S(1)} %copy-done.11), channel_id=1, source_target_pairs={{0,96},{32,0},{64,32},{96,64},{1,97},{33,1},{65,33},{97,65},{2,98}... | collective-permute-start | bytes 1572872 | tf_op jit(solution)/shard_map/ppermute | solution.py:222
  141.1 14.7 %collective-permute-start.11 = (bf16[16,32,512]{2,1,0:T(8,128)(2,1)S(1)}, bf16[16,32,512]{2,1,0:T(8,128)(2,1)S(1)}, u32[]{:S(2)}, u32[]{:S(2)}) collective-permute-start(bf16[16,32,512]{2,1,0:T(8,128)(2,1)S(1)} %copy-done.9), channel_id=1, source_target_pairs={{0,32},{32,64},{64,96},{96,0},{1,33},{33,65},{65,97},{97,1},{2,34}... | collective-permute-start | bytes 1572872 | tf_op jit(solution)/shard_map/ppermute | solution.py:222
  142.1 23.5 %collective-permute-start.9 = (bf16[16,32,512]{2,1,0:T(8,128)(2,1)S(1)}, bf16[16,32,512]{2,1,0:T(8,128)(2,1)S(1)}, u32[]{:S(2)}, u32[]{:S(2)}) collective-permute-start(bf16[16,32,512]{2,1,0:T(8,128)(2,1)S(1)} %copy-done.5), channel_id=1, source_target_pairs={{0,64},{32,96},{64,0},{96,32},{1,65},{33,97},{65,1},{97,33},{2,66}... | collective-permute-start | bytes 1572872 | tf_op jit(solution)/shard_map/ppermute | solution.py:222
  167.6 26.6 %all-to-all-start.4 = ((bf16[32,32,512]{2,1,0:T(8,128)(2,1)}), bf16[32,32,512]{2,1,0:T(8,128)(2,1)S(1)}, u32[]{:S(2)}, u32[]{:S(2)}) async-start(bf16[32,32,512]{2,1,0:T(8,128)(2,1)} %copy.30), calls=%async_computation.4 | async-start | bytes 2097152 | tf_op jit(solution)/shard_map/all_to_all | solution.py:271
  197.9 34.6 %all-to-all-start.5 = ((bf16[128,16,512]{2,1,0:T(8,128)(2,1)}), bf16[128,16,512]{2,1,0:T(8,128)(2,1)S(1)}, u32[]{:S(2)}, u32[]{:S(2)}) async-start(bf16[128,16,512]{2,1,0:T(8,128)(2,1)} %bitcast.8), calls=%async_computation.5 | async-start | bytes 4194304 | tf_op jit(solution)/shard_map/all_to_all | solution.py:273
  (5 other events, 4.3 us)

commit v4 on v3

--- a/solution.py
+++ b/solution.py
@@ -31,7 +31,11 @@
     return jnp.mean(value, axis=-1, keepdims=True)
 
 
-def attention_kernel(first, *refs):
+def cuts(piece, rows, last):
+    return [(0, rows // 2), (rows // 2, rows)] if last and piece else [(0, rows)]
+
+
+def attention_kernel(first, last, *refs):
     x_refs, (q_ref, do_ref, w_ref) = refs[:PIECES], refs[PIECES : PIECES + 3]
     acc_in = None if first else refs[PIECES + 3]
     att_ref, dq_ref, *part_refs, dw_ref, acc = refs[PIECES + (3 if first else 6) :]
@@ -90,9 +94,12 @@
     d_kv = jnp.concatenate(d_kv, axis=0)
     part = mm(d_kv, w_ref[...], COLS).astype(BF16)
     for s in range(per_step):
-        for i, ref in enumerate(part_refs):
+        outs = iter(part_refs)
+        for i in range(PIECES):
             at = s * count + i * knb * rows
-            ref[s * knb : (s + 1) * knb] = part[at : at + knb * rows].reshape(knb, rows, width)
+            piece = part[at : at + knb * rows].reshape(knb, rows, width)
+            for low, high in cuts(i, rows, last):
+                next(outs)[s * knb : (s + 1) * knb] = piece[:, low:high]
     acc[...] += mm(x, d_kv, ROWS)
 
     @pl.when(step == pl.num_programs(0) - 1)
@@ -119,13 +126,16 @@
         in_specs += [whole, pl.BlockSpec(memory_space=pl.ANY), pl.BlockSpec(memory_space=pl.ANY)]
         args += [acc, att, dq]
         aliases = {PIECES + 4: 0, PIECES + 5: 1}
+    sizes = [high - low for i in range(PIECES) for low, high in cuts(i, rows, last)]
     out = pl.pallas_call(
-        functools.partial(attention_kernel, first),
+        functools.partial(attention_kernel, first, last),
         grid=(steps,),
         in_specs=in_specs,
-        out_specs=[by_stretch, by_stretch] + [by_pair] * PIECES + [whole],
+        out_specs=[by_stretch, by_stretch]
+        + [pl.BlockSpec((PER_STEP * knb, size, width), lambda i: (i, 0, 0)) for size in sizes]
+        + [whole],
         out_shape=[jax.ShapeDtypeStruct(queries.shape, BF16)] * 2
-        + [jax.ShapeDtypeStruct((pairs, rows, width), BF16)] * PIECES
+        + [jax.ShapeDtypeStruct((pairs, size, width), BF16) for size in sizes]
         + [jax.ShapeDtypeStruct(w.shape, BF16 if last else F32)],
         scratch_shapes=[pltpu.VMEM(w.shape, F32)],
         input_output_aliases=aliases,
@@ -229,6 +239,16 @@
 def sum_pieces(parts):
     back = [shift(part, -by) for by, part in zip(FAR_FIRST, parts[1:])]
     return sum(part.astype(F32) for part in [parts[0], *back]).astype(BF16)
+
+
+def sum_halves(parts, earlier):
+    own, far_a, far_b, left_a, left_b, right_a, right_b = parts
+    add = lambda *terms: sum(term.astype(F32) for term in terms).astype(BF16)
+    far_a, far_b = shift(far_a, 1), shift(far_b, -1)
+    right_b, left_a = shift(right_b, 1), shift(left_a, -1)
+    far_a, far_b, *earlier = lax.optimization_barrier((far_a, far_b, *earlier))
+    right_a, left_b = shift(add(right_a, far_a), 1), shift(add(left_b, far_b), -1)
+    return *earlier, add(own, jnp.concatenate([right_a, right_b], axis=1), jnp.concatenate([left_a, left_b], axis=1))
 
 
 def body(queries, encodings, w_key, w_value, neighbours, d_out):
@@ -263,7 +283,9 @@
     returned = []
     for c in range(len(CHUNKS)):
         parts, carried = attention(c, pieces[c], queries, d_out, w, carried)
-        returned.append(sum_pieces(parts))
+        if c < len(CHUNKS) - 1:
+            returned.append(sum_pieces(parts))
+    returned = sum_halves(parts, returned)
     att, dq, acc = carried
     d_w = lax.all_to_all(acc.reshape(shards, -1, 2 * cols), "dp", 0, 0, tiled=True)
     summed = jnp.swapaxes(jnp.concatenate(returned, axis=0), 0, 1)

time: 236 us -> 227 us (0.962)
  waiting for transfers between devices: 88.8 us -> 74.6 us
  starting transfers between devices: 41.8 us -> 46.6 us
    ppermute x12 -> x15, waiting for transfers between devices: 24.6 us -> 10.4 us  [shift(): lax.ppermute(value, 'enc', [(i, (i + by) % count) for i in range(count)])]
    ppermute x12 -> x15, starting transfers between devices: 13.2 us -> 19.4 us  [shift(): lax.ppermute(value, 'enc', [(i, (i + by) % count) for i in range(count)])]
    all_to_all x1, starting transfers between devices: 9.41 us -> 5.34 us  [body(): lax.all_to_all(summed, 'dp', 0, 0, tiled=True)]
    unnamed x27 -> x23, local copies, waits for them, and re-layouts: 11.4 us -> 12.8 us
  transfers between devices with their start and end apart: 17 -> 20, of which waited for: 9 -> 10; matrix products, arithmetic and copies ran while one was open for 3% -> 4% of each run, Pallas kernels for 12% -> 12%
where the time goes in v4:
time: 227 us; the launch traced here: 226 us
  waiting for transfers between devices  74.6 us (33%)
  starting transfers between devices  46.6 us (21%)
  blocking collectives  44.6 us (20%)
  Pallas kernels  36.3 us (16%)
  local copies, waits for them, and re-layouts  18.8 us (8%)
  other arithmetic  4.32 us (2%)
    all_to_all x1, blocking collectives, body(): table = lax.all_to_all(by_row, BOTH, 0, 0, tiled=True)  44.6 us
    all_to_all x1, waiting for transfers between devices, body(): lax.all_to_all(placed, BOTH, 0, 0, tiled=True)  28.4 us
    pallas_call x2, Pallas kernels, attention(): pl.pallas_call(functools.partial(attention_kernel, first, last), grid=(st...  26 us
    ppermute x15, starting transfers between devices, shift(): lax.ppermute(value, 'enc', [(i, (i + by) % count) for i in range(count)])  19.4 us
    all_to_all x2, waiting for transfers between devices, body(): own = jnp.swapaxes(lax.all_to_all(sent[c], 'dp', 0, 0, tiled=True), 0, 1)  18.7 us
    all_to_all x1, waiting for transfers between devices, body(): lax.all_to_all(summed, 'dp', 0, 0, tiled=True)  17.1 us
    unnamed x23, local copies, waits for them, and re-layouts  12.8 us
    ppermute x15, waiting for transfers between devices, shift(): lax.ppermute(value, 'enc', [(i, (i + by) % count) for i in range(count)])  10.4 us
  transfers between devices with their start and end apart: 20, of which 10 were waited for; matrix products, arithmetic and copies ran while one was open for 4% of the time, Pallas kernels for 12%

profile of v4, /device:TPU:1, one launch (start us, length us, event | category | flops | bytes accessed | tf_op | source)
XLA Modules:
  0.0 226.0 jit_solution(3542405267087728071)
XLA Ops:
  3.1 2.1 spread_rows.1
  5.2 44.6 %all_to_all.30.table_ref = bf16[128,72,128]{2,1,0:T(8,128)(2,1)S(1)} all-to-all(bf16[128,72,128]{2,1,0:T(8,128)(2,1)S(1)} %spread_rows.1), channel_id=1, replica_groups=mesh['enc'=4,'dp'=32] {'enc','dp'}, dimensions={0} | all-to-all | bytes 4718592 | tf_op jit(solution)/shard_map/all_to_all | solution.py:266
  51.3 2.2 pick_rows.3
  53.5 4.6 %all-to-all-start.1 = ((bf16[32,16,512]{2,1,0:T(8,128)(2,1)}), bf16[32,16,512]{2,1,0:T(8,128)(2,1)S(1)}, u32[]{:S(2)}, u32[]{:S(2)}) async-start(bf16[32,16,512]{2,1,0:T(8,128)(2,1)} %bitcast.2), calls=%async_computation.1 | async-start | bytes 1048576 | tf_op jit(solution)/shard_map/all_to_all | solution.py:280
  58.3 2.2 pick_rows.2
  60.5 9.3 %all-to-all-done.1 = bf16[32,16,512]{2,1,0:T(8,128)(2,1)S(1)} async-done(((bf16[32,16,512]{2,1,0:T(8,128)(2,1)}), bf16[32,16,512]{2,1,0:T(8,128)(2,1)S(1)}, u32[]{:S(2)}, u32[]{:S(2)}) %all-to-all-start.1) | async-done | bytes 524320 | tf_op jit(solution)/shard_map/all_to_all | solution.py:280
  71.6 2.4 %collective-permute-start.5 = (bf16[16,32,512]{2,1,0:T(8,128)(2,1)S(1)}, bf16[16,32,512]{2,1,0:T(8,128)(2,1)S(1)}, u32[]{:S(2)}, u32[]{:S(2)}) collective-permute-start(bf16[16,32,512]{2,1,0:T(8,128)(2,1)S(1)} %bitcast.22), channel_id=1, source_target_pairs={{0,96},{32,0},{64,32},{96,64},{1,97},{33,1},{65,33},{97,65},{2,98}... | collective-permute-start | bytes 1572872 | tf_op jit(solution)/shard_map/ppermute | solution.py:232
  73.9 5.5 %all-to-all-start.2 = ((bf16[32,16,512]{2,1,0:T(8,128)(2,1)}), bf16[32,16,512]{2,1,0:T(8,128)(2,1)}, u32[]{:S(2)}, u32[]{:S(2)}) async-start(bf16[32,16,512]{2,1,0:T(8,128)(2,1)} %bitcast.1), calls=%async_computation.2 | async-start | bytes 1048576 | tf_op jit(solution)/shard_map/all_to_all | solution.py:280
  81.7 9.5 %all-to-all-done.2 = bf16[32,16,512]{2,1,0:T(8,128)(2,1)} async-done(((bf16[32,16,512]{2,1,0:T(8,128)(2,1)}), bf16[32,16,512]{2,1,0:T(8,128)(2,1)}, u32[]{:S(2)}, u32[]{:S(2)}) %all-to-all-start.2) | async-done | bytes 524320 | tf_op jit(solution)/shard_map/all_to_all | solution.py:280
  93.5 2.4 %collective-permute-start.2 = (bf16[16,32,512]{2,1,0:T(8,128)(2,1)S(1)}, bf16[16,32,512]{2,1,0:T(8,128)(2,1)S(1)}, u32[]{:S(2)}, u32[]{:S(2)}) collective-permute-start(bf16[16,32,512]{2,1,0:T(8,128)(2,1)S(1)} %bitcast.18), channel_id=1, source_target_pairs={{0,96},{32,0},{64,32},{96,64},{1,97},{33,1},{65,33},{97,65},{2,98}... | collective-permute-start | bytes 1572872 | tf_op jit(solution)/shard_map/ppermute | solution.py:232
  102.8 12.8 %attention.2 = (bf16[16,64,512]{2,1,0:T(8,128)(2,1)}, bf16[16,64,512]{2,1,0:T(8,128)(2,1)}, bf16[16,32,512]{2,1,0:T(8,128)(2,1)S(1)}, bf16[16,32,512]{2,1,0:T(8,...) custom-call(bf16[16,32,512]{2,1,0:T(8,128)(2,1)S(1)} %bitcast.23, ...), custom_call_target="tpu_custom_call" | custom-call | flops 7200000000 | bytes 6400000 | tf_op jit(solution)/shard_map/attention/pallas_call | solution.py:130
  119.2 13.2 %attention.3 = (bf16[16,64,512]{2,1,0:T(8,128)(2,1)}, bf16[16,64,512]{2,1,0:T(8,128)(2,1)}, bf16[16,32,512]{2,1,0:T(8,128)(2,1)S(1)}, bf16[16,16,512]{2,1,0:T(8,...) custom-call(bf16[16,32,512]{2,1,0:T(8,128)(2,1)S(1)} %bitcast.19, ...), custom_call_target="tpu_custom_call", output_to_operand_aliasing={{0}: (8, {}), {1}: (9, {})} | custom-call | flops 7200000000 | bytes 6400000 | tf_op jit(solution)/shard_map/attention/pallas_call | solution.py:130
  133.4 2.5 %collective-permute-start.7 = (bf16[16,16,512]{2,1,0:T(8,128)(2,1)}, bf16[16,16,512]{2,1,0:T(8,128)(2,1)S(1)}, u32[]{:S(2)}, u32[]{:S(2)}) collective-permute-start(bf16[16,16,512]{2,1,0:T(8,128)(2,1)} %get-tuple-element.37), channel_id=1, source_target_pairs={{0,96},{32,0},{64,32},{96,64},{1,97},{33,1},{65,33},{97,65},{2,98}... | collective-permute-start | bytes 786440 | tf_op jit(solution)/shard_map/ppermute | solution.py:232
  135.8 6.2 %all-to-all-start.3 = ((bf16[32,16,1024]{2,1,0:T(8,128)(2,1)}), bf16[32,16,1024]{2,1,0:T(8,128)(2,1)}, u32[]{:S(2)}, u32[]{:S(2)}) async-start(bf16[32,16,1024]{2,1,0:T(8,128)(2,1)} %bitcast.6), calls=%async_computation.3 | async-start | bytes 2097152 | tf_op jit(solution)/shard_map/all_to_all | solution.py:290
  142.1 2.7 %collective-permute-start.13 = (bf16[16,16,512]{2,1,0:T(8,128)(2,1)S(1)}, bf16[16,16,512]{2,1,0:T(8,128)(2,1)S(1)}, u32[]{:S(2)}, u32[]{:S(2)}) collective-permute-start(bf16[16,16,512]{2,1,0:T(8,128)(2,1)S(1)} %get-tuple-element.47), channel_id=1, source_target_pairs={{0,96},{32,0},{64,32},{96,64},{1,97},{33,1},{65,33},{97,65},{2,98}... | collective-permute-start | bytes 786440 | tf_op jit(solution)/shard_map/ppermute | solution.py:232
  147.8 3.2 %collective-permute-start.14 = (bf16[16,16,512]{2,1,0:T(8,128)(2,1)S(1)}, bf16[16,16,512]{2,1,0:T(8,128)(2,1)S(1)}, u32[]{:S(2)}, u32[]{:S(2)}) collective-permute-start(bf16[16,16,512]{2,1,0:T(8,128)(2,1)S(1)} %add_convert_fusion.2), channel_id=1, source_target_pairs={{0,96},{32,0},{64,32},{96,64},{1,97},{33,1},{65,33},{97,65},{2,98}... | collective-permute-start | bytes 786440 | tf_op jit(solution)/shard_map/ppermute | solution.py:232
  151.2 2.2 collective-permute-done.12
  153.4 5.2 %collective-permute-done.14 = bf16[16,16,512]{2,1,0:T(8,128)(2,1)S(1)} collective-permute-done((bf16[16,16,512]{2,1,0:T(8,128)(2,1)S(1)}, bf16[16,16,512]{2,1,0:T(8,128)(2,1)S(1)}, u32[]{:S(2)}, u32[]{:S(2)}) %collective-permute-start.14) | collective-permute-done | bytes 262176 | tf_op jit(solution)/shard_map/ppermute | solution.py:232
  161.4 5.3 %all-to-all-start.4 = ((bf16[32,32,512]{2,1,0:T(8,128)(2,1)}), bf16[32,32,512]{2,1,0:T(8,128)(2,1)S(1)}, u32[]{:S(2)}, u32[]{:S(2)}) async-start(bf16[32,32,512]{2,1,0:T(8,128)(2,1)} %copy.30), calls=%async_computation.4 | async-start | bytes 2097152 | tf_op jit(solution)/shard_map/all_to_all | solution.py:293
  166.8 17.1 %all-to-all-done.4 = bf16[32,32,512]{2,1,0:T(8,128)(2,1)S(1)} async-done(((bf16[32,32,512]{2,1,0:T(8,128)(2,1)}), bf16[32,32,512]{2,1,0:T(8,128)(2,1)S(1)}, u32[]{:S(2)}, u32[]{:S(2)}) %all-to-all-start.4) | async-done | bytes 1048608 | tf_op jit(solution)/shard_map/all_to_all | solution.py:293
  183.9 3.7 %place_rows.1 = bf16[2048,512]{1,0:T(8,128)(2,1)} custom-call(s32[1,1024]{1,0:T(1,128)S(1)} %add.63.ids_ref, bf16[1024,512]{1,0:T(8,128)(2,1)S(1)} %bitcast.15), custom_call_target="tpu_custom_call" | custom-call | tf_op jit(solution)/shard_map/place_rows/pallas_call | solution.py:216
  187.6 5.6 %all-to-all-start.5 = ((bf16[128,16,512]{2,1,0:T(8,128)(2,1)}), bf16[128,16,512]{2,1,0:T(8,128)(2,1)S(1)}, u32[]{:S(2)}, u32[]{:S(2)}) async-start(bf16[128,16,512]{2,1,0:T(8,128)(2,1)} %bitcast.8), calls=%async_computation.5 | async-start | bytes 4194304 | tf_op jit(solution)/shard_map/all_to_all | solution.py:295
  195.2 28.4 %all-to-all-done.5 = bf16[128,16,512]{2,1,0:T(8,128)(2,1)S(1)} async-done(((bf16[128,16,512]{2,1,0:T(8,128)(2,1)}), bf16[128,16,512]{2,1,0:T(8,128)(2,1)S(1)}, u32[]{:S(2)}, u32[]{:S(2)}) %all-to-all-start.5) | async-done | bytes 2097184 | tf_op jit(solution)/shard_map/all_to_all | solution.py:295
  223.6 2.5 %copy.31 = bf16[16,128,512]{2,1,0:T(8,128)(2,1)} copy(bf16[16,128,512]{2,0,1:T(8,128)(2,1)S(1)} %bitcast.24) | data formatting | bytes 4194304
  (67 shorter events, 30.0 us)
Async XLA Ops:
  1.5 1.6 copy-start
  53.5 16.3 %all-to-all-start.1 = ((bf16[32,16,512]{2,1,0:T(8,128)(2,1)}), bf16[32,16,512]{2,1,0:T(8,128)(2,1)S(1)}, u32[]{:S(2)}, u32[]{:S(2)}) async-start(bf16[32,16,512]{2,1,0:T(8,128)(2,1)} %bitcast.2), calls=%async_computation.1 | async-start | bytes 1048576 | tf_op jit(solution)/shard_map/all_to_all | solution.py:280
  70.1 23.5 %collective-permute-start.3 = (bf16[16,32,512]{2,1,0:T(8,128)(2,1)S(1)}, bf16[16,32,512]{2,1,0:T(8,128)(2,1)S(1)}, u32[]{:S(2)}, u32[]{:S(2)}) collective-permute-start(bf16[16,32,512]{2,1,0:T(8,128)(2,1)S(1)} %bitcast.20), channel_id=1, source_target_pairs={{0,64},{32,96},{64,0},{96,32},{1,65},{33,97},{65,1},{97,33},{2,66}... | collective-permute-start | bytes 1572872 | tf_op jit(solution)/shard_map/ppermute | solution.py:232
  71.3 25.5 %collective-permute-start.4 = (bf16[16,32,512]{2,1,0:T(8,128)(2,1)S(1)}, bf16[16,32,512]{2,1,0:T(8,128)(2,1)S(1)}, u32[]{:S(2)}, u32[]{:S(2)}) collective-permute-start(bf16[16,32,512]{2,1,0:T(8,128)(2,1)S(1)} %bitcast.21), channel_id=1, source_target_pairs={{0,32},{32,64},{64,96},{96,0},{1,33},{33,65},{65,97},{97,1},{2,34}... | collective-permute-start | bytes 1572872 | tf_op jit(solution)/shard_map/ppermute | solution.py:232
  71.6 25.9 %collective-permute-start.5 = (bf16[16,32,512]{2,1,0:T(8,128)(2,1)S(1)}, bf16[16,32,512]{2,1,0:T(8,128)(2,1)S(1)}, u32[]{:S(2)}, u32[]{:S(2)}) collective-permute-start(bf16[16,32,512]{2,1,0:T(8,128)(2,1)S(1)} %bitcast.22), channel_id=1, source_target_pairs={{0,96},{32,0},{64,32},{96,64},{1,97},{33,1},{65,33},{97,65},{2,98}... | collective-permute-start | bytes 1572872 | tf_op jit(solution)/shard_map/ppermute | solution.py:232
  73.9 17.2 %all-to-all-start.2 = ((bf16[32,16,512]{2,1,0:T(8,128)(2,1)}), bf16[32,16,512]{2,1,0:T(8,128)(2,1)}, u32[]{:S(2)}, u32[]{:S(2)}) async-start(bf16[32,16,512]{2,1,0:T(8,128)(2,1)} %bitcast.1), calls=%async_computation.2 | async-start | bytes 1048576 | tf_op jit(solution)/shard_map/all_to_all | solution.py:280
  91.1 28.1 %copy-start.3 = (bf16[16,64,512]{2,1,0:T(8,128)(2,1)S(1)}, bf16[16,64,512]{2,1,0:T(8,128)(2,1)}, u32[]{:S(2)}) copy-start(bf16[16,64,512]{2,1,0:T(8,128)(2,1)} %refs_5_.3) | copy-start | bytes 3145732
  92.6 24.7 %collective-permute-start = (bf16[16,32,512]{2,1,0:T(8,128)(2,1)S(1)}, bf16[16,32,512]{2,1,0:T(8,128)(2,1)S(1)}, u32[]{:S(2)}, u32[]{:S(2)}) collective-permute-start(bf16[16,32,512]{2,1,0:T(8,128)(2,1)S(1)} %bitcast.16), channel_id=1, source_target_pairs={{0,64},{32,96},{64,0},{96,32},{1,65},{33,97},{65,1},{97,33},{2,66}... | collective-permute-start | bytes 1572872 | tf_op jit(solution)/shard_map/ppermute | solution.py:232
  93.3 26.0 %collective-permute-start.1 = (bf16[16,32,512]{2,1,0:T(8,128)(2,1)S(1)}, bf16[16,32,512]{2,1,0:T(8,128)(2,1)S(1)}, u32[]{:S(2)}, u32[]{:S(2)}) collective-permute-start(bf16[16,32,512]{2,1,0:T(8,128)(2,1)S(1)} %bitcast.17), channel_id=1, source_target_pairs={{0,32},{32,64},{64,96},{96,0},{1,33},{33,65},{65,97},{97,1},{2,34}... | collective-permute-start | bytes 1572872 | tf_op jit(solution)/shard_map/ppermute | solution.py:232
  93.5 25.7 %collective-permute-start.2 = (bf16[16,32,512]{2,1,0:T(8,128)(2,1)S(1)}, bf16[16,32,512]{2,1,0:T(8,128)(2,1)S(1)}, u32[]{:S(2)}, u32[]{:S(2)}) collective-permute-start(bf16[16,32,512]{2,1,0:T(8,128)(2,1)S(1)} %bitcast.18), channel_id=1, source_target_pairs={{0,96},{32,0},{64,32},{96,64},{1,97},{33,1},{65,33},{97,65},{2,98}... | collective-permute-start | bytes 1572872 | tf_op jit(solution)/shard_map/ppermute | solution.py:232
  98.3 1.2 copy-start.1
  115.6 26.4 %collective-permute-start.10 = (bf16[16,32,512]{2,1,0:T(8,128)(2,1)}, bf16[16,32,512]{2,1,0:T(8,128)(2,1)}, u32[]{:S(2)}, u32[]{:S(2)}) collective-permute-start(bf16[16,32,512]{2,1,0:T(8,128)(2,1)} %get-tuple-element.41), channel_id=1, source_target_pairs={{0,32},{32,64},{64,96},{96,0},{1,33},{33,65},{65,97},{97,1},{2,34}... | collective-permute-start | bytes 1572872 | tf_op jit(solution)/shard_map/ppermute | solution.py:232
  115.9 26.3 %collective-permute-start.8 = (bf16[16,32,512]{2,1,0:T(8,128)(2,1)}, bf16[16,32,512]{2,1,0:T(8,128)(2,1)}, u32[]{:S(2)}, u32[]{:S(2)}) collective-permute-start(bf16[16,32,512]{2,1,0:T(8,128)(2,1)} %get-tuple-element.39), channel_id=1, source_target_pairs={{0,64},{32,96},{64,0},{96,32},{1,65},{33,97},{65,1},{97,33},{2,66}... | collective-permute-start | bytes 1572872 | tf_op jit(solution)/shard_map/ppermute | solution.py:232
  117.2 27.5 %collective-permute-start.9 = (bf16[16,32,512]{2,1,0:T(8,128)(2,1)S(1)}, bf16[16,32,512]{2,1,0:T(8,128)(2,1)}, u32[]{:S(2)}, u32[]{:S(2)}) collective-permute-start(bf16[16,32,512]{2,1,0:T(8,128)(2,1)S(1)} %get-tuple-element.40), channel_id=1, source_target_pairs={{0,96},{32,0},{64,32},{96,64},{1,97},{33,1},{65,33},{97,65},{2,98}... | collective-permute-start | bytes 1572872 | tf_op jit(solution)/shard_map/ppermute | solution.py:232
  133.2 8.9 %copy-start.9 = (bf16[16,16,512]{2,1,0:T(8,128)(2,1)S(1)}, bf16[16,16,512]{2,1,0:T(8,128)(2,1)}, u32[]{:S(2)}) copy-start(bf16[16,16,512]{2,1,0:T(8,128)(2,1)} %copy-done.8) | copy-start | bytes 786436
  133.2 14.6 %collective-permute-start.6 = (bf16[16,16,512]{2,1,0:T(8,128)(2,1)}, bf16[16,16,512]{2,1,0:T(8,128)(2,1)S(1)}, u32[]{:S(2)}, u32[]{:S(2)}) collective-permute-start(bf16[16,16,512]{2,1,0:T(8,128)(2,1)} %get-tuple-element.36), channel_id=1, source_target_pairs={{0,32},{32,64},{64,96},{96,0},{1,33},{33,65},{65,97},{97,1},{2,34}... | collective-permute-start | bytes 786440 | tf_op jit(solution)/shard_map/ppermute | solution.py:232
  133.4 14.4 %collective-permute-start.7 = (bf16[16,16,512]{2,1,0:T(8,128)(2,1)}, bf16[16,16,512]{2,1,0:T(8,128)(2,1)S(1)}, u32[]{:S(2)}, u32[]{:S(2)}) collective-permute-start(bf16[16,16,512]{2,1,0:T(8,128)(2,1)} %get-tuple-element.37), channel_id=1, source_target_pairs={{0,96},{32,0},{64,32},{96,64},{1,97},{33,1},{65,33},{97,65},{2,98}... | collective-permute-start | bytes 786440 | tf_op jit(solution)/shard_map/ppermute | solution.py:232
  135.8 23.9 %all-to-all-start.3 = ((bf16[32,16,1024]{2,1,0:T(8,128)(2,1)}), bf16[32,16,1024]{2,1,0:T(8,128)(2,1)}, u32[]{:S(2)}, u32[]{:S(2)}) async-start(bf16[32,16,1024]{2,1,0:T(8,128)(2,1)} %bitcast.6), calls=%async_computation.3 | async-start | bytes 2097152 | tf_op jit(solution)/shard_map/all_to_all | solution.py:290
  142.0 11.3 %collective-permute-start.12 = (bf16[16,16,512]{2,1,0:T(8,128)(2,1)S(1)}, bf16[16,16,512]{2,1,0:T(8,128)(2,1)S(1)}, u32[]{:S(2)}, u32[]{:S(2)}) collective-permute-start(bf16[16,16,512]{2,1,0:T(8,128)(2,1)S(1)} %copy-done.9), channel_id=1, source_target_pairs={{0,32},{32,64},{64,96},{96,0},{1,33},{33,65},{65,97},{97,1},{2,34}... | collective-permute-start | bytes 786440 | tf_op jit(solution)/shard_map/ppermute | solution.py:232
  142.1 11.2 %collective-permute-start.13 = (bf16[16,16,512]{2,1,0:T(8,128)(2,1)S(1)}, bf16[16,16,512]{2,1,0:T(8,128)(2,1)S(1)}, u32[]{:S(2)}, u32[]{:S(2)}) collective-permute-start(bf16[16,16,512]{2,1,0:T(8,128)(2,1)S(1)} %get-tuple-element.47), channel_id=1, source_target_pairs={{0,96},{32,0},{64,32},{96,64},{1,97},{33,1},{65,33},{97,65},{2,98}... | collective-permute-start | bytes 786440 | tf_op jit(solution)/shard_map/ppermute | solution.py:232
  147.8 10.7 %collective-permute-start.14 = (bf16[16,16,512]{2,1,0:T(8,128)(2,1)S(1)}, bf16[16,16,512]{2,1,0:T(8,128)(2,1)S(1)}, u32[]{:S(2)}, u32[]{:S(2)}) collective-permute-start(bf16[16,16,512]{2,1,0:T(8,128)(2,1)S(1)} %add_convert_fusion.2), channel_id=1, source_target_pairs={{0,96},{32,0},{64,32},{96,64},{1,97},{33,1},{65,33},{97,65},{2,98}... | collective-permute-start | bytes 786440 | tf_op jit(solution)/shard_map/ppermute | solution.py:232
  151.1 8.4 %collective-permute-start.11 = (bf16[16,16,512]{2,1,0:T(8,128)(2,1)S(1)}, bf16[16,16,512]{2,1,0:T(8,128)(2,1)S(1)}, u32[]{:S(2)}, u32[]{:S(2)}) collective-permute-start(bf16[16,16,512]{2,1,0:T(8,128)(2,1)S(1)} %add_convert_fusion.3), channel_id=1, source_target_pairs={{0,32},{32,64},{64,96},{96,0},{1,33},{33,65},{65,97},{97,1},{2,34}... | collective-permute-start | bytes 786440 | tf_op jit(solution)/shard_map/ppermute | solution.py:232
  161.4 22.5 %all-to-all-start.4 = ((bf16[32,32,512]{2,1,0:T(8,128)(2,1)}), bf16[32,32,512]{2,1,0:T(8,128)(2,1)S(1)}, u32[]{:S(2)}, u32[]{:S(2)}) async-start(bf16[32,32,512]{2,1,0:T(8,128)(2,1)} %copy.30), calls=%async_computation.4 | async-start | bytes 2097152 | tf_op jit(solution)/shard_map/all_to_all | solution.py:293
  187.6 36.0 %all-to-all-start.5 = ((bf16[128,16,512]{2,1,0:T(8,128)(2,1)}), bf16[128,16,512]{2,1,0:T(8,128)(2,1)S(1)}, u32[]{:S(2)}, u32[]{:S(2)}) async-start(bf16[128,16,512]{2,1,0:T(8,128)(2,1)} %bitcast.8), calls=%async_computation.5 | async-start | bytes 4194304 | tf_op jit(solution)/shard_map/all_to_all | solution.py:295
  (6 other events, 5.6 us)

commit v5 on v4

--- a/solution.py
+++ b/solution.py
@@ -12,10 +12,11 @@
 EPSILON = 1e-06
 BOTH = ("enc", "dp")
 CHUNKS = (8, 8)
-PER_STEP = 2
+PER_STEP = 4
 PIECES = 4
 LANES = 128
 EXTRA = 8
+SPREAD_TILE = 16
 FAR_FIRST = (2, 1, -1)
 F32 = jnp.float32
 BF16 = jnp.bfloat16
@@ -70,17 +71,26 @@
     key_bfs = each(lambda u: u.astype(BF16), key_units)
     values_all = mm(x, w_ref[:, cols:]).astype(BF16)
     values = [values_all[spans[s], at] for s, at in both]
-    raised = each(lambda q, k: jnp.exp(mm(q, k, COLS) * inverse), query_bfs, key_bfs)
-    d_probs = each(lambda g, v: mm(g, v, COLS), grads, values)
+    blank = jnp.zeros((span, D_HEAD), BF16)
+    rows_of = lambda top, bottom: jnp.concatenate([top, bottom], axis=0)
+    cols_of = lambda left, right: jnp.concatenate([left, right], axis=1)
+    outer = each(lambda q, g: rows_of(cols_of(q, blank), cols_of(blank, g)), query_bfs, grads)
+    inner = each(cols_of, key_bfs, values)
+    products = each(lambda o, i: mm(o, i, COLS), outer, inner)
+    raised = each(lambda p: jnp.exp(p[:span] * inverse), products)
+    d_probs = each(lambda p: p[span:], products)
     weights = each(lambda e: e * (1.0 / jnp.sum(e, axis=-1, keepdims=True)), raised)
     probs = each(lambda p: p.astype(BF16), weights)
-    attended = each(lambda p, v: mm(p, v).astype(BF16), probs, values)
-    d_values = each(lambda p, g: mm(p, g, ROWS).astype(BF16), probs, grads)
     d_scores = each(
         lambda p, d: (p * (d - jnp.sum(d * p, axis=-1, keepdims=True)) * inverse).astype(BF16), weights, d_probs
     )
-    d_query_units = each(lambda d, k: mm(d, k), d_scores, key_bfs)
-    d_key_units = each(lambda d, q: mm(d, q, ROWS), d_scores, query_bfs)
+    middle = each(rows_of, d_scores, probs)
+    to_queries = each(mm, middle, inner)
+    to_keys = each(lambda m, o: mm(m, o, ROWS), middle, outer)
+    d_query_units = each(lambda t: t[:span, :D_HEAD], to_queries)
+    attended = each(lambda t: t[span:, D_HEAD:].astype(BF16), to_queries)
+    d_key_units = each(lambda t: t[:, :D_HEAD], to_keys)
+    d_values = each(lambda t: t[:, D_HEAD:].astype(BF16), to_keys)
     d_queries = each(
         lambda c, d, u: (c * (d - u * mean(d * u))).astype(BF16), query_scales, d_query_units, query_units
     )
@@ -150,25 +160,26 @@
 
 def spread_kernel(x_ref, ids_ref, out_ref):
     held, rows, width = x_ref.shape
-    count = held * rows
+    count = held * SPREAD_TILE
     at = lax.broadcasted_iota(jnp.int32, (count, count), 0)
-    source = lax.rem(at, held) * rows + at // held
+    source = lax.rem(at, held) * SPREAD_TILE + at // held
     turn = (source == lax.broadcasted_iota(jnp.int32, (count, count), 1)).astype(BF16)
-    turned = mm(turn, x_ref[...].reshape(count, width)).astype(BF16).reshape(rows, held, width)
     blocks = width // LANES
-    for i in range(blocks):
-        out_ref[:, i * held : (i + 1) * held] = turned[:, :, i * LANES : (i + 1) * LANES]
     out_ref[:, blocks * held :] = jnp.broadcast_to(ids_ref[...], (rows, EXTRA, LANES))
-
-
-def spread_rows(x, ids, tile=16):
+    for r in range(0, rows, SPREAD_TILE):
+        turned = mm(turn, x_ref[:, r : r + SPREAD_TILE].reshape(count, width)).astype(BF16)
+        turned = turned.reshape(SPREAD_TILE, held, width)
+        for i in range(blocks):
+            out_ref[r : r + SPREAD_TILE, i * held : (i + 1) * held] = turned[:, :, i * LANES : (i + 1) * LANES]
+
+
+def spread_rows(x, ids):
     held, rows, width = x.shape
     lines = width // LANES * held + EXTRA
     return pl.pallas_call(
         spread_kernel,
-        grid=(rows // tile,),
-        in_specs=[pl.BlockSpec((held, tile, width), lambda i: (0, i, 0)), pl.BlockSpec(ids.shape, lambda i: (0, 0))],
-        out_specs=pl.BlockSpec((tile, lines, LANES), lambda i: (i, 0, 0)),
+        in_specs=[pl.BlockSpec(memory_space=pltpu.VMEM)] * 2,
+        out_specs=pl.BlockSpec(memory_space=pltpu.VMEM),
         out_shape=jax.ShapeDtypeStruct((rows, lines, LANES), BF16),
         compiler_params=pltpu.CompilerParams(vmem_limit_bytes=32 * 1024 * 1024),
         name="spread_rows",
@@ -186,22 +197,17 @@
         out_ref[:, i * lanes : (i + 2) * lanes] = picked.astype(BF16)
 
 
-def pick_rows(ids, table, held, tile=256):
+def pick_rows(ids, table, held):
     senders, lines, lanes = table.shape
     width = (lines - EXTRA) // held * lanes
-    wanted = ids.shape[0]
     return pl.pallas_call(
         functools.partial(pick_kernel, held),
-        grid=(wanted // tile,),
-        in_specs=[
-            pl.BlockSpec((tile, 1), lambda i: (i, 0)),
-            pl.BlockSpec(table.shape, lambda i: (0, 0, 0)),
-        ],
-        out_specs=pl.BlockSpec((tile, width), lambda i: (i, 0)),
-        out_shape=jax.ShapeDtypeStruct((wanted, width), BF16),
-        compiler_params=pltpu.CompilerParams(vmem_limit_bytes=48 * 1024 * 1024),
+        in_specs=[pl.BlockSpec(memory_space=pltpu.VMEM)] * 2,
+        out_specs=pl.BlockSpec(memory_space=pltpu.VMEM),
+        out_shape=jax.ShapeDtypeStruct((ids.shape[0], width), BF16),
+        compiler_params=pltpu.CompilerParams(vmem_limit_bytes=32 * 1024 * 1024),
         name="pick_rows",
-    )(ids.reshape(wanted, 1), table)
+    )(ids.reshape(-1, 1), table)
 
 
 def place_kernel(ids_ref, rows_ref, out_ref):

time: 227 us -> 224 us (0.987)
  waiting for transfers between devices: 74.6 us -> 78.6 us
  Pallas kernels: 36.3 us -> 32.4 us
  starting transfers between devices: 46.6 us -> 43 us
    ppermute x15, waiting for transfers between devices: 10.4 us -> 14.1 us  [shift(): lax.ppermute(value, 'enc', [(i, (i + by) % count) for i in range(count)])]
  transfers between devices with their start and end apart: 20 -> 20, of which waited for: 10 -> 11; matrix products, arithmetic and copies ran while one was open for 4% -> 4% of each run, Pallas kernels for 12% -> 12%
where the time goes in v5:
time: 224 us; the launch traced here: 223 us
  waiting for transfers between devices  78.6 us (35%)
  blocking collectives  44.6 us (20%)
  starting transfers between devices  43 us (19%)
  Pallas kernels  32.4 us (14%)
  local copies, waits for them, and re-layouts  18.8 us (8%)
  other arithmetic  4.32 us (2%)
    all_to_all x1, blocking collectives, body(): table = lax.all_to_all(by_row, BOTH, 0, 0, tiled=True)  44.6 us
    all_to_all x1, waiting for transfers between devices, body(): lax.all_to_all(placed, BOTH, 0, 0, tiled=True)  28.4 us
    pallas_call x2, Pallas kernels, attention(): pl.pallas_call(functools.partial(attention_kernel, first, last), grid=(st...  23.7 us
    all_to_all x2, waiting for transfers between devices, body(): own = jnp.swapaxes(lax.all_to_all(sent[c], 'dp', 0, 0, tiled=True), 0, 1)  18.9 us
    ppermute x15, starting transfers between devices, shift(): lax.ppermute(value, 'enc', [(i, (i + by) % count) for i in range(count)])  17.7 us
    all_to_all x1, waiting for transfers between devices, body(): lax.all_to_all(summed, 'dp', 0, 0, tiled=True)  17.2 us
    ppermute x15, waiting for transfers between devices, shift(): lax.ppermute(value, 'enc', [(i, (i + by) % count) for i in range(count)])  14.1 us
    unnamed x23, local copies, waits for them, and re-layouts  12.8 us
  transfers between devices with their start and end apart: 20, of which 11 were waited for; matrix products, arithmetic and copies ran while one was open for 4% of the time, Pallas kernels for 12%

profile of v5, /device:TPU:1, one launch (start us, length us, event | category | flops | bytes accessed | tf_op | source)
XLA Modules:
  0.0 222.6 jit_solution(18407052219858626924)
XLA Ops:
  3.8 44.6 %all_to_all.30.table_ref = bf16[128,72,128]{2,1,0:T(8,128)(2,1)S(1)} all-to-all(bf16[128,72,128]{2,1,0:T(8,128)(2,1)S(1)} %spread_rows.1), channel_id=1, replica_groups=mesh['enc'=4,'dp'=32] {'enc','dp'}, dimensions={0} | all-to-all | bytes 4718592 | tf_op jit(solution)/shard_map/all_to_all | solution.py:272
  49.9 2.1 pick_rows.3
  52.0 4.6 %all-to-all-start.1 = ((bf16[32,16,512]{2,1,0:T(8,128)(2,1)}), bf16[32,16,512]{2,1,0:T(8,128)(2,1)S(1)}, u32[]{:S(2)}, u32[]{:S(2)}) async-start(bf16[32,16,512]{2,1,0:T(8,128)(2,1)} %bitcast.2), calls=%async_computation.1 | async-start | bytes 1048576 | tf_op jit(solution)/shard_map/all_to_all | solution.py:286
  56.8 2.1 pick_rows.2
  58.8 9.4 %all-to-all-done.1 = bf16[32,16,512]{2,1,0:T(8,128)(2,1)S(1)} async-done(((bf16[32,16,512]{2,1,0:T(8,128)(2,1)}), bf16[32,16,512]{2,1,0:T(8,128)(2,1)S(1)}, u32[]{:S(2)}, u32[]{:S(2)}) %all-to-all-start.1) | async-done | bytes 524320 | tf_op jit(solution)/shard_map/all_to_all | solution.py:286
  70.1 2.4 %collective-permute-start.5 = (bf16[16,32,512]{2,1,0:T(8,128)(2,1)S(1)}, bf16[16,32,512]{2,1,0:T(8,128)(2,1)S(1)}, u32[]{:S(2)}, u32[]{:S(2)}) collective-permute-start(bf16[16,32,512]{2,1,0:T(8,128)(2,1)S(1)} %bitcast.22), channel_id=1, source_target_pairs={{0,96},{32,0},{64,32},{96,64},{1,97},{33,1},{65,33},{97,65},{2,98}... | collective-permute-start | bytes 1572872 | tf_op jit(solution)/shard_map/ppermute | solution.py:238
  72.4 5.5 %all-to-all-start.2 = ((bf16[32,16,512]{2,1,0:T(8,128)(2,1)}), bf16[32,16,512]{2,1,0:T(8,128)(2,1)}, u32[]{:S(2)}, u32[]{:S(2)}) async-start(bf16[32,16,512]{2,1,0:T(8,128)(2,1)} %bitcast.1), calls=%async_computation.2 | async-start | bytes 1048576 | tf_op jit(solution)/shard_map/all_to_all | solution.py:286
  80.2 9.5 %all-to-all-done.2 = bf16[32,16,512]{2,1,0:T(8,128)(2,1)} async-done(((bf16[32,16,512]{2,1,0:T(8,128)(2,1)}), bf16[32,16,512]{2,1,0:T(8,128)(2,1)}, u32[]{:S(2)}, u32[]{:S(2)}) %all-to-all-start.2) | async-done | bytes 524320 | tf_op jit(solution)/shard_map/all_to_all | solution.py:286
  92.0 2.4 %collective-permute-start.2 = (bf16[16,32,512]{2,1,0:T(8,128)(2,1)S(1)}, bf16[16,32,512]{2,1,0:T(8,128)(2,1)S(1)}, u32[]{:S(2)}, u32[]{:S(2)}) collective-permute-start(bf16[16,32,512]{2,1,0:T(8,128)(2,1)S(1)} %bitcast.18), channel_id=1, source_target_pairs={{0,96},{32,0},{64,32},{96,64},{1,97},{33,1},{65,33},{97,65},{2,98}... | collective-permute-start | bytes 1572872 | tf_op jit(solution)/shard_map/ppermute | solution.py:238
  101.3 11.7 %attention.2 = (bf16[16,64,512]{2,1,0:T(8,128)(2,1)}, bf16[16,64,512]{2,1,0:T(8,128)(2,1)}, bf16[16,32,512]{2,1,0:T(8,128)(2,1)S(1)}, bf16[16,32,512]{2,1,0:T(8,...) custom-call(bf16[16,32,512]{2,1,0:T(8,128)(2,1)S(1)} %bitcast.23, ...), custom_call_target="tpu_custom_call" | custom-call | flops 7200000000 | bytes 6400000 | tf_op jit(solution)/shard_map/attention/pallas_call | solution.py:140
  114.7 1.9 collective-permute-start.9
  117.7 12.0 %attention.3 = (bf16[16,64,512]{2,1,0:T(8,128)(2,1)}, bf16[16,64,512]{2,1,0:T(8,128)(2,1)}, bf16[16,32,512]{2,1,0:T(8,128)(2,1)S(1)}, bf16[16,16,512]{2,1,0:T(8,...) custom-call(bf16[16,32,512]{2,1,0:T(8,128)(2,1)S(1)} %bitcast.19, ...), custom_call_target="tpu_custom_call", output_to_operand_aliasing={{0}: (8, {}), {1}: (9, {})} | custom-call | flops 7200000000 | bytes 6400000 | tf_op jit(solution)/shard_map/attention/pallas_call | solution.py:140
  130.8 2.4 %collective-permute-start.7 = (bf16[16,16,512]{2,1,0:T(8,128)(2,1)}, bf16[16,16,512]{2,1,0:T(8,128)(2,1)S(1)}, u32[]{:S(2)}, u32[]{:S(2)}) collective-permute-start(bf16[16,16,512]{2,1,0:T(8,128)(2,1)} %get-tuple-element.37), channel_id=1, source_target_pairs={{0,96},{32,0},{64,32},{96,64},{1,97},{33,1},{65,33},{97,65},{2,98}... | collective-permute-start | bytes 786440 | tf_op jit(solution)/shard_map/ppermute | solution.py:238
  133.2 5.4 %all-to-all-start.3 = ((bf16[32,16,1024]{2,1,0:T(8,128)(2,1)}), bf16[32,16,1024]{2,1,0:T(8,128)(2,1)}, u32[]{:S(2)}, u32[]{:S(2)}) async-start(bf16[32,16,1024]{2,1,0:T(8,128)(2,1)} %bitcast.6), calls=%async_computation.3 | async-start | bytes 2097152 | tf_op jit(solution)/shard_map/all_to_all | solution.py:296
  143.0 2.9 %collective-permute-done.6 = bf16[16,16,512]{2,1,0:T(8,128)(2,1)S(1)} collective-permute-done((bf16[16,16,512]{2,1,0:T(8,128)(2,1)}, bf16[16,16,512]{2,1,0:T(8,128)(2,1)S(1)}, u32[]{:S(2)}, u32[]{:S(2)}) %collective-permute-start.6) | collective-permute-done | bytes 262176 | tf_op jit(solution)/shard_map/ppermute | solution.py:238
  146.1 2.4 %collective-permute-start.14 = (bf16[16,16,512]{2,1,0:T(8,128)(2,1)S(1)}, bf16[16,16,512]{2,1,0:T(8,128)(2,1)S(1)}, u32[]{:S(2)}, u32[]{:S(2)}) collective-permute-start(bf16[16,16,512]{2,1,0:T(8,128)(2,1)S(1)} %add_convert_fusion.2), channel_id=1, source_target_pairs={{0,96},{32,0},{64,32},{96,64},{1,97},{33,1},{65,33},{97,65},{2,98}... | collective-permute-start | bytes 786440 | tf_op jit(solution)/shard_map/ppermute | solution.py:238
  148.6 3.0 %collective-permute-done.12 = bf16[16,16,512]{2,1,0:T(8,128)(2,1)S(1)} collective-permute-done((bf16[16,16,512]{2,1,0:T(8,128)(2,1)S(1)}, bf16[16,16,512]{2,1,0:T(8,128)(2,1)S(1)}, u32[]{:S(2)}, u32[]{:S(2)}) %collective-permute-start.12) | collective-permute-done | bytes 262176 | tf_op jit(solution)/shard_map/ppermute | solution.py:238
  151.6 4.4 %collective-permute-done.14 = bf16[16,16,512]{2,1,0:T(8,128)(2,1)S(1)} collective-permute-done((bf16[16,16,512]{2,1,0:T(8,128)(2,1)S(1)}, bf16[16,16,512]{2,1,0:T(8,128)(2,1)S(1)}, u32[]{:S(2)}, u32[]{:S(2)}) %collective-permute-start.14) | collective-permute-done | bytes 262176 | tf_op jit(solution)/shard_map/ppermute | solution.py:238
  158.8 5.2 %all-to-all-start.4 = ((bf16[32,32,512]{2,1,0:T(8,128)(2,1)}), bf16[32,32,512]{2,1,0:T(8,128)(2,1)S(1)}, u32[]{:S(2)}, u32[]{:S(2)}) async-start(bf16[32,32,512]{2,1,0:T(8,128)(2,1)} %copy.30), calls=%async_computation.4 | async-start | bytes 2097152 | tf_op jit(solution)/shard_map/all_to_all | solution.py:299
  164.1 17.2 %all-to-all-done.4 = bf16[32,32,512]{2,1,0:T(8,128)(2,1)S(1)} async-done(((bf16[32,32,512]{2,1,0:T(8,128)(2,1)}), bf16[32,32,512]{2,1,0:T(8,128)(2,1)S(1)}, u32[]{:S(2)}, u32[]{:S(2)}) %all-to-all-start.4) | async-done | bytes 1048608 | tf_op jit(solution)/shard_map/all_to_all | solution.py:299
  181.3 3.7 %place_rows.1 = bf16[2048,512]{1,0:T(8,128)(2,1)} custom-call(s32[1,1024]{1,0:T(1,128)S(1)} %add.63.ids_ref, bf16[1024,512]{1,0:T(8,128)(2,1)S(1)} %bitcast.15), custom_call_target="tpu_custom_call" | custom-call | tf_op jit(solution)/shard_map/place_rows/pallas_call | solution.py:222
  185.0 4.7 %all-to-all-start.5 = ((bf16[128,16,512]{2,1,0:T(8,128)(2,1)}), bf16[128,16,512]{2,1,0:T(8,128)(2,1)S(1)}, u32[]{:S(2)}, u32[]{:S(2)}) async-start(bf16[128,16,512]{2,1,0:T(8,128)(2,1)} %bitcast.8), calls=%async_computation.5 | async-start | bytes 4194304 | tf_op jit(solution)/shard_map/all_to_all | solution.py:301
  191.7 28.4 %all-to-all-done.5 = bf16[128,16,512]{2,1,0:T(8,128)(2,1)S(1)} async-done(((bf16[128,16,512]{2,1,0:T(8,128)(2,1)}), bf16[128,16,512]{2,1,0:T(8,128)(2,1)S(1)}, u32[]{:S(2)}, u32[]{:S(2)}) %all-to-all-start.5) | async-done | bytes 2097184 | tf_op jit(solution)/shard_map/all_to_all | solution.py:301
  220.1 2.5 %copy.31 = bf16[16,128,512]{2,1,0:T(8,128)(2,1)} copy(bf16[16,128,512]{2,0,1:T(8,128)(2,1)S(1)} %bitcast.24) | data formatting | bytes 4194304
  (67 shorter events, 31.5 us)
Async XLA Ops:
  1.5 1.6 copy-start
  52.0 16.3 %all-to-all-start.1 = ((bf16[32,16,512]{2,1,0:T(8,128)(2,1)}), bf16[32,16,512]{2,1,0:T(8,128)(2,1)S(1)}, u32[]{:S(2)}, u32[]{:S(2)}) async-start(bf16[32,16,512]{2,1,0:T(8,128)(2,1)} %bitcast.2), calls=%async_computation.1 | async-start | bytes 1048576 | tf_op jit(solution)/shard_map/all_to_all | solution.py:286
  68.6 23.5 %collective-permute-start.3 = (bf16[16,32,512]{2,1,0:T(8,128)(2,1)S(1)}, bf16[16,32,512]{2,1,0:T(8,128)(2,1)S(1)}, u32[]{:S(2)}, u32[]{:S(2)}) collective-permute-start(bf16[16,32,512]{2,1,0:T(8,128)(2,1)S(1)} %bitcast.20), channel_id=1, source_target_pairs={{0,64},{32,96},{64,0},{96,32},{1,65},{33,97},{65,1},{97,33},{2,66}... | collective-permute-start | bytes 1572872 | tf_op jit(solution)/shard_map/ppermute | solution.py:238
  69.8 25.5 %collective-permute-start.4 = (bf16[16,32,512]{2,1,0:T(8,128)(2,1)S(1)}, bf16[16,32,512]{2,1,0:T(8,128)(2,1)S(1)}, u32[]{:S(2)}, u32[]{:S(2)}) collective-permute-start(bf16[16,32,512]{2,1,0:T(8,128)(2,1)S(1)} %bitcast.21), channel_id=1, source_target_pairs={{0,32},{32,64},{64,96},{96,0},{1,33},{33,65},{65,97},{97,1},{2,34}... | collective-permute-start | bytes 1572872 | tf_op jit(solution)/shard_map/ppermute | solution.py:238
  70.1 25.9 %collective-permute-start.5 = (bf16[16,32,512]{2,1,0:T(8,128)(2,1)S(1)}, bf16[16,32,512]{2,1,0:T(8,128)(2,1)S(1)}, u32[]{:S(2)}, u32[]{:S(2)}) collective-permute-start(bf16[16,32,512]{2,1,0:T(8,128)(2,1)S(1)} %bitcast.22), channel_id=1, source_target_pairs={{0,96},{32,0},{64,32},{96,64},{1,97},{33,1},{65,33},{97,65},{2,98}... | collective-permute-start | bytes 1572872 | tf_op jit(solution)/shard_map/ppermute | solution.py:238
  72.4 17.2 %all-to-all-start.2 = ((bf16[32,16,512]{2,1,0:T(8,128)(2,1)}), bf16[32,16,512]{2,1,0:T(8,128)(2,1)}, u32[]{:S(2)}, u32[]{:S(2)}) async-start(bf16[32,16,512]{2,1,0:T(8,128)(2,1)} %bitcast.1), calls=%async_computation.2 | async-start | bytes 1048576 | tf_op jit(solution)/shard_map/all_to_all | solution.py:286
  89.6 28.1 %copy-start.3 = (bf16[16,64,512]{2,1,0:T(8,128)(2,1)S(1)}, bf16[16,64,512]{2,1,0:T(8,128)(2,1)}, u32[]{:S(2)}) copy-start(bf16[16,64,512]{2,1,0:T(8,128)(2,1)} %refs_5_.3) | copy-start | bytes 3145732
  91.1 23.6 %collective-permute-start = (bf16[16,32,512]{2,1,0:T(8,128)(2,1)S(1)}, bf16[16,32,512]{2,1,0:T(8,128)(2,1)S(1)}, u32[]{:S(2)}, u32[]{:S(2)}) collective-permute-start(bf16[16,32,512]{2,1,0:T(8,128)(2,1)S(1)} %bitcast.16), channel_id=1, source_target_pairs={{0,64},{32,96},{64,0},{96,32},{1,65},{33,97},{65,1},{97,33},{2,66}... | collective-permute-start | bytes 1572872 | tf_op jit(solution)/shard_map/ppermute | solution.py:238
  91.8 26.0 %collective-permute-start.1 = (bf16[16,32,512]{2,1,0:T(8,128)(2,1)S(1)}, bf16[16,32,512]{2,1,0:T(8,128)(2,1)S(1)}, u32[]{:S(2)}, u32[]{:S(2)}) collective-permute-start(bf16[16,32,512]{2,1,0:T(8,128)(2,1)S(1)} %bitcast.17), channel_id=1, source_target_pairs={{0,32},{32,64},{64,96},{96,0},{1,33},{33,65},{65,97},{97,1},{2,34}... | collective-permute-start | bytes 1572872 | tf_op jit(solution)/shard_map/ppermute | solution.py:238
  92.0 25.7 %collective-permute-start.2 = (bf16[16,32,512]{2,1,0:T(8,128)(2,1)S(1)}, bf16[16,32,512]{2,1,0:T(8,128)(2,1)S(1)}, u32[]{:S(2)}, u32[]{:S(2)}) collective-permute-start(bf16[16,32,512]{2,1,0:T(8,128)(2,1)S(1)} %bitcast.18), channel_id=1, source_target_pairs={{0,96},{32,0},{64,32},{96,64},{1,97},{33,1},{65,33},{97,65},{2,98}... | collective-permute-start | bytes 1572872 | tf_op jit(solution)/shard_map/ppermute | solution.py:238
  98.0 1.2 copy-start.2
  113.1 25.5 %collective-permute-start.10 = (bf16[16,32,512]{2,1,0:T(8,128)(2,1)}, bf16[16,32,512]{2,1,0:T(8,128)(2,1)}, u32[]{:S(2)}, u32[]{:S(2)}) collective-permute-start(bf16[16,32,512]{2,1,0:T(8,128)(2,1)} %get-tuple-element.41), channel_id=1, source_target_pairs={{0,32},{32,64},{64,96},{96,0},{1,33},{33,65},{65,97},{97,1},{2,34}... | collective-permute-start | bytes 1572872 | tf_op jit(solution)/shard_map/ppermute | solution.py:238
  113.3 26.3 %collective-permute-start.8 = (bf16[16,32,512]{2,1,0:T(8,128)(2,1)}, bf16[16,32,512]{2,1,0:T(8,128)(2,1)}, u32[]{:S(2)}, u32[]{:S(2)}) collective-permute-start(bf16[16,32,512]{2,1,0:T(8,128)(2,1)} %get-tuple-element.39), channel_id=1, source_target_pairs={{0,64},{32,96},{64,0},{96,32},{1,65},{33,97},{65,1},{97,33},{2,66}... | collective-permute-start | bytes 1572872 | tf_op jit(solution)/shard_map/ppermute | solution.py:238
  114.7 26.7 %collective-permute-start.9 = (bf16[16,32,512]{2,1,0:T(8,128)(2,1)S(1)}, bf16[16,32,512]{2,1,0:T(8,128)(2,1)}, u32[]{:S(2)}, u32[]{:S(2)}) collective-permute-start(bf16[16,32,512]{2,1,0:T(8,128)(2,1)S(1)} %get-tuple-element.40), channel_id=1, source_target_pairs={{0,96},{32,0},{64,32},{96,64},{1,97},{33,1},{65,33},{97,65},{2,98}... | collective-permute-start | bytes 1572872 | tf_op jit(solution)/shard_map/ppermute | solution.py:238
  130.5 8.1 %copy-start.9 = (bf16[16,16,512]{2,1,0:T(8,128)(2,1)S(1)}, bf16[16,16,512]{2,1,0:T(8,128)(2,1)}, u32[]{:S(2)}) copy-start(bf16[16,16,512]{2,1,0:T(8,128)(2,1)} %copy-done.8) | copy-start | bytes 786436
  130.5 15.5 %collective-permute-start.6 = (bf16[16,16,512]{2,1,0:T(8,128)(2,1)}, bf16[16,16,512]{2,1,0:T(8,128)(2,1)S(1)}, u32[]{:S(2)}, u32[]{:S(2)}) collective-permute-start(bf16[16,16,512]{2,1,0:T(8,128)(2,1)} %get-tuple-element.36), channel_id=1, source_target_pairs={{0,32},{32,64},{64,96},{96,0},{1,33},{33,65},{65,97},{97,1},{2,34}... | collective-permute-start | bytes 786440 | tf_op jit(solution)/shard_map/ppermute | solution.py:238
  130.8 15.2 %collective-permute-start.7 = (bf16[16,16,512]{2,1,0:T(8,128)(2,1)}, bf16[16,16,512]{2,1,0:T(8,128)(2,1)S(1)}, u32[]{:S(2)}, u32[]{:S(2)}) collective-permute-start(bf16[16,16,512]{2,1,0:T(8,128)(2,1)} %get-tuple-element.37), channel_id=1, source_target_pairs={{0,96},{32,0},{64,32},{96,64},{1,97},{33,1},{65,33},{97,65},{2,98}... | collective-permute-start | bytes 786440 | tf_op jit(solution)/shard_map/ppermute | solution.py:238
  133.2 24.1 %all-to-all-start.3 = ((bf16[32,16,1024]{2,1,0:T(8,128)(2,1)}), bf16[32,16,1024]{2,1,0:T(8,128)(2,1)}, u32[]{:S(2)}, u32[]{:S(2)}) async-start(bf16[32,16,1024]{2,1,0:T(8,128)(2,1)} %bitcast.6), calls=%async_computation.3 | async-start | bytes 2097152 | tf_op jit(solution)/shard_map/all_to_all | solution.py:296
  138.6 13.0 %collective-permute-start.12 = (bf16[16,16,512]{2,1,0:T(8,128)(2,1)S(1)}, bf16[16,16,512]{2,1,0:T(8,128)(2,1)S(1)}, u32[]{:S(2)}, u32[]{:S(2)}) collective-permute-start(bf16[16,16,512]{2,1,0:T(8,128)(2,1)S(1)} %copy-done.9), channel_id=1, source_target_pairs={{0,32},{32,64},{64,96},{96,0},{1,33},{33,65},{65,97},{97,1},{2,34}... | collective-permute-start | bytes 786440 | tf_op jit(solution)/shard_map/ppermute | solution.py:238
  139.6 12.0 %collective-permute-start.13 = (bf16[16,16,512]{2,1,0:T(8,128)(2,1)S(1)}, bf16[16,16,512]{2,1,0:T(8,128)(2,1)S(1)}, u32[]{:S(2)}, u32[]{:S(2)}) collective-permute-start(bf16[16,16,512]{2,1,0:T(8,128)(2,1)S(1)} %get-tuple-element.47), channel_id=1, source_target_pairs={{0,96},{32,0},{64,32},{96,64},{1,97},{33,1},{65,33},{97,65},{2,98}... | collective-permute-start | bytes 786440 | tf_op jit(solution)/shard_map/ppermute | solution.py:238
  146.1 9.9 %collective-permute-start.14 = (bf16[16,16,512]{2,1,0:T(8,128)(2,1)S(1)}, bf16[16,16,512]{2,1,0:T(8,128)(2,1)S(1)}, u32[]{:S(2)}, u32[]{:S(2)}) collective-permute-start(bf16[16,16,512]{2,1,0:T(8,128)(2,1)S(1)} %add_convert_fusion.2), channel_id=1, source_target_pairs={{0,96},{32,0},{64,32},{96,64},{1,97},{33,1},{65,33},{97,65},{2,98}... | collective-permute-start | bytes 786440 | tf_op jit(solution)/shard_map/ppermute | solution.py:238
  148.5 8.4 %collective-permute-start.11 = (bf16[16,16,512]{2,1,0:T(8,128)(2,1)S(1)}, bf16[16,16,512]{2,1,0:T(8,128)(2,1)S(1)}, u32[]{:S(2)}, u32[]{:S(2)}) collective-permute-start(bf16[16,16,512]{2,1,0:T(8,128)(2,1)S(1)} %add_convert_fusion.3), channel_id=1, source_target_pairs={{0,32},{32,64},{64,96},{96,0},{1,33},{33,65},{65,97},{97,1},{2,34}... | collective-permute-start | bytes 786440 | tf_op jit(solution)/shard_map/ppermute | solution.py:238
  158.8 22.5 %all-to-all-start.4 = ((bf16[32,32,512]{2,1,0:T(8,128)(2,1)}), bf16[32,32,512]{2,1,0:T(8,128)(2,1)S(1)}, u32[]{:S(2)}, u32[]{:S(2)}) async-start(bf16[32,32,512]{2,1,0:T(8,128)(2,1)} %copy.30), calls=%async_computation.4 | async-start | bytes 2097152 | tf_op jit(solution)/shard_map/all_to_all | solution.py:299
  185.0 35.1 %all-to-all-start.5 = ((bf16[128,16,512]{2,1,0:T(8,128)(2,1)}), bf16[128,16,512]{2,1,0:T(8,128)(2,1)S(1)}, u32[]{:S(2)}, u32[]{:S(2)}) async-start(bf16[128,16,512]{2,1,0:T(8,128)(2,1)} %bitcast.8), calls=%async_computation.5 | async-start | bytes 4194304 | tf_op jit(solution)/shard_map/all_to_all | solution.py:301
  (6 other events, 5.6 us)

commit v6 on v5

--- a/solution.py
+++ b/solution.py
@@ -17,6 +17,7 @@
 LANES = 128
 EXTRA = 8
 SPREAD_TILE = 16
+PLACE_TILE = 512
 FAR_FIRST = (2, 1, -1)
 F32 = jnp.float32
 BF16 = jnp.bfloat16
@@ -186,6 +187,37 @@
     )(x, ids)
 
 
+def pick_first_kernel(held, shards, first, table_ref, out_ref):
+    senders, lines, lanes = table_ref.shape
+    count, wanted = senders * held, out_ref.shape[0]
+    each = wanted // shards
+    ends = table_ref[:shards, lines - EXTRA :].astype(F32)
+    row = lax.broadcasted_iota(jnp.int32, (wanted, shards), 0)
+    owner = (row // each == lax.broadcasted_iota(jnp.int32, (wanted, shards), 1)).astype(BF16)
+    high, low = (mm(owner, ends[:, i].astype(BF16)) for i in range(2))
+    lane = lax.broadcasted_iota(jnp.int32, (wanted, lanes), 1)
+    mine = lane == lax.rem(lax.broadcasted_iota(jnp.int32, (wanted, lanes), 0), each) + first
+    ids = jnp.sum(jnp.where(mine, high * held + low, 0.0), axis=-1, keepdims=True).astype(jnp.int32)
+    hit = (ids == lax.broadcasted_iota(jnp.int32, (wanted, count), 1)).astype(BF16)
+    blocks = [table_ref[:, at : at + held].reshape(count, lanes) for at in range(0, lines - EXTRA, held)]
+    for i in range(0, len(blocks), 2):
+        picked = mm(hit, jnp.concatenate(blocks[i : i + 2], axis=1))
+        out_ref[:, i * lanes : (i + 2) * lanes] = picked.astype(BF16)
+
+
+def pick_first_rows(table, held, shards, first, each):
+    senders, lines, lanes = table.shape
+    width = (lines - EXTRA) // held * lanes
+    return pl.pallas_call(
+        functools.partial(pick_first_kernel, held, shards, first),
+        in_specs=[pl.BlockSpec(memory_space=pltpu.VMEM)],
+        out_specs=pl.BlockSpec(memory_space=pltpu.VMEM),
+        out_shape=jax.ShapeDtypeStruct((shards * each, width), BF16),
+        compiler_params=pltpu.CompilerParams(vmem_limit_bytes=32 * 1024 * 1024),
+        name="pick_first_rows",
+    )(table)
+
+
 def pick_kernel(held, ids_ref, table_ref, out_ref):
     ids = ids_ref[...]
     senders, lines, lanes = table_ref.shape
@@ -212,25 +244,20 @@
 
 def place_kernel(ids_ref, rows_ref, out_ref):
     ids = ids_ref[...]
-    tile = out_ref.shape[0]
-    row = lax.broadcasted_iota(jnp.int32, (tile, ids.shape[1]), 0) + pl.program_id(0) * tile
-    out_ref[...] = mm((ids == row).astype(BF16), rows_ref[...]).astype(BF16)
-
-
-def place_rows(ids, rows, count, tile=512):
-    given, width = rows.shape
+    for at in range(0, out_ref.shape[0], PLACE_TILE):
+        row = lax.broadcasted_iota(jnp.int32, (PLACE_TILE, ids.shape[1]), 0) + at
+        out_ref[at : at + PLACE_TILE] = mm((ids == row).astype(BF16), rows_ref[...]).astype(BF16)
+
+
+def place_rows(ids, rows, count):
     return pl.pallas_call(
         place_kernel,
-        grid=(count // tile,),
-        in_specs=[
-            pl.BlockSpec((1, given), lambda i: (0, 0)),
-            pl.BlockSpec((given, width), lambda i: (0, 0)),
-        ],
-        out_specs=pl.BlockSpec((tile, width), lambda i: (i, 0)),
-        out_shape=jax.ShapeDtypeStruct((count, width), BF16),
-        compiler_params=pltpu.CompilerParams(vmem_limit_bytes=48 * 1024 * 1024),
+        in_specs=[pl.BlockSpec(memory_space=pltpu.VMEM)] * 2,
+        out_specs=pl.BlockSpec(memory_space=pltpu.VMEM),
+        out_shape=jax.ShapeDtypeStruct((count, rows.shape[1]), BF16),
+        compiler_params=pltpu.CompilerParams(vmem_limit_bytes=32 * 1024 * 1024),
         name="place_rows",
-    )(ids.reshape(1, given), rows)
+    )(ids.reshape(1, -1), rows)
 
 
 def shift(value, by):
@@ -275,8 +302,12 @@
     knb = pair_count // stretches
     sent, start = [], 0
     for size in CHUNKS:
-        wanted = ids[:, start * knb : (start + size) * knb]
-        sent.append(pick_rows(wanted.reshape(-1), table, held).reshape(shards, size * knb, width))
+        if start == 0:
+            sent.append(pick_first_rows(table, held, shards, 0, size * knb))
+        else:
+            wanted = ids[:, start * knb : (start + size) * knb]
+            sent.append(pick_rows(wanted.reshape(-1), table, held))
+        sent[-1] = sent[-1].reshape(shards, size * knb, width)
         start += size
     pieces = []
     for c in range(len(CHUNKS)):

time: 224 us -> 222 us (level)
    pallas_call x1 -> x2, Pallas kernels: 3.73 us -> 5.91 us  [the longest x1 3.66 us: place_rows(): pl.pallas_call(place_kernel, in_specs=[pl.BlockSpec(memory_space=pltpu.VM...]
  transfers between devices with their start and end apart: 20 -> 20, of which waited for: 11 -> 11; matrix products, arithmetic and copies ran while one was open for 4% -> 5% of each run, Pallas kernels for 12% -> 12%
where the time goes in v6:
time: 222 us; the launch traced here: 221 us
  waiting for transfers between devices  77.2 us (35%)
  blocking collectives  44.6 us (20%)
  starting transfers between devices  42.3 us (19%)
  Pallas kernels  32.5 us (15%)
  local copies, waits for them, and re-layouts  18.7 us (8%)
  other arithmetic  5.27 us (2%)
    all_to_all x1, blocking collectives, body(): table = lax.all_to_all(by_row, BOTH, 0, 0, tiled=True)  44.6 us
    all_to_all x1, waiting for transfers between devices, body(): lax.all_to_all(placed, BOTH, 0, 0, tiled=True)  28.5 us
    pallas_call x2, Pallas kernels, attention(): pl.pallas_call(functools.partial(attention_kernel, first, last), grid=(st...  23.8 us
    ppermute x15, starting transfers between devices, shift(): lax.ppermute(value, 'enc', [(i, (i + by) % count) for i in range(count)])  17.7 us
    all_to_all x2, waiting for transfers between devices, body(): own = jnp.swapaxes(lax.all_to_all(sent[c], 'dp', 0, 0, tiled=True), 0, 1)  17.6 us
    all_to_all x1, waiting for transfers between devices, body(): lax.all_to_all(summed, 'dp', 0, 0, tiled=True)  17.2 us
    ppermute x15, waiting for transfers between devices, shift(): lax.ppermute(value, 'enc', [(i, (i + by) % count) for i in range(count)])  14 us
    unnamed x23, local copies, waits for them, and re-layouts  12.7 us
  transfers between devices with their start and end apart: 20, of which 11 were waited for; matrix products, arithmetic and copies ran while one was open for 5% of the time, Pallas kernels for 12%

profile of v6, /device:TPU:1, one launch (start us, length us, event | category | flops | bytes accessed | tf_op | source)
XLA Modules:
  0.0 221.4 jit_solution(12010088606549258764)
XLA Ops:
  3.8 44.6 %all_to_all.30.table_ref = bf16[128,72,128]{2,1,0:T(8,128)(2,1)S(1)} all-to-all(bf16[128,72,128]{2,1,0:T(8,128)(2,1)S(1)} %spread_rows.1), channel_id=1, replica_groups=mesh['enc'=4,'dp'=32] {'enc','dp'}, dimensions={0} | all-to-all | bytes 4718592 | tf_op jit(solution)/shard_map/all_to_all | solution.py:299
  48.4 2.2 %pick_first_rows.1 = bf16[512,512]{1,0:T(8,128)(2,1)} custom-call(bf16[128,72,128]{2,1,0:T(8,128)(2,1)S(1)} %all_to_all.30.table_ref), custom_call_target="tpu_custom_call" | custom-call | tf_op jit(solution)/shard_map/pick_first_rows/pallas_call | solution.py:211
  50.7 4.6 %all-to-all-start.1 = ((bf16[32,16,512]{2,1,0:T(8,128)(2,1)}), bf16[32,16,512]{2,1,0:T(8,128)(2,1)S(1)}, u32[]{:S(2)}, u32[]{:S(2)}) async-start(bf16[32,16,512]{2,1,0:T(8,128)(2,1)} %bitcast.2), calls=%async_computation.1 | async-start | bytes 1048576 | tf_op jit(solution)/shard_map/all_to_all | solution.py:317
  56.8 2.1 pick_rows.1
  58.9 8.1 %all-to-all-done.1 = bf16[32,16,512]{2,1,0:T(8,128)(2,1)S(1)} async-done(((bf16[32,16,512]{2,1,0:T(8,128)(2,1)}), bf16[32,16,512]{2,1,0:T(8,128)(2,1)S(1)}, u32[]{:S(2)}, u32[]{:S(2)}) %all-to-all-start.1) | async-done | bytes 524320 | tf_op jit(solution)/shard_map/all_to_all | solution.py:317
  68.8 2.4 %collective-permute-start.5 = (bf16[16,32,512]{2,1,0:T(8,128)(2,1)S(1)}, bf16[16,32,512]{2,1,0:T(8,128)(2,1)S(1)}, u32[]{:S(2)}, u32[]{:S(2)}) collective-permute-start(bf16[16,32,512]{2,1,0:T(8,128)(2,1)S(1)} %bitcast.22), channel_id=1, source_target_pairs={{0,96},{32,0},{64,32},{96,64},{1,97},{33,1},{65,33},{97,65},{2,98}... | collective-permute-start | bytes 1572872 | tf_op jit(solution)/shard_map/ppermute | solution.py:265
  71.1 5.5 %all-to-all-start.2 = ((bf16[32,16,512]{2,1,0:T(8,128)(2,1)}), bf16[32,16,512]{2,1,0:T(8,128)(2,1)}, u32[]{:S(2)}, u32[]{:S(2)}) async-start(bf16[32,16,512]{2,1,0:T(8,128)(2,1)} %bitcast.1), calls=%async_computation.2 | async-start | bytes 1048576 | tf_op jit(solution)/shard_map/all_to_all | solution.py:317
  78.8 9.5 %all-to-all-done.2 = bf16[32,16,512]{2,1,0:T(8,128)(2,1)} async-done(((bf16[32,16,512]{2,1,0:T(8,128)(2,1)}), bf16[32,16,512]{2,1,0:T(8,128)(2,1)}, u32[]{:S(2)}, u32[]{:S(2)}) %all-to-all-start.2) | async-done | bytes 524320 | tf_op jit(solution)/shard_map/all_to_all | solution.py:317
  90.7 2.4 %collective-permute-start.2 = (bf16[16,32,512]{2,1,0:T(8,128)(2,1)S(1)}, bf16[16,32,512]{2,1,0:T(8,128)(2,1)S(1)}, u32[]{:S(2)}, u32[]{:S(2)}) collective-permute-start(bf16[16,32,512]{2,1,0:T(8,128)(2,1)S(1)} %bitcast.18), channel_id=1, source_target_pairs={{0,96},{32,0},{64,32},{96,64},{1,97},{33,1},{65,33},{97,65},{2,98}... | collective-permute-start | bytes 1572872 | tf_op jit(solution)/shard_map/ppermute | solution.py:265
  100.0 11.7 %attention.2 = (bf16[16,64,512]{2,1,0:T(8,128)(2,1)}, bf16[16,64,512]{2,1,0:T(8,128)(2,1)}, bf16[16,32,512]{2,1,0:T(8,128)(2,1)S(1)}, bf16[16,32,512]{2,1,0:T(8,...) custom-call(bf16[16,32,512]{2,1,0:T(8,128)(2,1)S(1)} %bitcast.23, ...), custom_call_target="tpu_custom_call" | custom-call | flops 7200000000 | bytes 6400000 | tf_op jit(solution)/shard_map/attention/pallas_call | solution.py:141
  113.3 1.9 collective-permute-start.9
  116.4 12.0 %attention.3 = (bf16[16,64,512]{2,1,0:T(8,128)(2,1)}, bf16[16,64,512]{2,1,0:T(8,128)(2,1)}, bf16[16,32,512]{2,1,0:T(8,128)(2,1)S(1)}, bf16[16,16,512]{2,1,0:T(8,...) custom-call(bf16[16,32,512]{2,1,0:T(8,128)(2,1)S(1)} %bitcast.19, ...), custom_call_target="tpu_custom_call", output_to_operand_aliasing={{0}: (8, {}), {1}: (9, {})} | custom-call | flops 7200000000 | bytes 6400000 | tf_op jit(solution)/shard_map/attention/pallas_call | solution.py:141
  129.5 2.4 %collective-permute-start.7 = (bf16[16,16,512]{2,1,0:T(8,128)(2,1)}, bf16[16,16,512]{2,1,0:T(8,128)(2,1)}, u32[]{:S(2)}, u32[]{:S(2)}) collective-permute-start(bf16[16,16,512]{2,1,0:T(8,128)(2,1)} %get-tuple-element.37), channel_id=1, source_target_pairs={{0,96},{32,0},{64,32},{96,64},{1,97},{33,1},{65,33},{97,65},{2,98}... | collective-permute-start | bytes 786440 | tf_op jit(solution)/shard_map/ppermute | solution.py:265
  131.8 5.4 %all-to-all-start.3 = ((bf16[32,16,1024]{2,1,0:T(8,128)(2,1)}), bf16[32,16,1024]{2,1,0:T(8,128)(2,1)}, u32[]{:S(2)}, u32[]{:S(2)}) async-start(bf16[32,16,1024]{2,1,0:T(8,128)(2,1)} %bitcast.6), calls=%async_computation.3 | async-start | bytes 2097152 | tf_op jit(solution)/shard_map/all_to_all | solution.py:327
  141.7 2.9 %collective-permute-done.6 = bf16[16,16,512]{2,1,0:T(8,128)(2,1)S(1)} collective-permute-done((bf16[16,16,512]{2,1,0:T(8,128)(2,1)}, bf16[16,16,512]{2,1,0:T(8,128)(2,1)S(1)}, u32[]{:S(2)}, u32[]{:S(2)}) %collective-permute-start.6) | collective-permute-done | bytes 262176 | tf_op jit(solution)/shard_map/ppermute | solution.py:265
  145.7 2.4 %collective-permute-start.14 = (bf16[16,16,512]{2,1,0:T(8,128)(2,1)S(1)}, bf16[16,16,512]{2,1,0:T(8,128)(2,1)S(1)}, u32[]{:S(2)}, u32[]{:S(2)}) collective-permute-start(bf16[16,16,512]{2,1,0:T(8,128)(2,1)S(1)} %add_convert_fusion.2), channel_id=1, source_target_pairs={{0,96},{32,0},{64,32},{96,64},{1,97},{33,1},{65,33},{97,65},{2,98}... | collective-permute-start | bytes 786440 | tf_op jit(solution)/shard_map/ppermute | solution.py:265
  148.2 2.1 collective-permute-done.12
  150.3 4.3 %collective-permute-done.14 = bf16[16,16,512]{2,1,0:T(8,128)(2,1)S(1)} collective-permute-done((bf16[16,16,512]{2,1,0:T(8,128)(2,1)S(1)}, bf16[16,16,512]{2,1,0:T(8,128)(2,1)S(1)}, u32[]{:S(2)}, u32[]{:S(2)}) %collective-permute-start.14) | collective-permute-done | bytes 262176 | tf_op jit(solution)/shard_map/ppermute | solution.py:265
  158.3 5.3 %all-to-all-start.4 = ((bf16[32,32,512]{2,1,0:T(8,128)(2,1)}), bf16[32,32,512]{2,1,0:T(8,128)(2,1)S(1)}, u32[]{:S(2)}, u32[]{:S(2)}) async-start(bf16[32,32,512]{2,1,0:T(8,128)(2,1)} %copy.27), calls=%async_computation.4 | async-start | bytes 2097152 | tf_op jit(solution)/shard_map/all_to_all | solution.py:330
  163.7 17.2 %all-to-all-done.4 = bf16[32,32,512]{2,1,0:T(8,128)(2,1)S(1)} async-done(((bf16[32,32,512]{2,1,0:T(8,128)(2,1)}), bf16[32,32,512]{2,1,0:T(8,128)(2,1)S(1)}, u32[]{:S(2)}, u32[]{:S(2)}) %all-to-all-start.4) | async-done | bytes 1048608 | tf_op jit(solution)/shard_map/all_to_all | solution.py:330
  180.9 3.7 %place_rows.1 = bf16[2048,512]{1,0:T(8,128)(2,1)} custom-call(s32[1,1024]{1,0:T(1,128)S(1)} %add.63.ids_ref, bf16[1024,512]{1,0:T(8,128)(2,1)S(1)} %bitcast.15), custom_call_target="tpu_custom_call" | custom-call | tf_op jit(solution)/shard_map/place_rows/pallas_call | solution.py:253
  184.6 3.8 %all-to-all-start.5 = ((bf16[128,16,512]{2,1,0:T(8,128)(2,1)}), bf16[128,16,512]{2,1,0:T(8,128)(2,1)S(1)}, u32[]{:S(2)}, u32[]{:S(2)}) async-start(bf16[128,16,512]{2,1,0:T(8,128)(2,1)} %bitcast.8), calls=%async_computation.5 | async-start | bytes 4194304 | tf_op jit(solution)/shard_map/all_to_all | solution.py:332
  190.4 28.5 %all-to-all-done.5 = bf16[128,16,512]{2,1,0:T(8,128)(2,1)S(1)} async-done(((bf16[128,16,512]{2,1,0:T(8,128)(2,1)}), bf16[128,16,512]{2,1,0:T(8,128)(2,1)S(1)}, u32[]{:S(2)}, u32[]{:S(2)}) %all-to-all-start.5) | async-done | bytes 2097184 | tf_op jit(solution)/shard_map/all_to_all | solution.py:332
  219.0 2.5 %copy.28 = bf16[16,128,512]{2,1,0:T(8,128)(2,1)} copy(bf16[16,128,512]{2,0,1:T(8,128)(2,1)S(1)} %bitcast.24) | data formatting | bytes 4194304
  (66 shorter events, 33.1 us)
Async XLA Ops:
  1.5 1.6 copy-start
  50.7 16.3 %all-to-all-start.1 = ((bf16[32,16,512]{2,1,0:T(8,128)(2,1)}), bf16[32,16,512]{2,1,0:T(8,128)(2,1)S(1)}, u32[]{:S(2)}, u32[]{:S(2)}) async-start(bf16[32,16,512]{2,1,0:T(8,128)(2,1)} %bitcast.2), calls=%async_computation.1 | async-start | bytes 1048576 | tf_op jit(solution)/shard_map/all_to_all | solution.py:317
  67.2 23.5 %collective-permute-start.3 = (bf16[16,32,512]{2,1,0:T(8,128)(2,1)S(1)}, bf16[16,32,512]{2,1,0:T(8,128)(2,1)S(1)}, u32[]{:S(2)}, u32[]{:S(2)}) collective-permute-start(bf16[16,32,512]{2,1,0:T(8,128)(2,1)S(1)} %bitcast.20), channel_id=1, source_target_pairs={{0,64},{32,96},{64,0},{96,32},{1,65},{33,97},{65,1},{97,33},{2,66}... | collective-permute-start | bytes 1572872 | tf_op jit(solution)/shard_map/ppermute | solution.py:265
  68.4 25.5 %collective-permute-start.4 = (bf16[16,32,512]{2,1,0:T(8,128)(2,1)S(1)}, bf16[16,32,512]{2,1,0:T(8,128)(2,1)S(1)}, u32[]{:S(2)}, u32[]{:S(2)}) collective-permute-start(bf16[16,32,512]{2,1,0:T(8,128)(2,1)S(1)} %bitcast.21), channel_id=1, source_target_pairs={{0,32},{32,64},{64,96},{96,0},{1,33},{33,65},{65,97},{97,1},{2,34}... | collective-permute-start | bytes 1572872 | tf_op jit(solution)/shard_map/ppermute | solution.py:265
  68.8 25.9 %collective-permute-start.5 = (bf16[16,32,512]{2,1,0:T(8,128)(2,1)S(1)}, bf16[16,32,512]{2,1,0:T(8,128)(2,1)S(1)}, u32[]{:S(2)}, u32[]{:S(2)}) collective-permute-start(bf16[16,32,512]{2,1,0:T(8,128)(2,1)S(1)} %bitcast.22), channel_id=1, source_target_pairs={{0,96},{32,0},{64,32},{96,64},{1,97},{33,1},{65,33},{97,65},{2,98}... | collective-permute-start | bytes 1572872 | tf_op jit(solution)/shard_map/ppermute | solution.py:265
  71.1 17.2 %all-to-all-start.2 = ((bf16[32,16,512]{2,1,0:T(8,128)(2,1)}), bf16[32,16,512]{2,1,0:T(8,128)(2,1)}, u32[]{:S(2)}, u32[]{:S(2)}) async-start(bf16[32,16,512]{2,1,0:T(8,128)(2,1)} %bitcast.1), calls=%async_computation.2 | async-start | bytes 1048576 | tf_op jit(solution)/shard_map/all_to_all | solution.py:317
  88.3 28.1 %copy-start.3 = (bf16[16,64,512]{2,1,0:T(8,128)(2,1)S(1)}, bf16[16,64,512]{2,1,0:T(8,128)(2,1)}, u32[]{:S(2)}) copy-start(bf16[16,64,512]{2,1,0:T(8,128)(2,1)} %refs_5_.3) | copy-start | bytes 3145732
  89.8 23.6 %collective-permute-start = (bf16[16,32,512]{2,1,0:T(8,128)(2,1)S(1)}, bf16[16,32,512]{2,1,0:T(8,128)(2,1)S(1)}, u32[]{:S(2)}, u32[]{:S(2)}) collective-permute-start(bf16[16,32,512]{2,1,0:T(8,128)(2,1)S(1)} %bitcast.16), channel_id=1, source_target_pairs={{0,64},{32,96},{64,0},{96,32},{1,65},{33,97},{65,1},{97,33},{2,66}... | collective-permute-start | bytes 1572872 | tf_op jit(solution)/shard_map/ppermute | solution.py:265
  90.5 26.0 %collective-permute-start.1 = (bf16[16,32,512]{2,1,0:T(8,128)(2,1)S(1)}, bf16[16,32,512]{2,1,0:T(8,128)(2,1)S(1)}, u32[]{:S(2)}, u32[]{:S(2)}) collective-permute-start(bf16[16,32,512]{2,1,0:T(8,128)(2,1)S(1)} %bitcast.17), channel_id=1, source_target_pairs={{0,32},{32,64},{64,96},{96,0},{1,33},{33,65},{65,97},{97,1},{2,34}... | collective-permute-start | bytes 1572872 | tf_op jit(solution)/shard_map/ppermute | solution.py:265
  90.7 25.7 %collective-permute-start.2 = (bf16[16,32,512]{2,1,0:T(8,128)(2,1)S(1)}, bf16[16,32,512]{2,1,0:T(8,128)(2,1)S(1)}, u32[]{:S(2)}, u32[]{:S(2)}) collective-permute-start(bf16[16,32,512]{2,1,0:T(8,128)(2,1)S(1)} %bitcast.18), channel_id=1, source_target_pairs={{0,96},{32,0},{64,32},{96,64},{1,97},{33,1},{65,33},{97,65},{2,98}... | collective-permute-start | bytes 1572872 | tf_op jit(solution)/shard_map/ppermute | solution.py:265
  95.5 1.2 copy-start.1
  111.7 25.5 %collective-permute-start.10 = (bf16[16,32,512]{2,1,0:T(8,128)(2,1)}, bf16[16,32,512]{2,1,0:T(8,128)(2,1)}, u32[]{:S(2)}, u32[]{:S(2)}) collective-permute-start(bf16[16,32,512]{2,1,0:T(8,128)(2,1)} %get-tuple-element.41), channel_id=1, source_target_pairs={{0,32},{32,64},{64,96},{96,0},{1,33},{33,65},{65,97},{97,1},{2,34}... | collective-permute-start | bytes 1572872 | tf_op jit(solution)/shard_map/ppermute | solution.py:265
  112.0 26.3 %collective-permute-start.8 = (bf16[16,32,512]{2,1,0:T(8,128)(2,1)}, bf16[16,32,512]{2,1,0:T(8,128)(2,1)}, u32[]{:S(2)}, u32[]{:S(2)}) collective-permute-start(bf16[16,32,512]{2,1,0:T(8,128)(2,1)} %get-tuple-element.39), channel_id=1, source_target_pairs={{0,64},{32,96},{64,0},{96,32},{1,65},{33,97},{65,1},{97,33},{2,66}... | collective-permute-start | bytes 1572872 | tf_op jit(solution)/shard_map/ppermute | solution.py:265
  113.3 26.7 %collective-permute-start.9 = (bf16[16,32,512]{2,1,0:T(8,128)(2,1)S(1)}, bf16[16,32,512]{2,1,0:T(8,128)(2,1)}, u32[]{:S(2)}, u32[]{:S(2)}) collective-permute-start(bf16[16,32,512]{2,1,0:T(8,128)(2,1)S(1)} %get-tuple-element.40), channel_id=1, source_target_pairs={{0,96},{32,0},{64,32},{96,64},{1,97},{33,1},{65,33},{97,65},{2,98}... | collective-permute-start | bytes 1572872 | tf_op jit(solution)/shard_map/ppermute | solution.py:265
  129.2 8.1 %copy-start.9 = (bf16[16,16,512]{2,1,0:T(8,128)(2,1)S(1)}, bf16[16,16,512]{2,1,0:T(8,128)(2,1)}, u32[]{:S(2)}) copy-start(bf16[16,16,512]{2,1,0:T(8,128)(2,1)} %copy-done.8) | copy-start | bytes 786436
  129.2 15.5 %collective-permute-start.6 = (bf16[16,16,512]{2,1,0:T(8,128)(2,1)}, bf16[16,16,512]{2,1,0:T(8,128)(2,1)S(1)}, u32[]{:S(2)}, u32[]{:S(2)}) collective-permute-start(bf16[16,16,512]{2,1,0:T(8,128)(2,1)} %get-tuple-element.36), channel_id=1, source_target_pairs={{0,32},{32,64},{64,96},{96,0},{1,33},{33,65},{65,97},{97,1},{2,34}... | collective-permute-start | bytes 786440 | tf_op jit(solution)/shard_map/ppermute | solution.py:265
  129.5 15.2 %collective-permute-start.7 = (bf16[16,16,512]{2,1,0:T(8,128)(2,1)}, bf16[16,16,512]{2,1,0:T(8,128)(2,1)}, u32[]{:S(2)}, u32[]{:S(2)}) collective-permute-start(bf16[16,16,512]{2,1,0:T(8,128)(2,1)} %get-tuple-element.37), channel_id=1, source_target_pairs={{0,96},{32,0},{64,32},{96,64},{1,97},{33,1},{65,33},{97,65},{2,98}... | collective-permute-start | bytes 786440 | tf_op jit(solution)/shard_map/ppermute | solution.py:265
  131.8 24.9 %all-to-all-start.3 = ((bf16[32,16,1024]{2,1,0:T(8,128)(2,1)}), bf16[32,16,1024]{2,1,0:T(8,128)(2,1)}, u32[]{:S(2)}, u32[]{:S(2)}) async-start(bf16[32,16,1024]{2,1,0:T(8,128)(2,1)} %bitcast.6), calls=%async_computation.3 | async-start | bytes 2097152 | tf_op jit(solution)/shard_map/all_to_all | solution.py:327
  137.3 13.0 %collective-permute-start.12 = (bf16[16,16,512]{2,1,0:T(8,128)(2,1)S(1)}, bf16[16,16,512]{2,1,0:T(8,128)(2,1)S(1)}, u32[]{:S(2)}, u32[]{:S(2)}) collective-permute-start(bf16[16,16,512]{2,1,0:T(8,128)(2,1)S(1)} %copy-done.9), channel_id=1, source_target_pairs={{0,32},{32,64},{64,96},{96,0},{1,33},{33,65},{65,97},{97,1},{2,34}... | collective-permute-start | bytes 786440 | tf_op jit(solution)/shard_map/ppermute | solution.py:265
  138.3 12.0 %collective-permute-start.13 = (bf16[16,16,512]{2,1,0:T(8,128)(2,1)S(1)}, bf16[16,16,512]{2,1,0:T(8,128)(2,1)S(1)}, u32[]{:S(2)}, u32[]{:S(2)}) collective-permute-start(bf16[16,16,512]{2,1,0:T(8,128)(2,1)S(1)} %get-tuple-element.47), channel_id=1, source_target_pairs={{0,96},{32,0},{64,32},{96,64},{1,97},{33,1},{65,33},{97,65},{2,98}... | collective-permute-start | bytes 786440 | tf_op jit(solution)/shard_map/ppermute | solution.py:265
  145.7 8.9 %collective-permute-start.14 = (bf16[16,16,512]{2,1,0:T(8,128)(2,1)S(1)}, bf16[16,16,512]{2,1,0:T(8,128)(2,1)S(1)}, u32[]{:S(2)}, u32[]{:S(2)}) collective-permute-start(bf16[16,16,512]{2,1,0:T(8,128)(2,1)S(1)} %add_convert_fusion.2), channel_id=1, source_target_pairs={{0,96},{32,0},{64,32},{96,64},{1,97},{33,1},{65,33},{97,65},{2,98}... | collective-permute-start | bytes 786440 | tf_op jit(solution)/shard_map/ppermute | solution.py:265
  148.1 8.2 %collective-permute-start.11 = (bf16[16,16,512]{2,1,0:T(8,128)(2,1)S(1)}, bf16[16,16,512]{2,1,0:T(8,128)(2,1)S(1)}, u32[]{:S(2)}, u32[]{:S(2)}) collective-permute-start(bf16[16,16,512]{2,1,0:T(8,128)(2,1)S(1)} %add_convert_fusion.3), channel_id=1, source_target_pairs={{0,32},{32,64},{64,96},{96,0},{1,33},{33,65},{65,97},{97,1},{2,34}... | collective-permute-start | bytes 786440 | tf_op jit(solution)/shard_map/ppermute | solution.py:265
  158.3 22.6 %all-to-all-start.4 = ((bf16[32,32,512]{2,1,0:T(8,128)(2,1)}), bf16[32,32,512]{2,1,0:T(8,128)(2,1)S(1)}, u32[]{:S(2)}, u32[]{:S(2)}) async-start(bf16[32,32,512]{2,1,0:T(8,128)(2,1)} %copy.27), calls=%async_computation.4 | async-start | bytes 2097152 | tf_op jit(solution)/shard_map/all_to_all | solution.py:330
  184.6 34.4 %all-to-all-start.5 = ((bf16[128,16,512]{2,1,0:T(8,128)(2,1)}), bf16[128,16,512]{2,1,0:T(8,128)(2,1)S(1)}, u32[]{:S(2)}, u32[]{:S(2)}) async-start(bf16[128,16,512]{2,1,0:T(8,128)(2,1)} %bitcast.8), calls=%async_computation.5 | async-start | bytes 4194304 | tf_op jit(solution)/shard_map/all_to_all | solution.py:332
  (6 other events, 5.6 us)

commit v7 on v6

--- a/solution.py
+++ b/solution.py
@@ -185,6 +185,29 @@
         compiler_params=pltpu.CompilerParams(vmem_limit_bytes=32 * 1024 * 1024),
         name="spread_rows",
     )(x, ids)
+
+
+def gather_kernel(x_ref, out_ref):
+    rows, held, width = x_ref.shape
+    count = held * SPREAD_TILE
+    at = lax.broadcasted_iota(jnp.int32, (count, count), 0)
+    source = lax.rem(at, SPREAD_TILE) * held + at // SPREAD_TILE
+    turn = (source == lax.broadcasted_iota(jnp.int32, (count, count), 1)).astype(BF16)
+    for r in range(0, rows, SPREAD_TILE):
+        turned = mm(turn, x_ref[r : r + SPREAD_TILE].reshape(count, width)).astype(BF16)
+        out_ref[:, r : r + SPREAD_TILE] = turned.reshape(held, SPREAD_TILE, width)
+
+
+def gather_rows(x):
+    rows, held, width = x.shape
+    return pl.pallas_call(
+        gather_kernel,
+        in_specs=[pl.BlockSpec(memory_space=pltpu.VMEM)],
+        out_specs=pl.BlockSpec(memory_space=pltpu.VMEM),
+        out_shape=jax.ShapeDtypeStruct((held, rows, width), BF16),
+        compiler_params=pltpu.CompilerParams(vmem_limit_bytes=32 * 1024 * 1024),
+        name="gather_rows",
+    )(x)
 
 
 def pick_first_kernel(held, shards, first, table_ref, out_ref):
@@ -329,7 +352,7 @@
     summed, d_w = lax.optimization_barrier((summed, d_w))
     rows = lax.all_to_all(summed, "dp", 0, 0, tiled=True).reshape(shards * pair_count, width)
     placed = place_rows(ids.reshape(-1), rows, devices * held).reshape(devices, held, width)
-    d_encodings = jnp.swapaxes(lax.all_to_all(placed, BOTH, 0, 0, tiled=True), 0, 1)
+    d_encodings = gather_rows(lax.all_to_all(placed, BOTH, 0, 0, tiled=True))
     d_w = jnp.sum(d_w.astype(F32), axis=0)
     return att, dq, d_encodings, d_w[:, :cols], d_w[:, cols:]
 

time: 222 us -> 222 us (level)
    unnamed x23 -> x24, local copies, waits for them, and re-layouts: 12.7 us -> 11.6 us
  transfers between devices with their start and end apart: 20 -> 20, of which waited for: 11 -> 11; matrix products, arithmetic and copies ran while one was open for 5% -> 4% of each run, Pallas kernels for 12% -> 12%
where the time goes in v7:
time: 222 us; the launch traced here: 221 us
  waiting for transfers between devices  77.3 us (35%)
  blocking collectives  44.6 us (20%)
  starting transfers between devices  43 us (19%)
  Pallas kernels  33.2 us (15%)
  local copies, waits for them, and re-layouts  17.5 us (8%)
  other arithmetic  4.32 us (2%)
    all_to_all x1, blocking collectives, body(): table = lax.all_to_all(by_row, BOTH, 0, 0, tiled=True)  44.6 us
    all_to_all x1, waiting for transfers between devices, body(): d_encodings = gather_rows(lax.all_to_all(placed, BOTH, 0, 0, tiled=True))  28.4 us
    pallas_call x2, Pallas kernels, attention(): pl.pallas_call(functools.partial(attention_kernel, first, last), grid=(st...  23.7 us
    ppermute x15, starting transfers between devices, shift(): lax.ppermute(value, 'enc', [(i, (i + by) % count) for i in range(count)])  17.7 us
    all_to_all x2, waiting for transfers between devices, body(): own = jnp.swapaxes(lax.all_to_all(sent[c], 'dp', 0, 0, tiled=True), 0, 1)  17.6 us
    all_to_all x1, waiting for transfers between devices, body(): lax.all_to_all(summed, 'dp', 0, 0, tiled=True)  17.2 us
    ppermute x15, waiting for transfers between devices, shift(): lax.ppermute(value, 'enc', [(i, (i + by) % count) for i in range(count)])  14.1 us
    unnamed x24, local copies, waits for them, and re-layouts  11.6 us
  transfers between devices with their start and end apart: 20, of which 11 were waited for; matrix products, arithmetic and copies ran while one was open for 4% of the time, Pallas kernels for 12%

profile of v7, /device:TPU:1, one launch (start us, length us, event | category | flops | bytes accessed | tf_op | source)
XLA Modules:
  0.0 220.7 jit_solution(3526948212596336871)
XLA Ops:
  3.8 44.6 %all_to_all.30.table_ref = bf16[128,72,128]{2,1,0:T(8,128)(2,1)S(1)} all-to-all(bf16[128,72,128]{2,1,0:T(8,128)(2,1)S(1)} %spread_rows.1), channel_id=1, replica_groups=mesh['enc'=4,'dp'=32] {'enc','dp'}, dimensions={0} | all-to-all | bytes 4718592 | tf_op jit(solution)/shard_map/all_to_all | solution.py:322
  48.4 2.2 %pick_first_rows.1 = bf16[512,512]{1,0:T(8,128)(2,1)} custom-call(bf16[128,72,128]{2,1,0:T(8,128)(2,1)S(1)} %all_to_all.30.table_ref), custom_call_target="tpu_custom_call" | custom-call | tf_op jit(solution)/shard_map/pick_first_rows/pallas_call | solution.py:234
  50.7 4.6 %all-to-all-start.1 = ((bf16[32,16,512]{2,1,0:T(8,128)(2,1)}), bf16[32,16,512]{2,1,0:T(8,128)(2,1)S(1)}, u32[]{:S(2)}, u32[]{:S(2)}) async-start(bf16[32,16,512]{2,1,0:T(8,128)(2,1)} %bitcast.2), calls=%async_computation.1 | async-start | bytes 1048576 | tf_op jit(solution)/shard_map/all_to_all | solution.py:340
  56.8 2.1 pick_rows.1
  58.9 8.1 %all-to-all-done.1 = bf16[32,16,512]{2,1,0:T(8,128)(2,1)S(1)} async-done(((bf16[32,16,512]{2,1,0:T(8,128)(2,1)}), bf16[32,16,512]{2,1,0:T(8,128)(2,1)S(1)}, u32[]{:S(2)}, u32[]{:S(2)}) %all-to-all-start.1) | async-done | bytes 524320 | tf_op jit(solution)/shard_map/all_to_all | solution.py:340
  68.8 2.4 %collective-permute-start.5 = (bf16[16,32,512]{2,1,0:T(8,128)(2,1)S(1)}, bf16[16,32,512]{2,1,0:T(8,128)(2,1)S(1)}, u32[]{:S(2)}, u32[]{:S(2)}) collective-permute-start(bf16[16,32,512]{2,1,0:T(8,128)(2,1)S(1)} %bitcast.22), channel_id=1, source_target_pairs={{0,96},{32,0},{64,32},{96,64},{1,97},{33,1},{65,33},{97,65},{2,98}... | collective-permute-start | bytes 1572872 | tf_op jit(solution)/shard_map/ppermute | solution.py:288
  71.1 5.5 %all-to-all-start.2 = ((bf16[32,16,512]{2,1,0:T(8,128)(2,1)}), bf16[32,16,512]{2,1,0:T(8,128)(2,1)}, u32[]{:S(2)}, u32[]{:S(2)}) async-start(bf16[32,16,512]{2,1,0:T(8,128)(2,1)} %bitcast.1), calls=%async_computation.2 | async-start | bytes 1048576 | tf_op jit(solution)/shard_map/all_to_all | solution.py:340
  78.8 9.5 %all-to-all-done.2 = bf16[32,16,512]{2,1,0:T(8,128)(2,1)} async-done(((bf16[32,16,512]{2,1,0:T(8,128)(2,1)}), bf16[32,16,512]{2,1,0:T(8,128)(2,1)}, u32[]{:S(2)}, u32[]{:S(2)}) %all-to-all-start.2) | async-done | bytes 524320 | tf_op jit(solution)/shard_map/all_to_all | solution.py:340
  90.7 2.4 %collective-permute-start.2 = (bf16[16,32,512]{2,1,0:T(8,128)(2,1)S(1)}, bf16[16,32,512]{2,1,0:T(8,128)(2,1)S(1)}, u32[]{:S(2)}, u32[]{:S(2)}) collective-permute-start(bf16[16,32,512]{2,1,0:T(8,128)(2,1)S(1)} %bitcast.18), channel_id=1, source_target_pairs={{0,96},{32,0},{64,32},{96,64},{1,97},{33,1},{65,33},{97,65},{2,98}... | collective-permute-start | bytes 1572872 | tf_op jit(solution)/shard_map/ppermute | solution.py:288
  100.0 11.7 %attention.2 = (bf16[16,64,512]{2,1,0:T(8,128)(2,1)}, bf16[16,64,512]{2,1,0:T(8,128)(2,1)}, bf16[16,32,512]{2,1,0:T(8,128)(2,1)S(1)}, bf16[16,32,512]{2,1,0:T(8,...) custom-call(bf16[16,32,512]{2,1,0:T(8,128)(2,1)S(1)} %bitcast.23, ...), custom_call_target="tpu_custom_call" | custom-call | flops 7200000000 | bytes 6400000 | tf_op jit(solution)/shard_map/attention/pallas_call | solution.py:141
  113.3 1.9 collective-permute-start.9
  116.4 12.0 %attention.3 = (bf16[16,64,512]{2,1,0:T(8,128)(2,1)}, bf16[16,64,512]{2,1,0:T(8,128)(2,1)}, bf16[16,32,512]{2,1,0:T(8,128)(2,1)S(1)}, bf16[16,16,512]{2,1,0:T(8,...) custom-call(bf16[16,32,512]{2,1,0:T(8,128)(2,1)S(1)} %bitcast.19, ...), custom_call_target="tpu_custom_call", output_to_operand_aliasing={{0}: (8, {}), {1}: (9, {})} | custom-call | flops 7200000000 | bytes 6400000 | tf_op jit(solution)/shard_map/attention/pallas_call | solution.py:141
  129.5 2.4 %collective-permute-start.7 = (bf16[16,16,512]{2,1,0:T(8,128)(2,1)}, bf16[16,16,512]{2,1,0:T(8,128)(2,1)S(1)}, u32[]{:S(2)}, u32[]{:S(2)}) collective-permute-start(bf16[16,16,512]{2,1,0:T(8,128)(2,1)} %get-tuple-element.37), channel_id=1, source_target_pairs={{0,96},{32,0},{64,32},{96,64},{1,97},{33,1},{65,33},{97,65},{2,98}... | collective-permute-start | bytes 786440 | tf_op jit(solution)/shard_map/ppermute | solution.py:288
  131.8 5.4 %all-to-all-start.3 = ((bf16[32,16,1024]{2,1,0:T(8,128)(2,1)}), bf16[32,16,1024]{2,1,0:T(8,128)(2,1)}, u32[]{:S(2)}, u32[]{:S(2)}) async-start(bf16[32,16,1024]{2,1,0:T(8,128)(2,1)} %bitcast.6), calls=%async_computation.3 | async-start | bytes 2097152 | tf_op jit(solution)/shard_map/all_to_all | solution.py:350
  141.7 2.9 %collective-permute-done.6 = bf16[16,16,512]{2,1,0:T(8,128)(2,1)S(1)} collective-permute-done((bf16[16,16,512]{2,1,0:T(8,128)(2,1)}, bf16[16,16,512]{2,1,0:T(8,128)(2,1)S(1)}, u32[]{:S(2)}, u32[]{:S(2)}) %collective-permute-start.6) | collective-permute-done | bytes 262176 | tf_op jit(solution)/shard_map/ppermute | solution.py:288
  144.7 2.4 %collective-permute-start.14 = (bf16[16,16,512]{2,1,0:T(8,128)(2,1)S(1)}, bf16[16,16,512]{2,1,0:T(8,128)(2,1)S(1)}, u32[]{:S(2)}, u32[]{:S(2)}) collective-permute-start(bf16[16,16,512]{2,1,0:T(8,128)(2,1)S(1)} %add_convert_fusion.2), channel_id=1, source_target_pairs={{0,96},{32,0},{64,32},{96,64},{1,97},{33,1},{65,33},{97,65},{2,98}... | collective-permute-start | bytes 786440 | tf_op jit(solution)/shard_map/ppermute | solution.py:288
  147.3 3.0 %collective-permute-done.12 = bf16[16,16,512]{2,1,0:T(8,128)(2,1)S(1)} collective-permute-done((bf16[16,16,512]{2,1,0:T(8,128)(2,1)S(1)}, bf16[16,16,512]{2,1,0:T(8,128)(2,1)S(1)}, u32[]{:S(2)}, u32[]{:S(2)}) %collective-permute-start.12) | collective-permute-done | bytes 262176 | tf_op jit(solution)/shard_map/ppermute | solution.py:288
  150.3 4.4 %collective-permute-done.14 = bf16[16,16,512]{2,1,0:T(8,128)(2,1)S(1)} collective-permute-done((bf16[16,16,512]{2,1,0:T(8,128)(2,1)S(1)}, bf16[16,16,512]{2,1,0:T(8,128)(2,1)S(1)}, u32[]{:S(2)}, u32[]{:S(2)}) %collective-permute-start.14) | collective-permute-done | bytes 262176 | tf_op jit(solution)/shard_map/ppermute | solution.py:288
  157.4 5.2 %all-to-all-start.4 = ((bf16[32,32,512]{2,1,0:T(8,128)(2,1)}), bf16[32,32,512]{2,1,0:T(8,128)(2,1)S(1)}, u32[]{:S(2)}, u32[]{:S(2)}) async-start(bf16[32,32,512]{2,1,0:T(8,128)(2,1)} %copy.25), calls=%async_computation.4 | async-start | bytes 2097152 | tf_op jit(solution)/shard_map/all_to_all | solution.py:353
  162.8 17.2 %all-to-all-done.4 = bf16[32,32,512]{2,1,0:T(8,128)(2,1)S(1)} async-done(((bf16[32,32,512]{2,1,0:T(8,128)(2,1)}), bf16[32,32,512]{2,1,0:T(8,128)(2,1)S(1)}, u32[]{:S(2)}, u32[]{:S(2)}) %all-to-all-start.4) | async-done | bytes 1048608 | tf_op jit(solution)/shard_map/all_to_all | solution.py:353
  180.0 2.3 %place_rows.1 = bf16[2048,512]{1,0:T(8,128)(2,1)S(1)} custom-call(s32[1,1024]{1,0:T(1,128)S(1)} %add.63.ids_ref, bf16[1024,512]{1,0:T(8,128)(2,1)S(1)} %bitcast.15), custom_call_target="tpu_custom_call" | custom-call | tf_op jit(solution)/shard_map/place_rows/pallas_call | solution.py:276
  183.6 4.7 %all-to-all-start.5 = ((bf16[128,16,512]{2,1,0:T(8,128)(2,1)}), bf16[128,16,512]{2,1,0:T(8,128)(2,1)S(1)}, u32[]{:S(2)}, u32[]{:S(2)}) async-start(bf16[128,16,512]{2,1,0:T(8,128)(2,1)} %bitcast.14), calls=%async_computation.5 | async-start | bytes 4194304 | tf_op jit(solution)/shard_map/all_to_all | solution.py:355
  190.3 28.4 %all-to-all-done.5.x_ref = bf16[128,16,512]{2,1,0:T(8,128)(2,1)S(1)} async-done(((bf16[128,16,512]{2,1,0:T(8,128)(2,1)}), bf16[128,16,512]{2,1,0:T(8,128)(2,1)S(1)}, u32[]{:S(2)}, u32[]{:S(2)}) %all-to-all-start.5) | async-done | bytes 2097184 | tf_op jit(solution)/shard_map/all_to_all | solution.py:355
  218.7 2.0 gather_rows.1
  (68 shorter events, 32.6 us)
Async XLA Ops:
  1.5 1.6 copy-start.1
  50.7 16.3 %all-to-all-start.1 = ((bf16[32,16,512]{2,1,0:T(8,128)(2,1)}), bf16[32,16,512]{2,1,0:T(8,128)(2,1)S(1)}, u32[]{:S(2)}, u32[]{:S(2)}) async-start(bf16[32,16,512]{2,1,0:T(8,128)(2,1)} %bitcast.2), calls=%async_computation.1 | async-start | bytes 1048576 | tf_op jit(solution)/shard_map/all_to_all | solution.py:340
  67.2 23.5 %collective-permute-start.3 = (bf16[16,32,512]{2,1,0:T(8,128)(2,1)S(1)}, bf16[16,32,512]{2,1,0:T(8,128)(2,1)S(1)}, u32[]{:S(2)}, u32[]{:S(2)}) collective-permute-start(bf16[16,32,512]{2,1,0:T(8,128)(2,1)S(1)} %bitcast.20), channel_id=1, source_target_pairs={{0,64},{32,96},{64,0},{96,32},{1,65},{33,97},{65,1},{97,33},{2,66}... | collective-permute-start | bytes 1572872 | tf_op jit(solution)/shard_map/ppermute | solution.py:288
  68.4 25.5 %collective-permute-start.4 = (bf16[16,32,512]{2,1,0:T(8,128)(2,1)S(1)}, bf16[16,32,512]{2,1,0:T(8,128)(2,1)S(1)}, u32[]{:S(2)}, u32[]{:S(2)}) collective-permute-start(bf16[16,32,512]{2,1,0:T(8,128)(2,1)S(1)} %bitcast.21), channel_id=1, source_target_pairs={{0,32},{32,64},{64,96},{96,0},{1,33},{33,65},{65,97},{97,1},{2,34}... | collective-permute-start | bytes 1572872 | tf_op jit(solution)/shard_map/ppermute | solution.py:288
  68.8 25.9 %collective-permute-start.5 = (bf16[16,32,512]{2,1,0:T(8,128)(2,1)S(1)}, bf16[16,32,512]{2,1,0:T(8,128)(2,1)S(1)}, u32[]{:S(2)}, u32[]{:S(2)}) collective-permute-start(bf16[16,32,512]{2,1,0:T(8,128)(2,1)S(1)} %bitcast.22), channel_id=1, source_target_pairs={{0,96},{32,0},{64,32},{96,64},{1,97},{33,1},{65,33},{97,65},{2,98}... | collective-permute-start | bytes 1572872 | tf_op jit(solution)/shard_map/ppermute | solution.py:288
  71.1 17.2 %all-to-all-start.2 = ((bf16[32,16,512]{2,1,0:T(8,128)(2,1)}), bf16[32,16,512]{2,1,0:T(8,128)(2,1)}, u32[]{:S(2)}, u32[]{:S(2)}) async-start(bf16[32,16,512]{2,1,0:T(8,128)(2,1)} %bitcast.1), calls=%async_computation.2 | async-start | bytes 1048576 | tf_op jit(solution)/shard_map/all_to_all | solution.py:340
  88.3 28.1 %copy-start.4 = (bf16[16,64,512]{2,1,0:T(8,128)(2,1)S(1)}, bf16[16,64,512]{2,1,0:T(8,128)(2,1)}, u32[]{:S(2)}) copy-start(bf16[16,64,512]{2,1,0:T(8,128)(2,1)} %refs_5_.3) | copy-start | bytes 3145732
  89.7 23.6 %collective-permute-start = (bf16[16,32,512]{2,1,0:T(8,128)(2,1)S(1)}, bf16[16,32,512]{2,1,0:T(8,128)(2,1)S(1)}, u32[]{:S(2)}, u32[]{:S(2)}) collective-permute-start(bf16[16,32,512]{2,1,0:T(8,128)(2,1)S(1)} %bitcast.16), channel_id=1, source_target_pairs={{0,64},{32,96},{64,0},{96,32},{1,65},{33,97},{65,1},{97,33},{2,66}... | collective-permute-start | bytes 1572872 | tf_op jit(solution)/shard_map/ppermute | solution.py:288
  90.5 26.0 %collective-permute-start.1 = (bf16[16,32,512]{2,1,0:T(8,128)(2,1)S(1)}, bf16[16,32,512]{2,1,0:T(8,128)(2,1)S(1)}, u32[]{:S(2)}, u32[]{:S(2)}) collective-permute-start(bf16[16,32,512]{2,1,0:T(8,128)(2,1)S(1)} %bitcast.17), channel_id=1, source_target_pairs={{0,32},{32,64},{64,96},{96,0},{1,33},{33,65},{65,97},{97,1},{2,34}... | collective-permute-start | bytes 1572872 | tf_op jit(solution)/shard_map/ppermute | solution.py:288
  90.7 25.7 %collective-permute-start.2 = (bf16[16,32,512]{2,1,0:T(8,128)(2,1)S(1)}, bf16[16,32,512]{2,1,0:T(8,128)(2,1)S(1)}, u32[]{:S(2)}, u32[]{:S(2)}) collective-permute-start(bf16[16,32,512]{2,1,0:T(8,128)(2,1)S(1)} %bitcast.18), channel_id=1, source_target_pairs={{0,96},{32,0},{64,32},{96,64},{1,97},{33,1},{65,33},{97,65},{2,98}... | collective-permute-start | bytes 1572872 | tf_op jit(solution)/shard_map/ppermute | solution.py:288
  111.7 25.5 %collective-permute-start.10 = (bf16[16,32,512]{2,1,0:T(8,128)(2,1)}, bf16[16,32,512]{2,1,0:T(8,128)(2,1)}, u32[]{:S(2)}, u32[]{:S(2)}) collective-permute-start(bf16[16,32,512]{2,1,0:T(8,128)(2,1)} %get-tuple-element.41), channel_id=1, source_target_pairs={{0,32},{32,64},{64,96},{96,0},{1,33},{33,65},{65,97},{97,1},{2,34}... | collective-permute-start | bytes 1572872 | tf_op jit(solution)/shard_map/ppermute | solution.py:288
  112.0 26.3 %collective-permute-start.8 = (bf16[16,32,512]{2,1,0:T(8,128)(2,1)}, bf16[16,32,512]{2,1,0:T(8,128)(2,1)}, u32[]{:S(2)}, u32[]{:S(2)}) collective-permute-start(bf16[16,32,512]{2,1,0:T(8,128)(2,1)} %get-tuple-element.39), channel_id=1, source_target_pairs={{0,64},{32,96},{64,0},{96,32},{1,65},{33,97},{65,1},{97,33},{2,66}... | collective-permute-start | bytes 1572872 | tf_op jit(solution)/shard_map/ppermute | solution.py:288
  113.3 26.7 %collective-permute-start.9 = (bf16[16,32,512]{2,1,0:T(8,128)(2,1)S(1)}, bf16[16,32,512]{2,1,0:T(8,128)(2,1)}, u32[]{:S(2)}, u32[]{:S(2)}) collective-permute-start(bf16[16,32,512]{2,1,0:T(8,128)(2,1)S(1)} %get-tuple-element.40), channel_id=1, source_target_pairs={{0,96},{32,0},{64,32},{96,64},{1,97},{33,1},{65,33},{97,65},{2,98}... | collective-permute-start | bytes 1572872 | tf_op jit(solution)/shard_map/ppermute | solution.py:288
  129.2 8.1 %copy-start.10 = (bf16[16,16,512]{2,1,0:T(8,128)(2,1)S(1)}, bf16[16,16,512]{2,1,0:T(8,128)(2,1)}, u32[]{:S(2)}) copy-start(bf16[16,16,512]{2,1,0:T(8,128)(2,1)} %copy-done.9) | copy-start | bytes 786436
  129.2 15.5 %collective-permute-start.6 = (bf16[16,16,512]{2,1,0:T(8,128)(2,1)}, bf16[16,16,512]{2,1,0:T(8,128)(2,1)S(1)}, u32[]{:S(2)}, u32[]{:S(2)}) collective-permute-start(bf16[16,16,512]{2,1,0:T(8,128)(2,1)} %get-tuple-element.36), channel_id=1, source_target_pairs={{0,32},{32,64},{64,96},{96,0},{1,33},{33,65},{65,97},{97,1},{2,34}... | collective-permute-start | bytes 786440 | tf_op jit(solution)/shard_map/ppermute | solution.py:288
  129.5 15.2 %collective-permute-start.7 = (bf16[16,16,512]{2,1,0:T(8,128)(2,1)}, bf16[16,16,512]{2,1,0:T(8,128)(2,1)S(1)}, u32[]{:S(2)}, u32[]{:S(2)}) collective-permute-start(bf16[16,16,512]{2,1,0:T(8,128)(2,1)} %get-tuple-element.37), channel_id=1, source_target_pairs={{0,96},{32,0},{64,32},{96,64},{1,97},{33,1},{65,33},{97,65},{2,98}... | collective-permute-start | bytes 786440 | tf_op jit(solution)/shard_map/ppermute | solution.py:288
  131.8 24.1 %all-to-all-start.3 = ((bf16[32,16,1024]{2,1,0:T(8,128)(2,1)}), bf16[32,16,1024]{2,1,0:T(8,128)(2,1)}, u32[]{:S(2)}, u32[]{:S(2)}) async-start(bf16[32,16,1024]{2,1,0:T(8,128)(2,1)} %bitcast.6), calls=%async_computation.3 | async-start | bytes 2097152 | tf_op jit(solution)/shard_map/all_to_all | solution.py:350
  137.3 13.0 %collective-permute-start.12 = (bf16[16,16,512]{2,1,0:T(8,128)(2,1)S(1)}, bf16[16,16,512]{2,1,0:T(8,128)(2,1)S(1)}, u32[]{:S(2)}, u32[]{:S(2)}) collective-permute-start(bf16[16,16,512]{2,1,0:T(8,128)(2,1)S(1)} %copy-done.10), channel_id=1, source_target_pairs={{0,32},{32,64},{64,96},{96,0},{1,33},{33,65},{65,97},{97,1},{2,34}... | collective-permute-start | bytes 786440 | tf_op jit(solution)/shard_map/ppermute | solution.py:288
  138.3 12.0 %collective-permute-start.13 = (bf16[16,16,512]{2,1,0:T(8,128)(2,1)S(1)}, bf16[16,16,512]{2,1,0:T(8,128)(2,1)S(1)}, u32[]{:S(2)}, u32[]{:S(2)}) collective-permute-start(bf16[16,16,512]{2,1,0:T(8,128)(2,1)S(1)} %get-tuple-element.47), channel_id=1, source_target_pairs={{0,96},{32,0},{64,32},{96,64},{1,97},{33,1},{65,33},{97,65},{2,98}... | collective-permute-start | bytes 786440 | tf_op jit(solution)/shard_map/ppermute | solution.py:288
  144.7 9.9 %collective-permute-start.14 = (bf16[16,16,512]{2,1,0:T(8,128)(2,1)S(1)}, bf16[16,16,512]{2,1,0:T(8,128)(2,1)S(1)}, u32[]{:S(2)}, u32[]{:S(2)}) collective-permute-start(bf16[16,16,512]{2,1,0:T(8,128)(2,1)S(1)} %add_convert_fusion.2), channel_id=1, source_target_pairs={{0,96},{32,0},{64,32},{96,64},{1,97},{33,1},{65,33},{97,65},{2,98}... | collective-permute-start | bytes 786440 | tf_op jit(solution)/shard_map/ppermute | solution.py:288
  147.2 8.4 %collective-permute-start.11 = (bf16[16,16,512]{2,1,0:T(8,128)(2,1)S(1)}, bf16[16,16,512]{2,1,0:T(8,128)(2,1)S(1)}, u32[]{:S(2)}, u32[]{:S(2)}) collective-permute-start(bf16[16,16,512]{2,1,0:T(8,128)(2,1)S(1)} %add_convert_fusion.3), channel_id=1, source_target_pairs={{0,32},{32,64},{64,96},{96,0},{1,33},{33,65},{65,97},{97,1},{2,34}... | collective-permute-start | bytes 786440 | tf_op jit(solution)/shard_map/ppermute | solution.py:288
  157.4 22.5 %all-to-all-start.4 = ((bf16[32,32,512]{2,1,0:T(8,128)(2,1)}), bf16[32,32,512]{2,1,0:T(8,128)(2,1)S(1)}, u32[]{:S(2)}, u32[]{:S(2)}) async-start(bf16[32,32,512]{2,1,0:T(8,128)(2,1)} %copy.25), calls=%async_computation.4 | async-start | bytes 2097152 | tf_op jit(solution)/shard_map/all_to_all | solution.py:353
  182.3 1.3 copy-start
  183.6 35.1 %all-to-all-start.5 = ((bf16[128,16,512]{2,1,0:T(8,128)(2,1)}), bf16[128,16,512]{2,1,0:T(8,128)(2,1)S(1)}, u32[]{:S(2)}, u32[]{:S(2)}) async-start(bf16[128,16,512]{2,1,0:T(8,128)(2,1)} %bitcast.14), calls=%async_computation.5 | async-start | bytes 4194304 | tf_op jit(solution)/shard_map/all_to_all | solution.py:355
  (7 other events, 6.8 us)

commit v8 on v7

--- a/solution.py
+++ b/solution.py
@@ -278,7 +278,7 @@
         in_specs=[pl.BlockSpec(memory_space=pltpu.VMEM)] * 2,
         out_specs=pl.BlockSpec(memory_space=pltpu.VMEM),
         out_shape=jax.ShapeDtypeStruct((count, rows.shape[1]), BF16),
-        compiler_params=pltpu.CompilerParams(vmem_limit_bytes=32 * 1024 * 1024),
+        compiler_params=pltpu.CompilerParams(vmem_limit_bytes=60 * 1024 * 1024),
         name="place_rows",
     )(ids.reshape(1, -1), rows)
 

time: 222 us -> 224 us (level)
  Pallas kernels: 33.2 us -> 35.7 us
    pallas_call x1, Pallas kernels: 2.33 us -> 4.9 us  [place_rows(): pl.pallas_call(place_kernel, in_specs=[pl.BlockSpec(memory_space=pltpu.VM...]
where the time goes in v8:
time: 224 us; the launch traced here: 223 us
  waiting for transfers between devices  76.7 us (34%)
  blocking collectives  44.6 us (20%)
  starting transfers between devices  43 us (19%)
  Pallas kernels  35.7 us (16%)
  local copies, waits for them, and re-layouts  17.7 us (8%)
  other arithmetic  4.32 us (2%)
    all_to_all x1, blocking collectives, body(): table = lax.all_to_all(by_row, BOTH, 0, 0, tiled=True)  44.6 us
    all_to_all x1, waiting for transfers between devices, body(): d_encodings = gather_rows(lax.all_to_all(placed, BOTH, 0, 0, tiled=True))  28.4 us
    pallas_call x2, Pallas kernels, attention(): pl.pallas_call(functools.partial(attention_kernel, first, last), grid=(st...  23.7 us
    ppermute x15, starting transfers between devices, shift(): lax.ppermute(value, 'enc', [(i, (i + by) % count) for i in range(count)])  17.7 us
    all_to_all x2, waiting for transfers between devices, body(): own = jnp.swapaxes(lax.all_to_all(sent[c], 'dp', 0, 0, tiled=True), 0, 1)  17.6 us
    all_to_all x1, waiting for transfers between devices, body(): lax.all_to_all(summed, 'dp', 0, 0, tiled=True)  16.6 us
    ppermute x15, waiting for transfers between devices, shift(): lax.ppermute(value, 'enc', [(i, (i + by) % count) for i in range(count)])  14.1 us
    unnamed x24, local copies, waits for them, and re-layouts  11.2 us
  transfers between devices with their start and end apart: 20, of which 11 were waited for; matrix products, arithmetic and copies ran while one was open for 4% of the time, Pallas kernels for 12%

profile of v8, /device:TPU:1, one launch (start us, length us, event | category | flops | bytes accessed | tf_op | source)
XLA Modules:
  0.0 222.9 jit_solution(16239018680675040297)
XLA Ops:
  3.8 44.6 %all_to_all.30.table_ref = bf16[128,72,128]{2,1,0:T(8,128)(2,1)S(1)} all-to-all(bf16[128,72,128]{2,1,0:T(8,128)(2,1)S(1)} %spread_rows.1), channel_id=1, replica_groups=mesh['enc'=4,'dp'=32] {'enc','dp'}, dimensions={0} | all-to-all | bytes 4718592 | tf_op jit(solution)/shard_map/all_to_all | solution.py:322
  48.4 2.2 %pick_first_rows.1 = bf16[512,512]{1,0:T(8,128)(2,1)} custom-call(bf16[128,72,128]{2,1,0:T(8,128)(2,1)S(1)} %all_to_all.30.table_ref), custom_call_target="tpu_custom_call" | custom-call | tf_op jit(solution)/shard_map/pick_first_rows/pallas_call | solution.py:234
  50.7 4.6 %all-to-all-start.1 = ((bf16[32,16,512]{2,1,0:T(8,128)(2,1)}), bf16[32,16,512]{2,1,0:T(8,128)(2,1)S(1)}, u32[]{:S(2)}, u32[]{:S(2)}) async-start(bf16[32,16,512]{2,1,0:T(8,128)(2,1)} %bitcast.2), calls=%async_computation.1 | async-start | bytes 1048576 | tf_op jit(solution)/shard_map/all_to_all | solution.py:340
  56.8 2.1 pick_rows.1
  58.9 8.1 %all-to-all-done.1 = bf16[32,16,512]{2,1,0:T(8,128)(2,1)S(1)} async-done(((bf16[32,16,512]{2,1,0:T(8,128)(2,1)}), bf16[32,16,512]{2,1,0:T(8,128)(2,1)S(1)}, u32[]{:S(2)}, u32[]{:S(2)}) %all-to-all-start.1) | async-done | bytes 524320 | tf_op jit(solution)/shard_map/all_to_all | solution.py:340
  68.8 2.4 %collective-permute-start.5 = (bf16[16,32,512]{2,1,0:T(8,128)(2,1)S(1)}, bf16[16,32,512]{2,1,0:T(8,128)(2,1)S(1)}, u32[]{:S(2)}, u32[]{:S(2)}) collective-permute-start(bf16[16,32,512]{2,1,0:T(8,128)(2,1)S(1)} %bitcast.20), channel_id=1, source_target_pairs={{0,96},{32,0},{64,32},{96,64},{1,97},{33,1},{65,33},{97,65},{2,98}... | collective-permute-start | bytes 1572872 | tf_op jit(solution)/shard_map/ppermute | solution.py:288
  71.1 5.5 %all-to-all-start.2 = ((bf16[32,16,512]{2,1,0:T(8,128)(2,1)}), bf16[32,16,512]{2,1,0:T(8,128)(2,1)}, u32[]{:S(2)}, u32[]{:S(2)}) async-start(bf16[32,16,512]{2,1,0:T(8,128)(2,1)} %bitcast.1), calls=%async_computation.2 | async-start | bytes 1048576 | tf_op jit(solution)/shard_map/all_to_all | solution.py:340
  78.8 9.5 %all-to-all-done.2 = bf16[32,16,512]{2,1,0:T(8,128)(2,1)} async-done(((bf16[32,16,512]{2,1,0:T(8,128)(2,1)}), bf16[32,16,512]{2,1,0:T(8,128)(2,1)}, u32[]{:S(2)}, u32[]{:S(2)}) %all-to-all-start.2) | async-done | bytes 524320 | tf_op jit(solution)/shard_map/all_to_all | solution.py:340
  90.7 2.4 %collective-permute-start.2 = (bf16[16,32,512]{2,1,0:T(8,128)(2,1)S(1)}, bf16[16,32,512]{2,1,0:T(8,128)(2,1)S(1)}, u32[]{:S(2)}, u32[]{:S(2)}) collective-permute-start(bf16[16,32,512]{2,1,0:T(8,128)(2,1)S(1)} %bitcast.16), channel_id=1, source_target_pairs={{0,96},{32,0},{64,32},{96,64},{1,97},{33,1},{65,33},{97,65},{2,98}... | collective-permute-start | bytes 1572872 | tf_op jit(solution)/shard_map/ppermute | solution.py:288
  100.0 11.7 %attention.2 = (bf16[16,64,512]{2,1,0:T(8,128)(2,1)}, bf16[16,64,512]{2,1,0:T(8,128)(2,1)}, bf16[16,32,512]{2,1,0:T(8,128)(2,1)S(1)}, bf16[16,32,512]{2,1,0:T(8,...) custom-call(bf16[16,32,512]{2,1,0:T(8,128)(2,1)S(1)} %bitcast.21, ...), custom_call_target="tpu_custom_call" | custom-call | flops 7200000000 | bytes 6400000 | tf_op jit(solution)/shard_map/attention/pallas_call | solution.py:141
  113.3 1.9 collective-permute-start.9
  116.4 12.0 %attention.3 = (bf16[16,64,512]{2,1,0:T(8,128)(2,1)}, bf16[16,64,512]{2,1,0:T(8,128)(2,1)}, bf16[16,32,512]{2,1,0:T(8,128)(2,1)S(1)}, bf16[16,16,512]{2,1,0:T(8,...) custom-call(bf16[16,32,512]{2,1,0:T(8,128)(2,1)S(1)} %bitcast.17, ...), custom_call_target="tpu_custom_call", output_to_operand_aliasing={{0}: (8, {}), {1}: (9, {})} | custom-call | flops 7200000000 | bytes 6400000 | tf_op jit(solution)/shard_map/attention/pallas_call | solution.py:141
  129.5 2.4 %collective-permute-start.7 = (bf16[16,16,512]{2,1,0:T(8,128)(2,1)}, bf16[16,16,512]{2,1,0:T(8,128)(2,1)S(1)}, u32[]{:S(2)}, u32[]{:S(2)}) collective-permute-start(bf16[16,16,512]{2,1,0:T(8,128)(2,1)} %get-tuple-element.37), channel_id=1, source_target_pairs={{0,96},{32,0},{64,32},{96,64},{1,97},{33,1},{65,33},{97,65},{2,98}... | collective-permute-start | bytes 786440 | tf_op jit(solution)/shard_map/ppermute | solution.py:288
  131.8 5.4 %all-to-all-start.3 = ((bf16[32,16,1024]{2,1,0:T(8,128)(2,1)}), bf16[32,16,1024]{2,1,0:T(8,128)(2,1)}, u32[]{:S(2)}, u32[]{:S(2)}) async-start(bf16[32,16,1024]{2,1,0:T(8,128)(2,1)} %bitcast.6), calls=%async_computation.3 | async-start | bytes 2097152 | tf_op jit(solution)/shard_map/all_to_all | solution.py:350
  141.7 2.9 %collective-permute-done.6 = bf16[16,16,512]{2,1,0:T(8,128)(2,1)S(1)} collective-permute-done((bf16[16,16,512]{2,1,0:T(8,128)(2,1)}, bf16[16,16,512]{2,1,0:T(8,128)(2,1)S(1)}, u32[]{:S(2)}, u32[]{:S(2)}) %collective-permute-start.6) | collective-permute-done | bytes 262176 | tf_op jit(solution)/shard_map/ppermute | solution.py:288
  144.7 2.4 %collective-permute-start.14 = (bf16[16,16,512]{2,1,0:T(8,128)(2,1)S(1)}, bf16[16,16,512]{2,1,0:T(8,128)(2,1)S(1)}, u32[]{:S(2)}, u32[]{:S(2)}) collective-permute-start(bf16[16,16,512]{2,1,0:T(8,128)(2,1)S(1)} %add_convert_fusion.2), channel_id=1, source_target_pairs={{0,96},{32,0},{64,32},{96,64},{1,97},{33,1},{65,33},{97,65},{2,98}... | collective-permute-start | bytes 786440 | tf_op jit(solution)/shard_map/ppermute | solution.py:288
  147.3 3.0 %collective-permute-done.12 = bf16[16,16,512]{2,1,0:T(8,128)(2,1)S(1)} collective-permute-done((bf16[16,16,512]{2,1,0:T(8,128)(2,1)S(1)}, bf16[16,16,512]{2,1,0:T(8,128)(2,1)S(1)}, u32[]{:S(2)}, u32[]{:S(2)}) %collective-permute-start.12) | collective-permute-done | bytes 262176 | tf_op jit(solution)/shard_map/ppermute | solution.py:288
  150.3 4.4 %collective-permute-done.14 = bf16[16,16,512]{2,1,0:T(8,128)(2,1)S(1)} collective-permute-done((bf16[16,16,512]{2,1,0:T(8,128)(2,1)S(1)}, bf16[16,16,512]{2,1,0:T(8,128)(2,1)S(1)}, u32[]{:S(2)}, u32[]{:S(2)}) %collective-permute-start.14) | collective-permute-done | bytes 262176 | tf_op jit(solution)/shard_map/ppermute | solution.py:288
  157.4 5.2 %all-to-all-start.4 = ((bf16[32,32,512]{2,1,0:T(8,128)(2,1)}), bf16[32,32,512]{2,1,0:T(8,128)(2,1)S(1)}, u32[]{:S(2)}, u32[]{:S(2)}) async-start(bf16[32,32,512]{2,1,0:T(8,128)(2,1)} %copy.25), calls=%async_computation.4 | async-start | bytes 2097152 | tf_op jit(solution)/shard_map/all_to_all | solution.py:353
  163.4 16.6 %all-to-all-done.4 = bf16[32,32,512]{2,1,0:T(8,128)(2,1)S(1)} async-done(((bf16[32,32,512]{2,1,0:T(8,128)(2,1)}), bf16[32,32,512]{2,1,0:T(8,128)(2,1)S(1)}, u32[]{:S(2)}, u32[]{:S(2)}) %all-to-all-start.4) | async-done | bytes 1048608 | tf_op jit(solution)/shard_map/all_to_all | solution.py:353
  180.9 4.9 %place_rows.1 = bf16[2048,512]{1,0:T(8,128)(2,1)} custom-call(s32[1,1024]{1,0:T(1,128)} %add.63.ids_ref, bf16[1024,512]{1,0:T(8,128)(2,1)} %bitcast.23), custom_call_target="tpu_custom_call" | custom-call | tf_op jit(solution)/shard_map/place_rows/pallas_call | solution.py:276
  185.8 4.7 %all-to-all-start.5 = ((bf16[128,16,512]{2,1,0:T(8,128)(2,1)}), bf16[128,16,512]{2,1,0:T(8,128)(2,1)S(1)}, u32[]{:S(2)}, u32[]{:S(2)}) async-start(bf16[128,16,512]{2,1,0:T(8,128)(2,1)} %bitcast.22), calls=%async_computation.5 | async-start | bytes 4194304 | tf_op jit(solution)/shard_map/all_to_all | solution.py:355
  192.5 28.4 %all-to-all-done.5.x_ref = bf16[128,16,512]{2,1,0:T(8,128)(2,1)S(1)} async-done(((bf16[128,16,512]{2,1,0:T(8,128)(2,1)}), bf16[128,16,512]{2,1,0:T(8,128)(2,1)S(1)}, u32[]{:S(2)}, u32[]{:S(2)}) %all-to-all-start.5) | async-done | bytes 2097184 | tf_op jit(solution)/shard_map/all_to_all | solution.py:355
  220.9 2.0 gather_rows.1
  (68 shorter events, 32.9 us)
Async XLA Ops:
  1.5 1.6 copy-start
  50.7 16.3 %all-to-all-start.1 = ((bf16[32,16,512]{2,1,0:T(8,128)(2,1)}), bf16[32,16,512]{2,1,0:T(8,128)(2,1)S(1)}, u32[]{:S(2)}, u32[]{:S(2)}) async-start(bf16[32,16,512]{2,1,0:T(8,128)(2,1)} %bitcast.2), calls=%async_computation.1 | async-start | bytes 1048576 | tf_op jit(solution)/shard_map/all_to_all | solution.py:340
  67.2 23.5 %collective-permute-start.3 = (bf16[16,32,512]{2,1,0:T(8,128)(2,1)S(1)}, bf16[16,32,512]{2,1,0:T(8,128)(2,1)S(1)}, u32[]{:S(2)}, u32[]{:S(2)}) collective-permute-start(bf16[16,32,512]{2,1,0:T(8,128)(2,1)S(1)} %bitcast.18), channel_id=1, source_target_pairs={{0,64},{32,96},{64,0},{96,32},{1,65},{33,97},{65,1},{97,33},{2,66}... | collective-permute-start | bytes 1572872 | tf_op jit(solution)/shard_map/ppermute | solution.py:288
  68.4 25.5 %collective-permute-start.4 = (bf16[16,32,512]{2,1,0:T(8,128)(2,1)S(1)}, bf16[16,32,512]{2,1,0:T(8,128)(2,1)S(1)}, u32[]{:S(2)}, u32[]{:S(2)}) collective-permute-start(bf16[16,32,512]{2,1,0:T(8,128)(2,1)S(1)} %bitcast.19), channel_id=1, source_target_pairs={{0,32},{32,64},{64,96},{96,0},{1,33},{33,65},{65,97},{97,1},{2,34}... | collective-permute-start | bytes 1572872 | tf_op jit(solution)/shard_map/ppermute | solution.py:288
  68.8 25.9 %collective-permute-start.5 = (bf16[16,32,512]{2,1,0:T(8,128)(2,1)S(1)}, bf16[16,32,512]{2,1,0:T(8,128)(2,1)S(1)}, u32[]{:S(2)}, u32[]{:S(2)}) collective-permute-start(bf16[16,32,512]{2,1,0:T(8,128)(2,1)S(1)} %bitcast.20), channel_id=1, source_target_pairs={{0,96},{32,0},{64,32},{96,64},{1,97},{33,1},{65,33},{97,65},{2,98}... | collective-permute-start | bytes 1572872 | tf_op jit(solution)/shard_map/ppermute | solution.py:288
  71.1 17.2 %all-to-all-start.2 = ((bf16[32,16,512]{2,1,0:T(8,128)(2,1)}), bf16[32,16,512]{2,1,0:T(8,128)(2,1)}, u32[]{:S(2)}, u32[]{:S(2)}) async-start(bf16[32,16,512]{2,1,0:T(8,128)(2,1)} %bitcast.1), calls=%async_computation.2 | async-start | bytes 1048576 | tf_op jit(solution)/shard_map/all_to_all | solution.py:340
  88.3 28.1 %copy-start.3 = (bf16[16,64,512]{2,1,0:T(8,128)(2,1)S(1)}, bf16[16,64,512]{2,1,0:T(8,128)(2,1)}, u32[]{:S(2)}) copy-start(bf16[16,64,512]{2,1,0:T(8,128)(2,1)} %refs_5_.3) | copy-start | bytes 3145732
  89.7 23.6 %collective-permute-start = (bf16[16,32,512]{2,1,0:T(8,128)(2,1)S(1)}, bf16[16,32,512]{2,1,0:T(8,128)(2,1)S(1)}, u32[]{:S(2)}, u32[]{:S(2)}) collective-permute-start(bf16[16,32,512]{2,1,0:T(8,128)(2,1)S(1)} %bitcast.14), channel_id=1, source_target_pairs={{0,64},{32,96},{64,0},{96,32},{1,65},{33,97},{65,1},{97,33},{2,66}... | collective-permute-start | bytes 1572872 | tf_op jit(solution)/shard_map/ppermute | solution.py:288
  90.5 26.0 %collective-permute-start.1 = (bf16[16,32,512]{2,1,0:T(8,128)(2,1)S(1)}, bf16[16,32,512]{2,1,0:T(8,128)(2,1)S(1)}, u32[]{:S(2)}, u32[]{:S(2)}) collective-permute-start(bf16[16,32,512]{2,1,0:T(8,128)(2,1)S(1)} %bitcast.15), channel_id=1, source_target_pairs={{0,32},{32,64},{64,96},{96,0},{1,33},{33,65},{65,97},{97,1},{2,34}... | collective-permute-start | bytes 1572872 | tf_op jit(solution)/shard_map/ppermute | solution.py:288
  90.7 25.7 %collective-permute-start.2 = (bf16[16,32,512]{2,1,0:T(8,128)(2,1)S(1)}, bf16[16,32,512]{2,1,0:T(8,128)(2,1)S(1)}, u32[]{:S(2)}, u32[]{:S(2)}) collective-permute-start(bf16[16,32,512]{2,1,0:T(8,128)(2,1)S(1)} %bitcast.16), channel_id=1, source_target_pairs={{0,96},{32,0},{64,32},{96,64},{1,97},{33,1},{65,33},{97,65},{2,98}... | collective-permute-start | bytes 1572872 | tf_op jit(solution)/shard_map/ppermute | solution.py:288
  95.5 1.2 copy-start.1
  111.7 25.5 %collective-permute-start.10 = (bf16[16,32,512]{2,1,0:T(8,128)(2,1)}, bf16[16,32,512]{2,1,0:T(8,128)(2,1)}, u32[]{:S(2)}, u32[]{:S(2)}) collective-permute-start(bf16[16,32,512]{2,1,0:T(8,128)(2,1)} %get-tuple-element.41), channel_id=1, source_target_pairs={{0,32},{32,64},{64,96},{96,0},{1,33},{33,65},{65,97},{97,1},{2,34}... | collective-permute-start | bytes 1572872 | tf_op jit(solution)/shard_map/ppermute | solution.py:288
  112.0 26.3 %collective-permute-start.8 = (bf16[16,32,512]{2,1,0:T(8,128)(2,1)}, bf16[16,32,512]{2,1,0:T(8,128)(2,1)}, u32[]{:S(2)}, u32[]{:S(2)}) collective-permute-start(bf16[16,32,512]{2,1,0:T(8,128)(2,1)} %get-tuple-element.39), channel_id=1, source_target_pairs={{0,64},{32,96},{64,0},{96,32},{1,65},{33,97},{65,1},{97,33},{2,66}... | collective-permute-start | bytes 1572872 | tf_op jit(solution)/shard_map/ppermute | solution.py:288
  113.3 26.7 %collective-permute-start.9 = (bf16[16,32,512]{2,1,0:T(8,128)(2,1)S(1)}, bf16[16,32,512]{2,1,0:T(8,128)(2,1)}, u32[]{:S(2)}, u32[]{:S(2)}) collective-permute-start(bf16[16,32,512]{2,1,0:T(8,128)(2,1)S(1)} %get-tuple-element.40), channel_id=1, source_target_pairs={{0,96},{32,0},{64,32},{96,64},{1,97},{33,1},{65,33},{97,65},{2,98}... | collective-permute-start | bytes 1572872 | tf_op jit(solution)/shard_map/ppermute | solution.py:288
  129.2 8.1 %copy-start.9 = (bf16[16,16,512]{2,1,0:T(8,128)(2,1)S(1)}, bf16[16,16,512]{2,1,0:T(8,128)(2,1)}, u32[]{:S(2)}) copy-start(bf16[16,16,512]{2,1,0:T(8,128)(2,1)} %copy-done.8) | copy-start | bytes 786436
  129.2 15.5 %collective-permute-start.6 = (bf16[16,16,512]{2,1,0:T(8,128)(2,1)}, bf16[16,16,512]{2,1,0:T(8,128)(2,1)S(1)}, u32[]{:S(2)}, u32[]{:S(2)}) collective-permute-start(bf16[16,16,512]{2,1,0:T(8,128)(2,1)} %get-tuple-element.36), channel_id=1, source_target_pairs={{0,32},{32,64},{64,96},{96,0},{1,33},{33,65},{65,97},{97,1},{2,34}... | collective-permute-start | bytes 786440 | tf_op jit(solution)/shard_map/ppermute | solution.py:288
  129.5 15.2 %collective-permute-start.7 = (bf16[16,16,512]{2,1,0:T(8,128)(2,1)}, bf16[16,16,512]{2,1,0:T(8,128)(2,1)S(1)}, u32[]{:S(2)}, u32[]{:S(2)}) collective-permute-start(bf16[16,16,512]{2,1,0:T(8,128)(2,1)} %get-tuple-element.37), channel_id=1, source_target_pairs={{0,96},{32,0},{64,32},{96,64},{1,97},{33,1},{65,33},{97,65},{2,98}... | collective-permute-start | bytes 786440 | tf_op jit(solution)/shard_map/ppermute | solution.py:288
  131.8 24.1 %all-to-all-start.3 = ((bf16[32,16,1024]{2,1,0:T(8,128)(2,1)}), bf16[32,16,1024]{2,1,0:T(8,128)(2,1)}, u32[]{:S(2)}, u32[]{:S(2)}) async-start(bf16[32,16,1024]{2,1,0:T(8,128)(2,1)} %bitcast.6), calls=%async_computation.3 | async-start | bytes 2097152 | tf_op jit(solution)/shard_map/all_to_all | solution.py:350
  137.3 13.0 %collective-permute-start.12 = (bf16[16,16,512]{2,1,0:T(8,128)(2,1)S(1)}, bf16[16,16,512]{2,1,0:T(8,128)(2,1)S(1)}, u32[]{:S(2)}, u32[]{:S(2)}) collective-permute-start(bf16[16,16,512]{2,1,0:T(8,128)(2,1)S(1)} %copy-done.9), channel_id=1, source_target_pairs={{0,32},{32,64},{64,96},{96,0},{1,33},{33,65},{65,97},{97,1},{2,34}... | collective-permute-start | bytes 786440 | tf_op jit(solution)/shard_map/ppermute | solution.py:288
  138.3 12.0 %collective-permute-start.13 = (bf16[16,16,512]{2,1,0:T(8,128)(2,1)S(1)}, bf16[16,16,512]{2,1,0:T(8,128)(2,1)S(1)}, u32[]{:S(2)}, u32[]{:S(2)}) collective-permute-start(bf16[16,16,512]{2,1,0:T(8,128)(2,1)S(1)} %get-tuple-element.47), channel_id=1, source_target_pairs={{0,96},{32,0},{64,32},{96,64},{1,97},{33,1},{65,33},{97,65},{2,98}... | collective-permute-start | bytes 786440 | tf_op jit(solution)/shard_map/ppermute | solution.py:288
  144.7 9.9 %collective-permute-start.14 = (bf16[16,16,512]{2,1,0:T(8,128)(2,1)S(1)}, bf16[16,16,512]{2,1,0:T(8,128)(2,1)S(1)}, u32[]{:S(2)}, u32[]{:S(2)}) collective-permute-start(bf16[16,16,512]{2,1,0:T(8,128)(2,1)S(1)} %add_convert_fusion.2), channel_id=1, source_target_pairs={{0,96},{32,0},{64,32},{96,64},{1,97},{33,1},{65,33},{97,65},{2,98}... | collective-permute-start | bytes 786440 | tf_op jit(solution)/shard_map/ppermute | solution.py:288
  147.2 8.4 %collective-permute-start.11 = (bf16[16,16,512]{2,1,0:T(8,128)(2,1)S(1)}, bf16[16,16,512]{2,1,0:T(8,128)(2,1)S(1)}, u32[]{:S(2)}, u32[]{:S(2)}) collective-permute-start(bf16[16,16,512]{2,1,0:T(8,128)(2,1)S(1)} %add_convert_fusion.3), channel_id=1, source_target_pairs={{0,32},{32,64},{64,96},{96,0},{1,33},{33,65},{65,97},{97,1},{2,34}... | collective-permute-start | bytes 786440 | tf_op jit(solution)/shard_map/ppermute | solution.py:288
  157.4 22.5 %all-to-all-start.4 = ((bf16[32,32,512]{2,1,0:T(8,128)(2,1)}), bf16[32,32,512]{2,1,0:T(8,128)(2,1)S(1)}, u32[]{:S(2)}, u32[]{:S(2)}) async-start(bf16[32,32,512]{2,1,0:T(8,128)(2,1)} %copy.25), calls=%async_computation.4 | async-start | bytes 2097152 | tf_op jit(solution)/shard_map/all_to_all | solution.py:353
  185.8 35.1 %all-to-all-start.5 = ((bf16[128,16,512]{2,1,0:T(8,128)(2,1)}), bf16[128,16,512]{2,1,0:T(8,128)(2,1)S(1)}, u32[]{:S(2)}, u32[]{:S(2)}) async-start(bf16[128,16,512]{2,1,0:T(8,128)(2,1)} %bitcast.22), calls=%async_computation.5 | async-start | bytes 4194304 | tf_op jit(solution)/shard_map/all_to_all | solution.py:355
  (7 other events, 6.6 us)
